TPU v7x, 256 devices: a whole 4x4x8 slice. The times are simulated.
256 devices in a mesh: ctx: 32 (over x_lo, z, core), head: 8 (over x_hi, y).
Axes of the slice: x: 4 (x_hi: 2, x_lo: 2; x = x_hi * 2 + x_lo), y: 4, z: 8, core: 2. Of those that a mesh axis runs over, the one named last changes fastest.
Arguments:
- q_nope: bfloat16 [4096, 16384], P('ctx', 'head'), may hold values from -6 to 6
- q_rope: bfloat16 [4096, 8192], P('ctx', 'head'), may hold values from -32 to 32
- latent: bfloat16 [4096, 576], P(('ctx', 'head')), may hold values from -32 to 32
- block_start: int32 [64], replicated, may hold values from 0 to 4032, as said below
- w_uk: bfloat16 [128, 128, 512], P('head'), may hold values from -0.5 to 0.5
- w_uv: bfloat16 [128, 512, 128], P('head'), may hold values from -1.5 to 1.5
Outputs:
- attn_out: bfloat16 [4096, 16384], P('ctx', 'head')
Inputs may be any that keep to these rules, and one draw needn't show every extreme that they name: `block_start`: blocks 2 i and 2 i + 1 start at k * 64 and (63 - k) * 64 for a k that takes each value 0 to 31 once over i.
All inputs are finite; a program needn't handle non-finite values.
Results may differ from a plain program's by a relative error of at most 0.0065.
Values may be sent and summed in bfloat16 or wider, within the bound.
No kernel may reach another device: no remote copies, remote signals or barrier semaphores. Data moves between devices by JAX's collectives and lax.ppermute only.
A program may use at most 128 MiB of HBM per device.

v0:
```python
import math

import jax
import jax.numpy as jnp
from jax import lax
from jax.sharding import PartitionSpec as P


def laid_out(pieces, dim):
    shape = list(pieces.shape[1:])
    shape[dim] *= pieces.shape[0]
    return jnp.moveaxis(pieces, 0, dim).reshape(shape)


def from_everyone(x, axis):
    count = lax.axis_size(axis)
    return lax.all_to_all(jnp.broadcast_to(x[None], (count, *x.shape)), axis, 0, 0, tiled=True)


def gather_directly(x, axis, dim):
    return laid_out(from_everyone(x, axis), dim)


def lookup_positions(table, row_ids, block_rows):
    block_ids = row_ids // block_rows
    onehot = block_ids[:, None] == jnp.arange(table.shape[0], dtype=jnp.int32)[None, :]
    starts = jnp.sum(jnp.where(onehot, table[None, :], 0), axis=1)
    return starts + row_ids % block_rows


def update_state(state, query, query_pos, piece, key_pos, score_scale, latent_width):

    def compute():
        top_old, total_old, acc_old = state
        scores = (
            jnp.einsum("hqd,kd->hqk", query, piece, preferred_element_type=jnp.float32)
            * score_scale
        )
        allowed = key_pos[None, None, :] <= query_pos[None, :, None]
        top_new = jnp.maximum(top_old, jnp.max(jnp.where(allowed, scores, -1e30), axis=2))
        weights = jnp.where(allowed, jnp.exp(scores - top_new[:, :, None]), 0.0)
        total_new = jnp.sum(weights, axis=2)
        acc_new = jnp.einsum(
            "hqk,kl->hql",
            weights.astype(jnp.bfloat16),
            piece[:, :latent_width],
            preferred_element_type=jnp.float32,
        )
        return (top_new, total_new, acc_new)

    def keep():
        return state

    return lax.cond(jnp.min(key_pos) <= jnp.max(query_pos), compute, keep)


def shards(q_nope, q_rope, latent, block_start, w_uk, w_uv):
    head_count = w_uk.shape[0]
    nope_width = w_uk.shape[1]
    latent_width = w_uk.shape[2]
    value_width = w_uv.shape[2]
    tok_rows = q_nope.shape[0]
    block_rows = tok_rows // 2
    rope_width = q_rope.shape[1] // head_count
    score_scale = 1.0 / math.sqrt(nope_width + rope_width)
    first_row = lax.axis_index("ctx") * tok_rows
    query_pos = lookup_positions(
        block_start, first_row + jnp.arange(tok_rows, dtype=jnp.int32), block_rows
    )
    nope_heads = q_nope.reshape(tok_rows, head_count, nope_width)
    q_lat = jnp.einsum("thd,hdl->htl", nope_heads, w_uk, preferred_element_type=jnp.float32).astype(
        jnp.bfloat16
    )
    rope_heads = jnp.transpose(q_rope.reshape(tok_rows, head_count, rope_width), (1, 0, 2))
    query = jnp.concatenate([q_lat, rope_heads], axis=2)
    halves = (
        (query[:, :block_rows], query_pos[:block_rows]),
        (query[:, block_rows:], query_pos[block_rows:]),
    )

    def fresh_state():
        return (
            jnp.full((head_count, block_rows), -1e30, jnp.float32),
            jnp.zeros((head_count, block_rows), jnp.float32),
            jnp.zeros((head_count, block_rows, latent_width), jnp.float32),
        )

    initial = (fresh_state(), fresh_state())

    def absorb_piece(carry, piece):
        key_pos = lookup_positions(
            block_start, jnp.arange(piece.shape[0], dtype=jnp.int32), block_rows
        )
        return tuple(
            (
                update_state(state, half_query, half_pos, piece, key_pos, score_scale, latent_width)
                for state, (half_query, half_pos) in zip(carry, halves)
            )
        )

    shard_latent = gather_directly(latent, "head", 0)
    carry = absorb_piece(initial, lax.all_gather(shard_latent, "ctx", axis=0, tiled=True))
    o_lat = jnp.concatenate(
        [(state[2] / state[1][:, :, None]).astype(jnp.bfloat16) for state in carry], axis=1
    )
    result = jnp.einsum("hql,hlv->qhv", o_lat, w_uv, preferred_element_type=jnp.float32).astype(
        jnp.bfloat16
    )
    return result.reshape(tok_rows, head_count * value_width)


def solution(mesh):
    placed = (
        P("ctx", "head"),
        P("ctx", "head"),
        P(("ctx", "head"), None),
        P(),
        P("head", None, None),
        P("head", None, None),
    )
    return jax.shard_map(
        shards, mesh=mesh, in_specs=placed, out_specs=P("ctx", "head"), check_vma=False
    )
```

profile of v0, /device:TPU:1, one launch (start us, length us, event | category | flops | bytes accessed | tf_op | source)
XLA Modules:
  0.0 148.4 jit_solution(7943705534425906698)
XLA Ops:
  6.5 0.0 copy-start
  6.5 0.0 all-gather.2.cloned.1.call-start
  6.5 0.9 broadcast_in_dim.80
  7.4 14.5 %all_to_all.5 = bf16[8,16,576]{2,1,0:T(8,128)(2,1)} all-to-all(bf16[8,16,576]{2,1,0:T(8,128)(2,1)S(1)} %broadcast_in_dim.80), channel_id=1, replica_groups=mesh['ctx'=32,'head'=8] {'head'}, dimensions={0} | all-to-all | bytes 294912 | tf_op jit(solution)/shard_map/all_to_all | solution.py:17
  21.9 0.0 all-gather.2.cloned.1.call-update
  22.0 0.7 select_reduce_fusion.3
  22.7 0.9 select_reduce_fusion.2
  23.6 0.8 slice_reduce_fusion.1
  24.4 0.6 fusion.49
  27.6 1.1 copy.22
  28.7 0.3 copy.23
  29.0 0.0 copy-done
  29.0 1.7 %convolution_convert_fusion = bf16[16,128,512]{2,1,0:T(8,128)(2,1)S(1)} fusion(bf16[16,128,512]{2,1,0:T(8,128)(2,1)S(1)} %copy-done, bf16[128,2048]{1,0:T(8,128)(2,1)} %param.10), kind=kOutput, calls=%fused_computation.43 | convolution fusion | flops 269484032 | bytes 4718592 | tf_op jit(solution)/shard_map/thd,hdl->htl/dot_general | solution.py:71
  30.8 1.8 %pad_maximum_fusion = bf16[16,128,576]{2,1,0:T(8,128)(2,1)} fusion(bf16[16,128,64]{2,1,0:T(8,128)(2,1)S(1)} %bitcast.31, bf16[16,128,512]{2,1,0:T(8,128)(2,1)S(1)} %convolution_convert_fusion), kind=kLoop, calls=%fused_computation.36 | loop fusion | flops 4718592 | bytes 4718592 | tf_op jit(solution)/shard_map/concatenate | solution.py:75
  32.6 58.3 %all-gather.2.cloned.1.call-done = bf16[4096,576]{1,0:T(8,128)(2,1)} async-done(((bf16[128,576]{1,0:T(8,128)(2,1)}), bf16[4096,576]{1,0:T(8,128)(2,1)}) %all-gather.2.cloned.1.call-update) | async-done | bytes 4718608 | tf_op jit(solution)/shard_map/all_gather | solution.py:102
  90.9 23.0 %conditional.2 = (f32[16,64]{1,0:T(8,128)S(1)}, f32[16,64,512]{2,1,0:T(8,128)}) conditional(s32[]{:T(128)} %convert_element_type.27, () %tuple.21, (s32[4096]{0:T(1024)S(1)}, s32[64]{0:T(128)S(1)}, bf16[16,128,576]{2,1,0:T(8,128)(2,1)}, bf16[4096,576]{1,0:T(8,128)(2,1)}) %tuple.22), branch_computations={%region_4.5_spmd, %region_5.8_spmd} | conditional | flops 9173203968 | bytes 64266512 | solution.py:54
  90.9 0.2 broadcast_compare_fusion
  91.1 9.7 %select_reduce_fusion = (f32[16,64]{1,0:T(8,128)S(1)}, f32[16,64,4096]{2,1,0:T(8,128)S(1)}) fusion(pred[64,4096]{1,0:T(8,128)(4,1)S(1)} %broadcast_compare_fusion, bf16[4096,576]{1,0:T(8,128)(2,1)} %get-tuple-element.26, bf16[16,128,576]{2,1,0:T(8,128)(2,1)} %get-tuple-element.25), kind=kOutput, calls=%fused_computation.1 | convolution fusion | flops 4844420096 | bytes 23597056 | tf_op jit(solution)/shard_map/cond/branch_1_fun/hqd,kd->hqk/dot_general | solution.py:36
  100.8 8.2 %fusion.2 = f32[16,64,512]{2,1,0:T(8,128)} fusion(f32[16,64,4096]{2,1,0:T(8,128)S(1)} %get-tuple-element.44, f32[16,64]{1,0:T(8,128)S(1)} %broadcast_maximum_fusion, pred[64,4096]{1,0:T(8,128)(4,1)S(1)} %broadcast_compare_fusion, bf16[4096,576]{1,0:T(8,128)(2,1)} %get-tuple-element.26), kind=kOutput, calls=%fused_computation.4 | convolution fusion | flops 4311744512 | bytes 23334912 | tf_op jit(solution)/shard_map/cond/branch_1_fun/hqk,kl->hql/dot_general | solution.py:43
  109.0 4.9 %fusion.1 = f32[16,64]{1,0:T(8,128)S(1)} fusion(f32[16,64,4096]{2,1,0:T(8,128)S(1)} %get-tuple-element.44, f32[16,64]{1,0:T(8,128)S(1)} %broadcast_maximum_fusion, pred[64,4096]{1,0:T(8,128)(4,1)S(1)} %broadcast_compare_fusion), kind=kLoop, calls=%fused_computation.3 | loop fusion | flops 16776192 | bytes 17047552 | tf_op jit(solution)/shard_map/cond/branch_1_fun/reduce_sum | solution.py:42
  113.9 23.0 %conditional.3 = (f32[16,64]{1,0:T(8,128)S(1)}, f32[16,64,512]{2,1,0:T(8,128)}) conditional(s32[]{:T(128)} %convert_element_type.30, () %tuple.23, (s32[4096]{0:T(1024)S(1)}, s32[64]{0:T(128)S(1)}, bf16[16,128,576]{2,1,0:T(8,128)(2,1)}, bf16[4096,576]{1,0:T(8,128)(2,1)}) %tuple.24), branch_computations={%region_9.10_spmd, %region_10.13_spmd} | conditional | flops 9173203968 | bytes 64266512 | solution.py:54
  114.1 0.2 broadcast_compare_fusion.1
  114.3 9.6 %select_reduce_fusion.1 = (f32[16,64]{1,0:T(8,128)S(1)}, f32[16,64,4096]{2,1,0:T(8,128)S(1)}) fusion(pred[64,4096]{1,0:T(8,128)(4,1)S(1)} %broadcast_compare_fusion.1, bf16[4096,576]{1,0:T(8,128)(2,1)} %get-tuple-element.30, bf16[16,128,576]{2,1,0:T(8,128)(2,1)} %get-tuple-element.29), kind=kOutput, calls=%fused_computation.19 | convolution fusion | flops 4844420096 | bytes 23597056 | tf_op jit(solution)/shard_map/cond/branch_1_fun/hqd,kd->hqk/dot_general | solution.py:36
  123.9 8.1 %fusion.17 = f32[16,64,512]{2,1,0:T(8,128)} fusion(f32[16,64,4096]{2,1,0:T(8,128)S(1)} %get-tuple-element.46, f32[16,64]{1,0:T(8,128)S(1)} %broadcast_maximum_fusion.1, pred[64,4096]{1,0:T(8,128)(4,1)S(1)} %broadcast_compare_fusion.1, bf16[4096,576]{1,0:T(8,128)(2,1)} %get-tuple-element.30), kind=kOutput, calls=%fused_computation.22 | convolution fusion | flops 4311744512 | bytes 23334912 | tf_op jit(solution)/shard_map/cond/branch_1_fun/hqk,kl->hql/dot_general | solution.py:43
  132.0 4.9 %fusion.16 = f32[16,64]{1,0:T(8,128)S(1)} fusion(f32[16,64,4096]{2,1,0:T(8,128)S(1)} %get-tuple-element.46, f32[16,64]{1,0:T(8,128)S(1)} %broadcast_maximum_fusion.1, pred[64,4096]{1,0:T(8,128)(4,1)S(1)} %broadcast_compare_fusion.1), kind=kLoop, calls=%fused_computation.21 | loop fusion | flops 16776192 | bytes 17047552 | tf_op jit(solution)/shard_map/cond/branch_1_fun/reduce_sum | solution.py:42
  136.9 0.0 copy-start.1
  136.9 2.8 %divide_convert_fusion = (bf16[16,64,512]{2,1,0:T(8,128)(2,1)S(1)}, bf16[16,64,512]{2,1,0:T(8,128)(2,1)S(1)}) fusion(f32[16,64,512]{2,1,0:T(8,128)} %get-tuple-element.37, f32[16,64]{1,0:T(8,128)S(1)} %get-tuple-element.38, f32[16,64,512]{2,1,0:T(8,128)} %get-tuple-element.35, f32[16,64]{1,0:T(8,128)S(1)} %get-tuple-element.36), kind=kLoop, calls=%fused_computation.41 | loop fusion | flops 2097152 | bytes 6299648 | tf_op jit(solution)/shard_map/convert_element_type | solution.py:104
  139.7 0.1 copy-done.1
  139.8 0.8 fusion.34
  140.6 1.0 copy.25
  (5 shorter events, 0.0 us)
Async XLA Ops:
  6.5 22.5 %copy-start = (bf16[16,128,512]{2,1,0:T(8,128)(2,1)S(1)}, bf16[16,128,512]{2,1,0:T(8,128)(2,1)}, u32[]{:S(2)}) copy-start(bf16[16,128,512]{2,1,0:T(8,128)(2,1)} %param.14) | copy-start | bytes 6291460
  6.5 84.4 %all-gather.2.cloned.1.call-start = ((), (), s32[]{:S(2)}) async-start(), calls=%async_computation.1 | async-start | bytes 5406720 | tf_op jit(solution)/shard_map/all_gather | solution.py:102
  136.9 2.9 %copy-start.1 = (bf16[16,512,128]{2,1,0:T(8,128)(2,1)S(1)}, bf16[16,512,128]{2,1,0:T(8,128)(2,1)}, u32[]{:S(2)}) copy-start(bf16[16,512,128]{2,1,0:T(8,128)(2,1)} %param.15) | copy-start | bytes 6291460
Sparse Core Ops, SparseCore 0:
  22.1 68.8 all-gather.1
where the time goes:
time: 149 us; the launch traced here: 148 us
  waiting for transfers between devices  58.4 us (39%)
  matrix products  38.1 us (26%)
  other arithmetic  17.8 us (12%)
  between operations  16 us (11%)
  blocking collectives  14.5 us (10%)
  local copies, waits for them, and re-layouts  3.41 us (2%)
    all_gather x1, waiting for transfers between devices, shards(): lax.all_gather(shard_latent, 'ctx', axis=0, tiled=True)  58.3 us
    dot_general x2, matrix products, compute(): jnp.einsum('hqd,kd->hqk', query, piece, preferred_element_type=jnp.float32)  19.3 us
    dot_general x2, matrix products, compute(): jnp.einsum('hqk,kl->hql', weights.astype(jnp.bfloat16), piece[:, :latent_...  16.3 us
    all_to_all x1, blocking collectives, from_everyone(): lax.all_to_all(jnp.broadcast_to(x[None], (count, *x.shape)), axis, 0, 0,...  14.5 us
    reduce_sum x2, other arithmetic, compute(): total_new = jnp.sum(weights, axis=2)  9.78 us
  transfers between devices with their start and end apart: 1, of which 1 were waited for; matrix products, arithmetic and copies ran while one was open for 5% of the time, Pallas kernels for 0%

commit v1 on v0

v1 whole, which is shorter than its diff:
```python
import functools
import math

import jax
import jax.numpy as jnp
from jax import lax
from jax.experimental import pallas as pl
from jax.experimental.pallas import tpu as pltpu
from jax.sharding import PartitionSpec as P

BOTH = ("ctx", "head")
PIECE = 16
TILE = 256
OFFSETS = (0, 1, 3, 2)
WINDOW = (0, 1, 7, 3, 4, 2, 5, 6)


def device_index(x, y, z, core):
    return (((x % 2) * 8 + z) * 2 + core) * 8 + (x // 2) * 4 + y


def from_offset(value, first, second):
    pairs = []
    for x in range(4):
        for y in range(4):
            for z in range(8):
                for core in range(2):
                    dx, dy, dz = second if core else first
                    source = device_index((x + dx) % 4, (y + dy) % 4, (z + dz) % 8, core)
                    pairs.append((source, device_index(x, y, z, core)))
    return lax.ppermute(value, BOTH, pairs)


def other_core(value):
    return lax.ppermute(value, "ctx", [(i, i ^ 1) for i in range(32)])


def gather_own_core(latent):
    up = from_offset(latent, (0, 0, 1), (0, 0, 1))
    down = from_offset(latent, (0, 0, 7), (0, 0, 7))
    window = jnp.concatenate([latent, up, down])
    far_up = from_offset(window, (0, 0, 3), (0, 0, 3))
    far_down = from_offset(window[: 2 * PIECE], (0, 0, 5), (0, 0, 5))
    column = jnp.concatenate([window, far_up, far_down])
    plane = jnp.concatenate(
        [column] + [from_offset(column, (0, d, 0), (d, 0, 0)) for d in OFFSETS[1:]]
    )
    return [plane] + [from_offset(plane, (d, 0, 0), (0, d, 0)) for d in OFFSETS[1:]]


def query_kernel(nope_ref, rope_ref, uk_ref, query_ref):
    latent_width = uk_ref.shape[2]
    nope_width = uk_ref.shape[1]
    rope_width = rope_ref.shape[1] // uk_ref.shape[0]
    block = nope_ref.shape[0] // 2
    for head in range(uk_ref.shape[0]):
        lat = jnp.dot(
            nope_ref[:, head * nope_width : (head + 1) * nope_width],
            uk_ref[head],
            preferred_element_type=jnp.float32,
        ).astype(jnp.bfloat16)
        rope = rope_ref[:, head * rope_width : (head + 1) * rope_width]
        for half in range(2):
            rows = slice(half * block, (half + 1) * block)
            to = slice(head * block, (head + 1) * block)
            query_ref[half, to, :latent_width] = lat[rows]
            query_ref[half, to, latent_width:] = rope[rows]


def make_queries(q_nope, q_rope, w_uk):
    rows = q_nope.shape[0]
    heads, nope_width, latent_width = w_uk.shape
    rope_width = q_rope.shape[1] // heads
    at_once = 2
    width = latent_width + rope_width
    return pl.pallas_call(
        query_kernel,
        grid=(heads // at_once,),
        in_specs=[
            pl.BlockSpec((rows, at_once * nope_width), lambda g: (0, g)),
            pl.BlockSpec((rows, at_once * rope_width), lambda g: (0, g)),
            pl.BlockSpec((at_once, nope_width, latent_width), lambda g: (g, 0, 0)),
        ],
        out_specs=pl.BlockSpec((2, at_once * rows // 2, width), lambda g: (0, g, 0)),
        out_shape=jax.ShapeDtypeStruct((2, heads * rows // 2, width), jnp.bfloat16),
        cost_estimate=pl.CostEstimate(
            flops=2 * rows * heads * nope_width * latent_width,
            bytes_accessed=6 * 2**20,
            transcendentals=0,
        ),
        name="make_queries",
    )(q_nope, q_rope, w_uk)


def attention_kernel(starts_ref, query_ref, *refs):
    pieces = refs[:8]
    uv_ref, out_ref, keys, scores, top, total, acc = refs[8:]
    ctx, head_group = lax.axis_index("ctx"), lax.axis_index("head")
    x = (head_group // 4) * 2 + ctx // 16
    y, z, core = head_group % 4, (ctx // 2) % 8, ctx % 2
    count, block, latent_width = uv_ref.shape[0], out_ref.shape[0] // 2, uv_ref.shape[1]
    value_width = uv_ref.shape[2]
    rows = count * block
    factor = math.log2(math.e) / math.sqrt(value_width + query_ref.shape[2] - latent_width)

    for side in range(2):
        owner = core if side == 0 else 1 - core
        for last in range(4):
            ref = pieces[side * 4 + last]
            for middle in range(4):
                px = (x + jnp.where(owner == 0, OFFSETS[last], OFFSETS[middle])) % 4
                py = (y + jnp.where(owner == 0, OFFSETS[middle], OFFSETS[last])) % 4
                for first in range(8):
                    pz = (z + WINDOW[first]) % 8
                    token_block = 2 * (((px % 2) * 8 + pz) * 2 + owner) + px // 2
                    to = pl.multiple_of(starts_ref[token_block] + py * PIECE, PIECE)
                    at = (middle * 8 + first) * PIECE
                    keys[pl.ds(to, PIECE), :] = ref[at : at + PIECE, :]

    ahead = lax.broadcasted_iota(jnp.int32, (block, TILE), 0) - lax.broadcasted_iota(
        jnp.int32, (block, TILE), 1
    )
    chunk = 4 * block

    @pl.loop(0, 2)
    def _(half):
        start = starts_ref[2 * ctx + half]
        tiles = start // TILE + 1
        top[...] = jnp.full(top.shape, -1e30, jnp.float32)

        @pl.loop(0, tiles)
        def _(j):
            at = pl.multiple_of(j * TILE, TILE)
            tile = keys[pl.ds(at, TILE), :]
            allowed = ahead >= at - start
            for c in range(rows // chunk):
                own = slice(c * chunk, (c + 1) * chunk)
                s = lax.dot_general(
                    query_ref[half, own, :],
                    tile,
                    (((1,), (1,)), ((), ())),
                    preferred_element_type=jnp.float32,
                )
                s = jnp.where(allowed[None], s.reshape(chunk // block, block, TILE), -1e30)
                s = s.reshape(chunk, TILE)
                scores[own, pl.ds(at, TILE)] = s
                top[own, :] = jnp.maximum(top[own, :], jnp.maximum(s[:, :128], s[:, 128:]))

        top[...] = jnp.broadcast_to(
            jnp.max(top[...], axis=1, keepdims=True) * factor, top.shape
        )
        total[...] = jnp.zeros(total.shape, jnp.float32)
        acc[...] = jnp.zeros(acc.shape, jnp.float32)

        @pl.loop(0, tiles)
        def _(j):
            at = pl.multiple_of(j * TILE, TILE)
            tile = keys[pl.ds(at, TILE), :latent_width]
            for c in range(rows // chunk):
                own = slice(c * chunk, (c + 1) * chunk)
                shift = top[own, :]
                left = jnp.exp2(scores[own, pl.ds(at, 128)] * factor - shift)
                right = jnp.exp2(scores[own, pl.ds(at + 128, 128)] * factor - shift)
                total[own, :] += left + right
                weights = jnp.concatenate([left, right], axis=1).astype(jnp.bfloat16)
                acc[own, :] += jnp.dot(weights, tile, preferred_element_type=jnp.float32)

        to = pl.ds(pl.multiple_of(half * block, block), block)
        for h in range(count):
            own = slice(h * block, (h + 1) * block)
            whole = jnp.sum(total[own, :], axis=1, keepdims=True)
            lat = (acc[own, :] / whole).astype(jnp.bfloat16)
            out_ref[to, h * value_width : (h + 1) * value_width] = jnp.dot(
                lat, uv_ref[h], preferred_element_type=jnp.float32
            ).astype(jnp.bfloat16)


def attend(block_start, query, pieces, w_uv):
    heads, latent_width, value_width = w_uv.shape
    rows = query.shape[1]
    block = rows // heads
    keys = sum(p.shape[0] for p in pieces)
    width = query.shape[2]
    vmem = pl.BlockSpec(memory_space=pltpu.VMEM)
    return pl.pallas_call(
        attention_kernel,
        in_specs=[pl.BlockSpec(memory_space=pltpu.SMEM)] + [vmem] * (2 + len(pieces)),
        out_specs=vmem,
        out_shape=jax.ShapeDtypeStruct((2 * block, heads * value_width), jnp.bfloat16),
        scratch_shapes=[
            pltpu.VMEM((keys, width), jnp.bfloat16),
            pltpu.VMEM((rows, keys), jnp.float32),
            pltpu.VMEM((rows, 128), jnp.float32),
            pltpu.VMEM((rows, 128), jnp.float32),
            pltpu.VMEM((rows, latent_width), jnp.float32),
        ],
        compiler_params=pltpu.CompilerParams(vmem_limit_bytes=50 * 2**20),
        cost_estimate=pl.CostEstimate(
            flops=2 * rows * (keys + 256) * (width + latent_width),
            bytes_accessed=10 * 2**20,
            transcendentals=rows * keys,
        ),
        name="attention",
    )(block_start, query, *pieces, w_uv)


def shards(q_nope, q_rope, latent, block_start, w_uk, w_uv):
    query = make_queries(q_nope, q_rope, w_uk)
    own = gather_own_core(latent)
    pieces = own + [other_core(p) for p in own]
    return attend(block_start, query, pieces, w_uv)


def solution(mesh):
    placed = (P("ctx", "head"), P("ctx", "head"), P(BOTH, None), P(), P("head"), P("head"))
    return jax.shard_map(
        shards, mesh=mesh, in_specs=placed, out_specs=P("ctx", "head"), check_vma=False
    )
```

time: 149 us -> 106 us (0.71)
  waiting for transfers between devices: 58.4 us -> 10.6 us
  starting transfers between devices: 0.01 us -> 46.4 us
  matrix products: 38.1 us -> 0 us
  Pallas kernels: 0 us -> 32.2 us
  other arithmetic: 17.8 us -> 1.47 us
  between operations: 16 us -> 0.11 us
  blocking collectives: 14.5 us -> 0 us
  local copies, waits for them, and re-layouts: 3.41 us -> 14.1 us
    all_gather x1 -> x0, waiting for transfers between devices: 58.3 us -> none  [shards(): lax.all_gather(shard_latent, 'ctx', axis=0, tiled=True)]
    ppermute x0 -> x14, starting transfers between devices: none -> 46.4 us  [the longest x4 25.4 us: other_core(): return lax.ppermute(value, 'ctx', [(i, i ^ 1) for i in range(32)])]
    dot_general x6 -> x0, matrix products: 38.1 us -> none  [the longest x2 19.3 us: compute(): jnp.einsum('hqd,kd->hqk', query, piece, preferred_element_type=jnp.float32)]
    pallas_call x0 -> x2, Pallas kernels: none -> 32.2 us  [the longest x1 25.5 us: attend(): pl.pallas_call(attention_kernel, in_specs=[pl.BlockSpec(memory_space=pltp...]
    all_to_all x1 -> x0, blocking collectives: 14.5 us -> none  [from_everyone(): lax.all_to_all(jnp.broadcast_to(x[None], (count, *x.shape)), axis, 0, 0,...]
    ppermute x0 -> x7, local copies, waits for them, and re-layouts: none -> 11.9 us  [the longest x4 7.79 us: other_core(): return lax.ppermute(value, 'ctx', [(i, i ^ 1) for i in range(32)])]
    reduce_sum x4 -> x0, other arithmetic: 11.4 us -> none  [the longest x2 9.78 us: compute(): total_new = jnp.sum(weights, axis=2)]
    ppermute x0 -> x14, waiting for transfers between devices: none -> 10.6 us  [the longest x10 10.6 us: from_offset(): return lax.ppermute(value, BOTH, pairs)]
  transfers between devices with their start and end apart: 1 -> 14, of which waited for: 1 -> 4; matrix products, arithmetic and copies ran while one was open for 5% -> 11% of each run, Pallas kernels for 0% -> 6%
where the time goes in v1:
time: 106 us; the launch traced here: 105 us
  starting transfers between devices  46.4 us (44%)
  Pallas kernels  32.2 us (30%)
  local copies, waits for them, and re-layouts  14.1 us (13%)
  waiting for transfers between devices  10.6 us (10%)
  other arithmetic  1.47 us (1%)
    pallas_call x1, Pallas kernels, attend(): pl.pallas_call(attention_kernel, in_specs=[pl.BlockSpec(memory_space=pltp...  25.5 us
    ppermute x4, starting transfers between devices, other_core(): return lax.ppermute(value, 'ctx', [(i, i ^ 1) for i in range(32)])  25.4 us
    ppermute x10, starting transfers between devices, from_offset(): return lax.ppermute(value, BOTH, pairs)  20.9 us
    ppermute x10, waiting for transfers between devices, from_offset(): return lax.ppermute(value, BOTH, pairs)  10.6 us
    ppermute x4, local copies, waits for them, and re-layouts, other_core(): return lax.ppermute(value, 'ctx', [(i, i ^ 1) for i in range(32)])  7.79 us
    pallas_call x1, Pallas kernels, make_queries(): pl.pallas_call(query_kernel, grid=(heads // at_once,), in_specs=[pl.Block...  6.71 us
    ppermute x3, local copies, waits for them, and re-layouts, from_offset(): return lax.ppermute(value, BOTH, pairs)  4.07 us
  transfers between devices with their start and end apart: 14, of which 4 were waited for; matrix products, arithmetic and copies ran while one was open for 11% of the time, Pallas kernels for 6%

profile of v1, /device:TPU:1, one launch (start us, length us, event | category | flops | bytes accessed | tf_op | source)
XLA Modules:
  0.0 104.8 jit_solution(6012370059211200195)
XLA Ops:
  0.0 2.5 %collective-permute-start.1 = (bf16[16,576]{1,0:T(8,128)(2,1)}, bf16[16,576]{1,0:T(8,128)(2,1)S(1)}, u32[]{:S(2)}, u32[]{:S(2)}) collective-permute-start(bf16[16,576]{1,0:T(8,128)(2,1)} %param.8), channel_id=1, source_target_pairs={{112,0},{120,8},{0,16},{8,24},{16,32},{24,40},{32,48},{40,56},{48,... | collective-permute-start | bytes 55304 | tf_op jit(solution)/shard_map/ppermute | solution.py:31
  2.5 3.9 %collective-permute-start = (bf16[16,576]{1,0:T(8,128)(2,1)}, bf16[16,576]{1,0:T(8,128)(2,1)S(1)}, u32[]{:S(2)}, u32[]{:S(2)}) collective-permute-start(bf16[16,576]{1,0:T(8,128)(2,1)} %param.8), channel_id=1, source_target_pairs={{16,0},{24,8},{32,16},{40,24},{48,32},{56,40},{64,48},{72,56},{80,... | collective-permute-start | bytes 55304 | tf_op jit(solution)/shard_map/ppermute | solution.py:31
  6.4 0.8 constant_dynamic-update-slice_fusion.4
  7.2 0.4 collective-permute-done
  7.5 0.7 pad_maximum_fusion.1
  8.3 4.5 %collective-permute-start.3 = (bf16[32,576]{1,0:T(8,128)(2,1)S(1)}, bf16[32,576]{1,0:T(8,128)(2,1)S(1)}, u32[]{:S(2)}, u32[]{:S(2)}) collective-permute-start(bf16[32,576]{1,0:T(8,128)(2,1)S(1)} %pad_maximum_fusion.1), channel_id=1, source_target_pairs={{80,0},{88,8},{96,16},{104,24},{112,32},{120,40},{0,48},{8,56},{16... | collective-permute-start | bytes 110600 | tf_op jit(solution)/shard_map/ppermute | solution.py:31
  12.8 0.7 pad_maximum_fusion
  13.6 0.0 collective-permute-start.2
  13.6 4.8 %collective-permute-done.2 = bf16[48,576]{1,0:T(8,128)(2,1)S(1)} collective-permute-done((bf16[48,576]{1,0:T(8,128)(2,1)S(1)}, bf16[48,576]{1,0:T(8,128)(2,1)S(1)}, u32[]{:S(2)}, u32[]{:S(2)}) %collective-permute-start.2) | collective-permute-done | bytes 55328 | tf_op jit(solution)/shard_map/ppermute | solution.py:31
  18.5 2.6 %collective-permute-start.4 = (bf16[128,576]{1,0:T(8,128)(2,1)S(1)}, bf16[128,576]{1,0:T(8,128)(2,1)S(1)}, u32[]{:S(2)}, u32[]{:S(2)}) collective-permute-start(bf16[128,576]{1,0:T(8,128)(2,1)S(1)} %get-tuple-element.7), channel_id=1, source_target_pairs={{1,0},{136,8},{17,16},{152,24},{33,32},{168,40},{49,48},{184,56},{... | collective-permute-start | bytes 442376 | tf_op jit(solution)/shard_map/ppermute | solution.py:31
  21.0 1.7 %collective-permute-start.6 = (bf16[128,576]{1,0:T(8,128)(2,1)S(1)}, bf16[128,576]{1,0:T(8,128)(2,1)S(1)}, u32[]{:S(2)}, u32[]{:S(2)}) collective-permute-start(bf16[128,576]{1,0:T(8,128)(2,1)S(1)} %get-tuple-element.7), channel_id=1, source_target_pairs={{2,0},{12,8},{18,16},{28,24},{34,32},{44,40},{50,48},{60,56},{66,6... | collective-permute-start | bytes 442376 | tf_op jit(solution)/shard_map/ppermute | solution.py:31
  22.8 0.5 collective-permute-done.4
  23.3 4.8 %collective-permute-done.5 = bf16[128,576]{1,0:T(8,128)(2,1)S(1)} collective-permute-done((bf16[128,576]{1,0:T(8,128)(2,1)S(1)}, bf16[128,576]{1,0:T(8,128)(2,1)S(1)}, u32[]{:S(2)}, u32[]{:S(2)}) %collective-permute-start.5) | collective-permute-done | bytes 147488 | tf_op jit(solution)/shard_map/ppermute | solution.py:31
  28.2 0.2 copy.7
  28.5 3.0 %collective-permute-start.9 = (bf16[512,576]{0,1:T(8,128)(2,1)S(1)}, bf16[512,576]{0,1:T(8,128)(2,1)}, u32[]{:S(2)}, u32[]{:S(2)}) collective-permute-start(bf16[512,576]{0,1:T(8,128)(2,1)S(1)} %copy.7), channel_id=1, source_target_pairs={{4,0},{10,8},{20,16},{26,24},{36,32},{42,40},{52,48},{58,56},{68,6... | collective-permute-start | bytes 1769480 | tf_op jit(solution)/shard_map/ppermute | solution.py:31
  31.5 0.7 collective-permute-start.8
  32.2 2.0 %collective-permute-start.7 = (bf16[512,576]{0,1:T(8,128)(2,1)S(1)}, bf16[512,576]{0,1:T(8,128)(2,1)}, u32[]{:S(2)}, u32[]{:S(2)}) collective-permute-start(bf16[512,576]{0,1:T(8,128)(2,1)S(1)} %copy.7), channel_id=1, source_target_pairs={{128,0},{9,8},{144,16},{25,24},{160,32},{41,40},{176,48},{57,56},{... | collective-permute-start | bytes 1769480 | tf_op jit(solution)/shard_map/ppermute | solution.py:31
  34.2 13.8 %collective-permute-start.10 = (bf16[512,576]{0,1:T(8,128)(2,1)S(1)}, bf16[512,576]{0,1:T(8,128)(2,1)}, u32[]{:S(2)}, u32[]{:S(2)}) collective-permute-start(bf16[512,576]{0,1:T(8,128)(2,1)S(1)} %copy.7), channel_id=1, source_target_pairs={{0,8},{8,0},{16,24},{24,16},{32,40},{40,32},{48,56},{56,48},{64,72... | collective-permute-start | bytes 1769480 | tf_op jit(solution)/shard_map/ppermute | solution.py:35
  47.9 5.3 %collective-permute-start.13 = (bf16[512,576]{0,1:T(8,128)(2,1)}, bf16[512,576]{0,1:T(8,128)(2,1)}, u32[]{:S(2)}, u32[]{:S(2)}) collective-permute-start(bf16[512,576]{0,1:T(8,128)(2,1)} %collective-permute-done.9), channel_id=1, source_target_pairs={{0,8},{8,0},{16,24},{24,16},{32,40},{40,32},{48,56},{56,48},{64,72... | collective-permute-start | bytes 1769480 | tf_op jit(solution)/shard_map/ppermute | solution.py:35
  53.2 6.2 %collective-permute-start.12 = (bf16[512,576]{0,1:T(8,128)(2,1)}, bf16[512,576]{0,1:T(8,128)(2,1)}, u32[]{:S(2)}, u32[]{:S(2)}) collective-permute-start(bf16[512,576]{0,1:T(8,128)(2,1)} %collective-permute-done.8), channel_id=1, source_target_pairs={{0,8},{8,0},{16,24},{24,16},{32,40},{40,32},{48,56},{56,48},{64,72... | collective-permute-start | bytes 1769480 | tf_op jit(solution)/shard_map/ppermute | solution.py:35
  59.4 0.2 collective-permute-start.11
  59.6 6.7 %make_queries.1.query_ref = bf16[2,1024,576]{2,1,0:T(8,128)(2,1)} custom-call(bf16[128,2048]{1,0:T(8,128)(2,1)} %nope_ref.1, bf16[128,1024]{1,0:T(8,128)(2,1)} %rope_ref.1, bf16[16,128,512]{2,1,0:T(8,128)(2,1)} %uk_ref.1), custom_call_target="tpu_custom_call" | custom-call | flops 268435456 | bytes 6291456 | tf_op jit(solution)/shard_map/make_queries/pallas_call | solution.py:76
  66.3 1.4 %copy.11.refs_1_ = bf16[512,576]{1,0:T(8,128)(2,1)S(1)} copy(bf16[512,576]{0,1:T(8,128)(2,1)} %collective-permute-done.7) | data formatting | bytes 1179648 | tf_op jit(solution)/shard_map/ppermute | solution.py:31
  67.7 1.4 %copy.12.refs_2_ = bf16[512,576]{1,0:T(8,128)(2,1)S(1)} copy(bf16[512,576]{0,1:T(8,128)(2,1)} %collective-permute-done.8) | data formatting | bytes 1179648 | tf_op jit(solution)/shard_map/ppermute | solution.py:31
  69.0 1.4 %copy.13.refs_3_ = bf16[512,576]{1,0:T(8,128)(2,1)S(1)} copy(bf16[512,576]{0,1:T(8,128)(2,1)} %collective-permute-done.9) | data formatting | bytes 1179648 | tf_op jit(solution)/shard_map/ppermute | solution.py:31
  70.4 1.4 %copy.14.refs_4_ = bf16[512,576]{1,0:T(8,128)(2,1)S(1)} copy(bf16[512,576]{0,1:T(8,128)(2,1)} %collective-permute-done.10) | data formatting | bytes 1179648 | tf_op jit(solution)/shard_map/ppermute | solution.py:35
  71.8 0.0 copy-start.1
  71.8 2.1 %copy.17.refs_7_ = bf16[512,576]{1,0:T(8,128)(2,1)} copy(bf16[512,576]{0,1:T(8,128)(2,1)} %collective-permute-done.13) | data formatting | bytes 1179648 | tf_op jit(solution)/shard_map/ppermute | solution.py:35
  73.9 2.1 %copy.16.refs_6_ = bf16[512,576]{1,0:T(8,128)(2,1)} copy(bf16[512,576]{0,1:T(8,128)(2,1)} %collective-permute-done.12) | data formatting | bytes 1179648 | tf_op jit(solution)/shard_map/ppermute | solution.py:35
  76.1 2.1 %copy.15.refs_5_ = bf16[512,576]{1,0:T(8,128)(2,1)} copy(bf16[512,576]{0,1:T(8,128)(2,1)} %collective-permute-done.11) | data formatting | bytes 1179648 | tf_op jit(solution)/shard_map/ppermute | solution.py:35
  78.2 1.1 %copy-done = bf16[512,576]{1,0:T(8,128)(2,1)S(1)} copy-done((bf16[512,576]{1,0:T(8,128)(2,1)S(1)}, bf16[512,576]{1,0:T(8,128)(2,1)}, u32[]{:S(2)}) %copy-start) | copy-done | bytes 589848
  79.3 25.5 %attention.1 = bf16[128,2048]{1,0:T(8,128)(2,1)} custom-call(s32[64]{0:T(128)S(1)} %copy-done.1, bf16[2,1024,576]{2,1,0:T(8,128)(2,1)} %make_queries.1.query_ref, bf16[512,576]{1,0:T(8,128)(2,1)S(1)} %constant_dynamic-update-slice_fusion.5.refs_0_, bf16[512,576]{1,0:T(8,128)(2,1)S(1)} %copy.11.refs_1_, bf16[512,576]{1,0:T(8,128)(2,1)S(1)} %copy.12.refs_2_, ...), custom_call_target="tpu_custom_call" | custom-call | flops 9697230848 | bytes 10485760 | tf_op jit(solution)/shard_map/attention/pallas_call | solution.py:185
  (20 shorter events, 0.2 us)
Async XLA Ops:
  0.0 12.8 %collective-permute-start.1 = (bf16[16,576]{1,0:T(8,128)(2,1)}, bf16[16,576]{1,0:T(8,128)(2,1)S(1)}, u32[]{:S(2)}, u32[]{:S(2)}) collective-permute-start(bf16[16,576]{1,0:T(8,128)(2,1)} %param.8), channel_id=1, source_target_pairs={{112,0},{120,8},{0,16},{8,24},{16,32},{24,40},{32,48},{40,56},{48,... | collective-permute-start | bytes 55304 | tf_op jit(solution)/shard_map/ppermute | solution.py:31
  2.5 5.1 %collective-permute-start = (bf16[16,576]{1,0:T(8,128)(2,1)}, bf16[16,576]{1,0:T(8,128)(2,1)S(1)}, u32[]{:S(2)}, u32[]{:S(2)}) collective-permute-start(bf16[16,576]{1,0:T(8,128)(2,1)} %param.8), channel_id=1, source_target_pairs={{16,0},{24,8},{32,16},{40,24},{48,32},{56,40},{64,48},{72,56},{80,... | collective-permute-start | bytes 55304 | tf_op jit(solution)/shard_map/ppermute | solution.py:31
  8.3 10.2 %collective-permute-start.3 = (bf16[32,576]{1,0:T(8,128)(2,1)S(1)}, bf16[32,576]{1,0:T(8,128)(2,1)S(1)}, u32[]{:S(2)}, u32[]{:S(2)}) collective-permute-start(bf16[32,576]{1,0:T(8,128)(2,1)S(1)} %pad_maximum_fusion.1), channel_id=1, source_target_pairs={{80,0},{88,8},{96,16},{104,24},{112,32},{120,40},{0,48},{8,56},{16... | collective-permute-start | bytes 110600 | tf_op jit(solution)/shard_map/ppermute | solution.py:31
  13.6 4.9 %collective-permute-start.2 = (bf16[48,576]{1,0:T(8,128)(2,1)S(1)}, bf16[48,576]{1,0:T(8,128)(2,1)S(1)}, u32[]{:S(2)}, u32[]{:S(2)}) collective-permute-start(bf16[48,576]{1,0:T(8,128)(2,1)S(1)} %pad_maximum_fusion), channel_id=1, source_target_pairs={{48,0},{56,8},{64,16},{72,24},{80,32},{88,40},{96,48},{104,56},{11... | collective-permute-start | bytes 165896 | tf_op jit(solution)/shard_map/ppermute | solution.py:31
  18.5 4.8 %collective-permute-start.4 = (bf16[128,576]{1,0:T(8,128)(2,1)S(1)}, bf16[128,576]{1,0:T(8,128)(2,1)S(1)}, u32[]{:S(2)}, u32[]{:S(2)}) collective-permute-start(bf16[128,576]{1,0:T(8,128)(2,1)S(1)} %get-tuple-element.7), channel_id=1, source_target_pairs={{1,0},{136,8},{17,16},{152,24},{33,32},{168,40},{49,48},{184,56},{... | collective-permute-start | bytes 442376 | tf_op jit(solution)/shard_map/ppermute | solution.py:31
  21.0 7.1 %collective-permute-start.5 = (bf16[128,576]{1,0:T(8,128)(2,1)S(1)}, bf16[128,576]{1,0:T(8,128)(2,1)S(1)}, u32[]{:S(2)}, u32[]{:S(2)}) collective-permute-start(bf16[128,576]{1,0:T(8,128)(2,1)S(1)} %get-tuple-element.7), channel_id=1, source_target_pairs={{3,0},{140,8},{19,16},{156,24},{35,32},{172,40},{51,48},{188,56},{... | collective-permute-start | bytes 442376 | tf_op jit(solution)/shard_map/ppermute | solution.py:31
  21.0 7.2 %collective-permute-start.6 = (bf16[128,576]{1,0:T(8,128)(2,1)S(1)}, bf16[128,576]{1,0:T(8,128)(2,1)S(1)}, u32[]{:S(2)}, u32[]{:S(2)}) collective-permute-start(bf16[128,576]{1,0:T(8,128)(2,1)S(1)} %get-tuple-element.7), channel_id=1, source_target_pairs={{2,0},{12,8},{18,16},{28,24},{34,32},{44,40},{50,48},{60,56},{66,6... | collective-permute-start | bytes 442376 | tf_op jit(solution)/shard_map/ppermute | solution.py:31
  28.5 19.4 %collective-permute-start.9 = (bf16[512,576]{0,1:T(8,128)(2,1)S(1)}, bf16[512,576]{0,1:T(8,128)(2,1)}, u32[]{:S(2)}, u32[]{:S(2)}) collective-permute-start(bf16[512,576]{0,1:T(8,128)(2,1)S(1)} %copy.7), channel_id=1, source_target_pairs={{4,0},{10,8},{20,16},{26,24},{36,32},{42,40},{52,48},{58,56},{68,6... | collective-permute-start | bytes 1769480 | tf_op jit(solution)/shard_map/ppermute | solution.py:31
  31.5 21.7 %collective-permute-start.8 = (bf16[512,576]{0,1:T(8,128)(2,1)S(1)}, bf16[512,576]{0,1:T(8,128)(2,1)}, u32[]{:S(2)}, u32[]{:S(2)}) collective-permute-start(bf16[512,576]{0,1:T(8,128)(2,1)S(1)} %copy.7), channel_id=1, source_target_pairs={{132,0},{11,8},{148,16},{27,24},{164,32},{43,40},{180,48},{59,56},... | collective-permute-start | bytes 1769480 | tf_op jit(solution)/shard_map/ppermute | solution.py:31
  32.2 27.2 %collective-permute-start.7 = (bf16[512,576]{0,1:T(8,128)(2,1)S(1)}, bf16[512,576]{0,1:T(8,128)(2,1)}, u32[]{:S(2)}, u32[]{:S(2)}) collective-permute-start(bf16[512,576]{0,1:T(8,128)(2,1)S(1)} %copy.7), channel_id=1, source_target_pairs={{128,0},{9,8},{144,16},{25,24},{160,32},{41,40},{176,48},{57,56},{... | collective-permute-start | bytes 1769480 | tf_op jit(solution)/shard_map/ppermute | solution.py:31
  34.2 36.2 %collective-permute-start.10 = (bf16[512,576]{0,1:T(8,128)(2,1)S(1)}, bf16[512,576]{0,1:T(8,128)(2,1)}, u32[]{:S(2)}, u32[]{:S(2)}) collective-permute-start(bf16[512,576]{0,1:T(8,128)(2,1)S(1)} %copy.7), channel_id=1, source_target_pairs={{0,8},{8,0},{16,24},{24,16},{32,40},{40,32},{48,56},{56,48},{64,72... | collective-permute-start | bytes 1769480 | tf_op jit(solution)/shard_map/ppermute | solution.py:35
  47.9 23.9 %collective-permute-start.13 = (bf16[512,576]{0,1:T(8,128)(2,1)}, bf16[512,576]{0,1:T(8,128)(2,1)}, u32[]{:S(2)}, u32[]{:S(2)}) collective-permute-start(bf16[512,576]{0,1:T(8,128)(2,1)} %collective-permute-done.9), channel_id=1, source_target_pairs={{0,8},{8,0},{16,24},{24,16},{32,40},{40,32},{48,56},{56,48},{64,72... | collective-permute-start | bytes 1769480 | tf_op jit(solution)/shard_map/ppermute | solution.py:35
  53.2 20.8 %collective-permute-start.12 = (bf16[512,576]{0,1:T(8,128)(2,1)}, bf16[512,576]{0,1:T(8,128)(2,1)}, u32[]{:S(2)}, u32[]{:S(2)}) collective-permute-start(bf16[512,576]{0,1:T(8,128)(2,1)} %collective-permute-done.8), channel_id=1, source_target_pairs={{0,8},{8,0},{16,24},{24,16},{32,40},{40,32},{48,56},{56,48},{64,72... | collective-permute-start | bytes 1769480 | tf_op jit(solution)/shard_map/ppermute | solution.py:35
  59.4 16.7 %collective-permute-start.11 = (bf16[512,576]{0,1:T(8,128)(2,1)}, bf16[512,576]{0,1:T(8,128)(2,1)}, u32[]{:S(2)}, u32[]{:S(2)}) collective-permute-start(bf16[512,576]{0,1:T(8,128)(2,1)} %collective-permute-done.7), channel_id=1, source_target_pairs={{0,8},{8,0},{16,24},{24,16},{32,40},{40,32},{48,56},{56,48},{64,72... | collective-permute-start | bytes 1769480 | tf_op jit(solution)/shard_map/ppermute | solution.py:35
  71.8 6.5 %copy-start.1 = (s32[64]{0:T(128)S(1)}, s32[64]{0:T(128)}, u32[]{:S(2)}) copy-start(s32[64]{0:T(128)} %starts_ref.1) | copy-start | bytes 772
  78.2 1.1 %copy-start = (bf16[512,576]{1,0:T(8,128)(2,1)S(1)}, bf16[512,576]{1,0:T(8,128)(2,1)}, u32[]{:S(2)}) copy-start(bf16[512,576]{1,0:T(8,128)(2,1)} %copy.15.refs_5_) | copy-start | bytes 1769476

commit v2 on v1

--- a/solution.py
+++ b/solution.py
@@ -10,7 +10,7 @@
 
 BOTH = ("ctx", "head")
 PIECE = 16
-TILE = 256
+TILE = 512
 OFFSETS = (0, 1, 3, 2)
 WINDOW = (0, 1, 7, 3, 4, 2, 5, 6)
 
@@ -35,17 +35,20 @@
     return lax.ppermute(value, "ctx", [(i, i ^ 1) for i in range(32)])
 
 
-def gather_own_core(latent):
+def gather_own_core(latent, query):
+    latent = latent[None]
     up = from_offset(latent, (0, 0, 1), (0, 0, 1))
     down = from_offset(latent, (0, 0, 7), (0, 0, 7))
     window = jnp.concatenate([latent, up, down])
     far_up = from_offset(window, (0, 0, 3), (0, 0, 3))
-    far_down = from_offset(window[: 2 * PIECE], (0, 0, 5), (0, 0, 5))
+    far_down = from_offset(window[:2], (0, 0, 5), (0, 0, 5))
     column = jnp.concatenate([window, far_up, far_down])
     plane = jnp.concatenate(
         [column] + [from_offset(column, (0, d, 0), (d, 0, 0)) for d in OFFSETS[1:]]
     )
-    return [plane] + [from_offset(plane, (d, 0, 0), (0, d, 0)) for d in OFFSETS[1:]]
+    plane, query = lax.optimization_barrier((plane, query))
+    own = [plane] + [from_offset(plane, (d, 0, 0), (0, d, 0)) for d in OFFSETS[1:]]
+    return own, query
 
 
 def query_kernel(nope_ref, rope_ref, uk_ref, query_ref):
@@ -114,13 +117,12 @@
                     pz = (z + WINDOW[first]) % 8
                     token_block = 2 * (((px % 2) * 8 + pz) * 2 + owner) + px // 2
                     to = pl.multiple_of(starts_ref[token_block] + py * PIECE, PIECE)
-                    at = (middle * 8 + first) * PIECE
-                    keys[pl.ds(to, PIECE), :] = ref[at : at + PIECE, :]
+                    keys[pl.ds(to, PIECE), :] = ref[middle * 8 + first]
 
     ahead = lax.broadcasted_iota(jnp.int32, (block, TILE), 0) - lax.broadcasted_iota(
         jnp.int32, (block, TILE), 1
     )
-    chunk = 4 * block
+    chunk = 16 * block
 
     @pl.loop(0, 2)
     def _(half):
@@ -144,7 +146,7 @@
                 s = jnp.where(allowed[None], s.reshape(chunk // block, block, TILE), -1e30)
                 s = s.reshape(chunk, TILE)
                 scores[own, pl.ds(at, TILE)] = s
-                top[own, :] = jnp.maximum(top[own, :], jnp.maximum(s[:, :128], s[:, 128:]))
+                top[own, :] = functools.reduce(jnp.maximum, [s[:, i:i+128] for i in range(0, TILE, 128)], top[own, :])
 
         top[...] = jnp.broadcast_to(
             jnp.max(top[...], axis=1, keepdims=True) * factor, top.shape
@@ -159,10 +161,9 @@
             for c in range(rows // chunk):
                 own = slice(c * chunk, (c + 1) * chunk)
                 shift = top[own, :]
-                left = jnp.exp2(scores[own, pl.ds(at, 128)] * factor - shift)
-                right = jnp.exp2(scores[own, pl.ds(at + 128, 128)] * factor - shift)
-                total[own, :] += left + right
-                weights = jnp.concatenate([left, right], axis=1).astype(jnp.bfloat16)
+                parts = [jnp.exp2(scores[own, pl.ds(at + i, 128)] * factor - shift) for i in range(0, TILE, 128)]
+                total[own, :] += sum(parts[1:], parts[0])
+                weights = jnp.concatenate(parts, axis=1).astype(jnp.bfloat16)
                 acc[own, :] += jnp.dot(weights, tile, preferred_element_type=jnp.float32)
 
         to = pl.ds(pl.multiple_of(half * block, block), block)
@@ -179,7 +180,7 @@
     heads, latent_width, value_width = w_uv.shape
     rows = query.shape[1]
     block = rows // heads
-    keys = sum(p.shape[0] for p in pieces)
+    keys = sum(p.shape[0] * p.shape[1] for p in pieces)
     width = query.shape[2]
     vmem = pl.BlockSpec(memory_space=pltpu.VMEM)
     return pl.pallas_call(
@@ -194,7 +195,7 @@
             pltpu.VMEM((rows, 128), jnp.float32),
             pltpu.VMEM((rows, latent_width), jnp.float32),
         ],
-        compiler_params=pltpu.CompilerParams(vmem_limit_bytes=50 * 2**20),
+        compiler_params=pltpu.CompilerParams(vmem_limit_bytes=30 * 2**20),
         cost_estimate=pl.CostEstimate(
             flops=2 * rows * (keys + 256) * (width + latent_width),
             bytes_accessed=10 * 2**20,
@@ -206,7 +207,7 @@
 
 def shards(q_nope, q_rope, latent, block_start, w_uk, w_uv):
     query = make_queries(q_nope, q_rope, w_uk)
-    own = gather_own_core(latent)
+    own, query = gather_own_core(latent, query)
     pieces = own + [other_core(p) for p in own]
     return attend(block_start, query, pieces, w_uv)
 

time: 106 us -> 85.6 us (0.81)
  local copies, waits for them, and re-layouts: 14.1 us -> 2.64 us
  Pallas kernels: 32.2 us -> 27.4 us
  starting transfers between devices: 46.4 us -> 41.7 us
  waiting for transfers between devices: 10.6 us -> 11.8 us
    ppermute x7 -> x0, local copies, waits for them, and re-layouts: 11.9 us -> none  [the longest x4 7.79 us: other_core(): return lax.ppermute(value, 'ctx', [(i, i ^ 1) for i in range(32)])]
    pallas_call x1, Pallas kernels: 25.5 us -> 20.7 us  [attend(): pl.pallas_call(attention_kernel, in_specs=[pl.BlockSpec(memory_space=pltp...]
    ppermute x4, starting transfers between devices: 25.4 us -> 20.7 us  [other_core(): return lax.ppermute(value, 'ctx', [(i, i ^ 1) for i in range(32)])]
    ppermute x4, waiting for transfers between devices: 0.01 us -> 2.64 us  [other_core(): return lax.ppermute(value, 'ctx', [(i, i ^ 1) for i in range(32)])]
    ppermute x10, waiting for transfers between devices: 10.6 us -> 9.13 us  [from_offset(): return lax.ppermute(value, BOTH, pairs)]
    unnamed x10 -> x12, local copies, waits for them, and re-layouts: 1.94 us -> 2.61 us
  transfers between devices with their start and end apart: 14 -> 14, of which waited for: 4 -> 6; matrix products, arithmetic and copies ran while one was open for 11% -> 3% of each run, Pallas kernels for 6% -> 8%
where the time goes in v2:
time: 85.6 us; the launch traced here: 85.1 us
  starting transfers between devices  41.7 us (49%)
  Pallas kernels  27.4 us (32%)
  waiting for transfers between devices  11.8 us (14%)
  local copies, waits for them, and re-layouts  2.64 us (3%)
  other arithmetic  1.48 us (2%)
    ppermute x10, starting transfers between devices, from_offset(): return lax.ppermute(value, BOTH, pairs)  21.1 us
    pallas_call x1, Pallas kernels, attend(): pl.pallas_call(attention_kernel, in_specs=[pl.BlockSpec(memory_space=pltp...  20.7 us
    ppermute x4, starting transfers between devices, other_core(): return lax.ppermute(value, 'ctx', [(i, i ^ 1) for i in range(32)])  20.7 us
    ppermute x10, waiting for transfers between devices, from_offset(): return lax.ppermute(value, BOTH, pairs)  9.13 us
    pallas_call x1, Pallas kernels, make_queries(): pl.pallas_call(query_kernel, grid=(heads // at_once,), in_specs=[pl.Block...  6.69 us
    ppermute x4, waiting for transfers between devices, other_core(): return lax.ppermute(value, 'ctx', [(i, i ^ 1) for i in range(32)])  2.64 us
    unnamed x12, local copies, waits for them, and re-layouts  2.61 us
  transfers between devices with their start and end apart: 14, of which 6 were waited for; matrix products, arithmetic and copies ran while one was open for 3% of the time, Pallas kernels for 8%

profile of v2, /device:TPU:1, one launch (start us, length us, event | category | flops | bytes accessed | tf_op | source)
XLA Modules:
  0.0 85.1 jit_solution(9431365965446207009)
XLA Ops:
  0.0 2.5 %collective-permute-start.1 = (bf16[1,16,576]{2,1,0:T(8,128)(2,1)}, bf16[1,16,576]{2,1,0:T(8,128)(2,1)S(1)}, u32[]{:S(2)}, u32[]{:S(2)}) collective-permute-start(bf16[1,16,576]{2,1,0:T(8,128)(2,1)} %bitcast.3), channel_id=1, source_target_pairs={{112,0},{120,8},{0,16},{8,24},{16,32},{24,40},{32,48},{40,56},{48,... | collective-permute-start | bytes 55304 | tf_op jit(solution)/shard_map/ppermute | solution.py:31
  2.5 3.9 %collective-permute-start = (bf16[1,16,576]{2,1,0:T(8,128)(2,1)}, bf16[1,16,576]{2,1,0:T(8,128)(2,1)S(1)}, u32[]{:S(2)}, u32[]{:S(2)}) collective-permute-start(bf16[1,16,576]{2,1,0:T(8,128)(2,1)} %bitcast.4), channel_id=1, source_target_pairs={{16,0},{24,8},{32,16},{40,24},{48,32},{56,40},{64,48},{72,56},{80,... | collective-permute-start | bytes 55304 | tf_op jit(solution)/shard_map/ppermute | solution.py:31
  6.4 0.8 constant_dynamic-update-slice_fusion.4
  7.2 0.4 collective-permute-done
  7.5 0.7 pad_maximum_fusion.1
  8.3 4.6 %collective-permute-start.3 = (bf16[2,16,576]{2,1,0:T(8,128)(2,1)S(1)}, bf16[2,16,576]{2,1,0:T(8,128)(2,1)S(1)}, u32[]{:S(2)}, u32[]{:S(2)}) collective-permute-start(bf16[2,16,576]{2,1,0:T(8,128)(2,1)S(1)} %pad_maximum_fusion.1), channel_id=1, source_target_pairs={{80,0},{88,8},{96,16},{104,24},{112,32},{120,40},{0,48},{8,56},{16... | collective-permute-start | bytes 110600 | tf_op jit(solution)/shard_map/ppermute | solution.py:31
  12.9 0.7 pad_maximum_fusion
  13.6 0.1 collective-permute-start.2
  13.8 4.8 %collective-permute-done.2 = bf16[3,16,576]{2,1,0:T(8,128)(2,1)S(1)} collective-permute-done((bf16[3,16,576]{2,1,0:T(8,128)(2,1)S(1)}, bf16[3,16,576]{2,1,0:T(8,128)(2,1)S(1)}, u32[]{:S(2)}, u32[]{:S(2)}) %collective-permute-start.2) | collective-permute-done | bytes 55328 | tf_op jit(solution)/shard_map/ppermute | solution.py:31
  18.6 0.0 collective-permute-done.3
  18.6 0.0 copy-start.1
  18.7 0.0 copy-start.2
  18.7 2.6 %collective-permute-start.4 = (bf16[8,16,576]{2,1,0:T(8,128)(2,1)S(1)}, bf16[8,16,576]{2,1,0:T(8,128)(2,1)S(1)}, u32[]{:S(2)}, u32[]{:S(2)}) collective-permute-start(bf16[8,16,576]{2,1,0:T(8,128)(2,1)S(1)} %get-tuple-element.11), channel_id=1, source_target_pairs={{1,0},{136,8},{17,16},{152,24},{33,32},{168,40},{49,48},{184,56},{... | collective-permute-start | bytes 442376 | tf_op jit(solution)/shard_map/ppermute | solution.py:31
  21.2 0.0 collective-permute-start.5
  21.2 6.7 %make_queries.1.query_ref = bf16[2,1024,576]{2,1,0:T(8,128)(2,1)} custom-call(bf16[128,2048]{1,0:T(8,128)(2,1)} %nope_ref.1, bf16[128,1024]{1,0:T(8,128)(2,1)} %rope_ref.1, bf16[16,128,512]{2,1,0:T(8,128)(2,1)} %uk_ref.1), custom_call_target="tpu_custom_call" | custom-call | flops 268435456 | bytes 6291456 | tf_op jit(solution)/shard_map/make_queries/pallas_call | solution.py:79
  27.9 1.7 %collective-permute-start.6 = (bf16[8,16,576]{2,1,0:T(8,128)(2,1)S(1)}, bf16[8,16,576]{2,1,0:T(8,128)(2,1)S(1)}, u32[]{:S(2)}, u32[]{:S(2)}) collective-permute-start(bf16[8,16,576]{2,1,0:T(8,128)(2,1)S(1)} %get-tuple-element.11), channel_id=1, source_target_pairs={{2,0},{12,8},{18,16},{28,24},{34,32},{44,40},{50,48},{60,56},{66,6... | collective-permute-start | bytes 442376 | tf_op jit(solution)/shard_map/ppermute | solution.py:31
  29.7 0.0 collective-permute-done.4
  29.7 3.9 %collective-permute-done.6 = bf16[8,16,576]{2,1,0:T(8,128)(2,1)S(1)} collective-permute-done((bf16[8,16,576]{2,1,0:T(8,128)(2,1)S(1)}, bf16[8,16,576]{2,1,0:T(8,128)(2,1)S(1)}, u32[]{:S(2)}, u32[]{:S(2)}) %collective-permute-start.6) | collective-permute-done | bytes 147488 | tf_op jit(solution)/shard_map/ppermute | solution.py:31
  33.6 3.0 %collective-permute-start.9 = (bf16[32,16,576]{2,1,0:T(8,128)(2,1)S(1)}, bf16[32,16,576]{2,1,0:T(8,128)(2,1)S(1)}, u32[]{:S(2)}, u32[]{:S(2)}) collective-permute-start(bf16[32,16,576]{2,1,0:T(8,128)(2,1)S(1)} %constant_dynamic-update-slice_fusion.5.refs_0_), channel_id=1, source_target_pairs={{4,0},{10,8},{20,16},{26,24},{36,32},{42,40},{52,48},{58,56},{68,6... | collective-permute-start | bytes 1769480 | tf_op jit(solution)/shard_map/ppermute | solution.py:31
  36.6 0.4 collective-permute-start.8
  37.0 2.3 %collective-permute-start.7 = (bf16[32,16,576]{2,1,0:T(8,128)(2,1)S(1)}, bf16[32,16,576]{2,1,0:T(8,128)(2,1)S(1)}, u32[]{:S(2)}, u32[]{:S(2)}) collective-permute-start(bf16[32,16,576]{2,1,0:T(8,128)(2,1)S(1)} %constant_dynamic-update-slice_fusion.5.refs_0_), channel_id=1, source_target_pairs={{128,0},{9,8},{144,16},{25,24},{160,32},{41,40},{176,48},{57,56},{... | collective-permute-start | bytes 1769480 | tf_op jit(solution)/shard_map/ppermute | solution.py:31
  39.3 8.4 %collective-permute-start.10 = (bf16[32,16,576]{2,1,0:T(8,128)(2,1)S(1)}, bf16[32,16,576]{2,1,0:T(8,128)(2,1)S(1)}, u32[]{:S(2)}, u32[]{:S(2)}) collective-permute-start(bf16[32,16,576]{2,1,0:T(8,128)(2,1)S(1)} %constant_dynamic-update-slice_fusion.5.refs_0_), channel_id=1, source_target_pairs={{0,8},{8,0},{16,24},{24,16},{32,40},{40,32},{48,56},{56,48},{64,72... | collective-permute-start | bytes 1769480 | tf_op jit(solution)/shard_map/ppermute | solution.py:35
  47.7 0.0 collective-permute-done.9.refs_3_
  47.7 5.4 %collective-permute-start.13 = (bf16[32,16,576]{2,1,0:T(8,128)(2,1)S(1)}, bf16[32,16,576]{2,1,0:T(8,128)(2,1)S(1)}, u32[]{:S(2)}, u32[]{:S(2)}) collective-permute-start(bf16[32,16,576]{2,1,0:T(8,128)(2,1)S(1)} %collective-permute-done.9.refs_3_), channel_id=1, source_target_pairs={{0,8},{8,0},{16,24},{24,16},{32,40},{40,32},{48,56},{56,48},{64,72... | collective-permute-start | bytes 1769480 | tf_op jit(solution)/shard_map/ppermute | solution.py:35
  53.1 0.1 collective-permute-done.8.refs_2_
  53.2 6.9 %collective-permute-start.12 = (bf16[32,16,576]{2,1,0:T(8,128)(2,1)S(1)}, bf16[32,16,576]{2,1,0:T(8,128)(2,1)S(1)}, u32[]{:S(2)}, u32[]{:S(2)}) collective-permute-start(bf16[32,16,576]{2,1,0:T(8,128)(2,1)S(1)} %collective-permute-done.8.refs_2_), channel_id=1, source_target_pairs={{0,8},{8,0},{16,24},{24,16},{32,40},{40,32},{48,56},{56,48},{64,72... | collective-permute-start | bytes 1769480 | tf_op jit(solution)/shard_map/ppermute | solution.py:35
  60.0 0.0 collective-permute-done.7.refs_1_
  60.0 0.0 collective-permute-start.11
  60.0 1.7 %collective-permute-done.12.refs_6_ = bf16[32,16,576]{2,1,0:T(8,128)(2,1)S(1)} collective-permute-done((bf16[32,16,576]{2,1,0:T(8,128)(2,1)S(1)}, bf16[32,16,576]{2,1,0:T(8,128)(2,1)S(1)}, u32[]{:S(2)}, u32[]{:S(2)}) %collective-permute-start.12) | collective-permute-done | bytes 589856 | tf_op jit(solution)/shard_map/ppermute | solution.py:35
  61.7 0.9 %collective-permute-done.11.refs_5_ = bf16[32,16,576]{2,1,0:T(8,128)(2,1)S(1)} collective-permute-done((bf16[32,16,576]{2,1,0:T(8,128)(2,1)S(1)}, bf16[32,16,576]{2,1,0:T(8,128)(2,1)S(1)}, u32[]{:S(2)}, u32[]{:S(2)}) %collective-permute-start.11) | collective-permute-done | bytes 589856 | tf_op jit(solution)/shard_map/ppermute | solution.py:35
  62.7 1.7 %copy-done = bf16[2,1024,576]{2,1,0:T(8,128)(2,1)S(1)} copy-done((bf16[2,1024,576]{2,1,0:T(8,128)(2,1)S(1)}, bf16[2,1024,576]{2,1,0:T(8,128)(2,1)}, u32[]{:S(2)}) %copy-start) | copy-done | bytes 2359320
  64.4 20.7 %attention.1 = bf16[128,2048]{1,0:T(8,128)(2,1)} custom-call(s32[64]{0:T(128)S(1)} %copy-done.2, bf16[2,1024,576]{2,1,0:T(8,128)(2,1)S(1)} %copy-done, bf16[32,16,576]{2,1,0:T(8,128)(2,1)S(1)} %constant_dynamic-update-slice_fusion.5.refs_0_, bf16[32,16,576]{2,1,0:T(8,128)(2,1)S(1)} %collective-permute-done.7.refs_1_, ...), custom_call_target="tpu_custom_call" | custom-call | flops 9697230848 | bytes 10485760 | tf_op jit(solution)/shard_map/attention/pallas_call | solution.py:186
  (14 shorter events, 0.1 us)
Async XLA Ops:
  0.0 12.9 %collective-permute-start.1 = (bf16[1,16,576]{2,1,0:T(8,128)(2,1)}, bf16[1,16,576]{2,1,0:T(8,128)(2,1)S(1)}, u32[]{:S(2)}, u32[]{:S(2)}) collective-permute-start(bf16[1,16,576]{2,1,0:T(8,128)(2,1)} %bitcast.3), channel_id=1, source_target_pairs={{112,0},{120,8},{0,16},{8,24},{16,32},{24,40},{32,48},{40,56},{48,... | collective-permute-start | bytes 55304 | tf_op jit(solution)/shard_map/ppermute | solution.py:31
  2.5 5.1 %collective-permute-start = (bf16[1,16,576]{2,1,0:T(8,128)(2,1)}, bf16[1,16,576]{2,1,0:T(8,128)(2,1)S(1)}, u32[]{:S(2)}, u32[]{:S(2)}) collective-permute-start(bf16[1,16,576]{2,1,0:T(8,128)(2,1)} %bitcast.4), channel_id=1, source_target_pairs={{16,0},{24,8},{32,16},{40,24},{48,32},{56,40},{64,48},{72,56},{80,... | collective-permute-start | bytes 55304 | tf_op jit(solution)/shard_map/ppermute | solution.py:31
  8.3 10.3 %collective-permute-start.3 = (bf16[2,16,576]{2,1,0:T(8,128)(2,1)S(1)}, bf16[2,16,576]{2,1,0:T(8,128)(2,1)S(1)}, u32[]{:S(2)}, u32[]{:S(2)}) collective-permute-start(bf16[2,16,576]{2,1,0:T(8,128)(2,1)S(1)} %pad_maximum_fusion.1), channel_id=1, source_target_pairs={{80,0},{88,8},{96,16},{104,24},{112,32},{120,40},{0,48},{8,56},{16... | collective-permute-start | bytes 110600 | tf_op jit(solution)/shard_map/ppermute | solution.py:31
  13.6 5.0 %collective-permute-start.2 = (bf16[3,16,576]{2,1,0:T(8,128)(2,1)S(1)}, bf16[3,16,576]{2,1,0:T(8,128)(2,1)S(1)}, u32[]{:S(2)}, u32[]{:S(2)}) collective-permute-start(bf16[3,16,576]{2,1,0:T(8,128)(2,1)S(1)} %pad_maximum_fusion), channel_id=1, source_target_pairs={{48,0},{56,8},{64,16},{72,24},{80,32},{88,40},{96,48},{104,56},{11... | collective-permute-start | bytes 165896 | tf_op jit(solution)/shard_map/ppermute | solution.py:31
  18.6 44.0 %copy-start.1 = (bf16[16,512,128]{2,1,0:T(8,128)(2,1)S(1)}, bf16[16,512,128]{2,1,0:T(8,128)(2,1)}, u32[]{:S(2)}) copy-start(bf16[16,512,128]{2,1,0:T(8,128)(2,1)} %refs_8_.1) | copy-start | bytes 6291460
  18.7 44.0 %copy-start.2 = (s32[64]{0:T(128)S(1)}, s32[64]{0:T(128)}, u32[]{:S(2)}) copy-start(s32[64]{0:T(128)} %starts_ref.1) | copy-start | bytes 772
  18.7 11.0 %collective-permute-start.4 = (bf16[8,16,576]{2,1,0:T(8,128)(2,1)S(1)}, bf16[8,16,576]{2,1,0:T(8,128)(2,1)S(1)}, u32[]{:S(2)}, u32[]{:S(2)}) collective-permute-start(bf16[8,16,576]{2,1,0:T(8,128)(2,1)S(1)} %get-tuple-element.11), channel_id=1, source_target_pairs={{1,0},{136,8},{17,16},{152,24},{33,32},{168,40},{49,48},{184,56},{... | collective-permute-start | bytes 442376 | tf_op jit(solution)/shard_map/ppermute | solution.py:31
  21.2 8.5 %collective-permute-start.5 = (bf16[8,16,576]{2,1,0:T(8,128)(2,1)S(1)}, bf16[8,16,576]{2,1,0:T(8,128)(2,1)S(1)}, u32[]{:S(2)}, u32[]{:S(2)}) collective-permute-start(bf16[8,16,576]{2,1,0:T(8,128)(2,1)S(1)} %get-tuple-element.11), channel_id=1, source_target_pairs={{3,0},{140,8},{19,16},{156,24},{35,32},{172,40},{51,48},{188,56},{... | collective-permute-start | bytes 442376 | tf_op jit(solution)/shard_map/ppermute | solution.py:31
  27.9 5.7 %collective-permute-start.6 = (bf16[8,16,576]{2,1,0:T(8,128)(2,1)S(1)}, bf16[8,16,576]{2,1,0:T(8,128)(2,1)S(1)}, u32[]{:S(2)}, u32[]{:S(2)}) collective-permute-start(bf16[8,16,576]{2,1,0:T(8,128)(2,1)S(1)} %get-tuple-element.11), channel_id=1, source_target_pairs={{2,0},{12,8},{18,16},{28,24},{34,32},{44,40},{50,48},{60,56},{66,6... | collective-permute-start | bytes 442376 | tf_op jit(solution)/shard_map/ppermute | solution.py:31
  33.6 14.0 %collective-permute-start.9 = (bf16[32,16,576]{2,1,0:T(8,128)(2,1)S(1)}, bf16[32,16,576]{2,1,0:T(8,128)(2,1)S(1)}, u32[]{:S(2)}, u32[]{:S(2)}) collective-permute-start(bf16[32,16,576]{2,1,0:T(8,128)(2,1)S(1)} %constant_dynamic-update-slice_fusion.5.refs_0_), channel_id=1, source_target_pairs={{4,0},{10,8},{20,16},{26,24},{36,32},{42,40},{52,48},{58,56},{68,6... | collective-permute-start | bytes 1769480 | tf_op jit(solution)/shard_map/ppermute | solution.py:31
  36.6 16.5 %collective-permute-start.8 = (bf16[32,16,576]{2,1,0:T(8,128)(2,1)S(1)}, bf16[32,16,576]{2,1,0:T(8,128)(2,1)S(1)}, u32[]{:S(2)}, u32[]{:S(2)}) collective-permute-start(bf16[32,16,576]{2,1,0:T(8,128)(2,1)S(1)} %constant_dynamic-update-slice_fusion.5.refs_0_), channel_id=1, source_target_pairs={{132,0},{11,8},{148,16},{27,24},{164,32},{43,40},{180,48},{59,56},... | collective-permute-start | bytes 1769480 | tf_op jit(solution)/shard_map/ppermute | solution.py:31
  37.0 23.0 %collective-permute-start.7 = (bf16[32,16,576]{2,1,0:T(8,128)(2,1)S(1)}, bf16[32,16,576]{2,1,0:T(8,128)(2,1)S(1)}, u32[]{:S(2)}, u32[]{:S(2)}) collective-permute-start(bf16[32,16,576]{2,1,0:T(8,128)(2,1)S(1)} %constant_dynamic-update-slice_fusion.5.refs_0_), channel_id=1, source_target_pairs={{128,0},{9,8},{144,16},{25,24},{160,32},{41,40},{176,48},{57,56},{... | collective-permute-start | bytes 1769480 | tf_op jit(solution)/shard_map/ppermute | solution.py:31
  39.3 20.7 %collective-permute-start.10 = (bf16[32,16,576]{2,1,0:T(8,128)(2,1)S(1)}, bf16[32,16,576]{2,1,0:T(8,128)(2,1)S(1)}, u32[]{:S(2)}, u32[]{:S(2)}) collective-permute-start(bf16[32,16,576]{2,1,0:T(8,128)(2,1)S(1)} %constant_dynamic-update-slice_fusion.5.refs_0_), channel_id=1, source_target_pairs={{0,8},{8,0},{16,24},{24,16},{32,40},{40,32},{48,56},{56,48},{64,72... | collective-permute-start | bytes 1769480 | tf_op jit(solution)/shard_map/ppermute | solution.py:35
  47.7 12.4 %collective-permute-start.13 = (bf16[32,16,576]{2,1,0:T(8,128)(2,1)S(1)}, bf16[32,16,576]{2,1,0:T(8,128)(2,1)S(1)}, u32[]{:S(2)}, u32[]{:S(2)}) collective-permute-start(bf16[32,16,576]{2,1,0:T(8,128)(2,1)S(1)} %collective-permute-done.9.refs_3_), channel_id=1, source_target_pairs={{0,8},{8,0},{16,24},{24,16},{32,40},{40,32},{48,56},{56,48},{64,72... | collective-permute-start | bytes 1769480 | tf_op jit(solution)/shard_map/ppermute | solution.py:35
  53.2 8.6 %collective-permute-start.12 = (bf16[32,16,576]{2,1,0:T(8,128)(2,1)S(1)}, bf16[32,16,576]{2,1,0:T(8,128)(2,1)S(1)}, u32[]{:S(2)}, u32[]{:S(2)}) collective-permute-start(bf16[32,16,576]{2,1,0:T(8,128)(2,1)S(1)} %collective-permute-done.8.refs_2_), channel_id=1, source_target_pairs={{0,8},{8,0},{16,24},{24,16},{32,40},{40,32},{48,56},{56,48},{64,72... | collective-permute-start | bytes 1769480 | tf_op jit(solution)/shard_map/ppermute | solution.py:35
  60.0 2.7 %collective-permute-start.11 = (bf16[32,16,576]{2,1,0:T(8,128)(2,1)S(1)}, bf16[32,16,576]{2,1,0:T(8,128)(2,1)S(1)}, u32[]{:S(2)}, u32[]{:S(2)}) collective-permute-start(bf16[32,16,576]{2,1,0:T(8,128)(2,1)S(1)} %collective-permute-done.7.refs_1_), channel_id=1, source_target_pairs={{0,8},{8,0},{16,24},{24,16},{32,40},{40,32},{48,56},{56,48},{64,72... | collective-permute-start | bytes 1769480 | tf_op jit(solution)/shard_map/ppermute | solution.py:35
  62.7 1.7 %copy-start = (bf16[2,1024,576]{2,1,0:T(8,128)(2,1)S(1)}, bf16[2,1024,576]{2,1,0:T(8,128)(2,1)}, u32[]{:S(2)}) copy-start(bf16[2,1024,576]{2,1,0:T(8,128)(2,1)} %make_queries.1.query_ref) | copy-start | bytes 7077892

commit v3 on v2

v3 whole, which is shorter than its diff:
```python
import functools
import math

import jax
import jax.numpy as jnp
from jax import lax
from jax.experimental import pallas as pl
from jax.experimental.pallas import tpu as pltpu
from jax.sharding import PartitionSpec as P

BOTH = ("ctx", "head")
PIECE = 16
TILE = 256
CHUNK = 1024
NOPE = 128
OFFSETS = (0, 1, 3, 2)
WINDOW = (0, 1, 7, 3, 4, 2, 5, 6)


def device_index(x, y, z, core):
    return (((x % 2) * 8 + z) * 2 + core) * 8 + (x // 2) * 4 + y


def from_offset(value, first, second):
    pairs = []
    for x in range(4):
        for y in range(4):
            for z in range(8):
                for core in range(2):
                    dx, dy, dz = second if core else first
                    source = device_index((x + dx) % 4, (y + dy) % 4, (z + dz) % 8, core)
                    pairs.append((source, device_index(x, y, z, core)))
    return lax.ppermute(value, BOTH, pairs)


def other_core(value):
    return lax.ppermute(value, "ctx", [(i, i ^ 1) for i in range(32)])


def gather_own_core(latent, query):
    latent = latent[None]
    up = from_offset(latent, (0, 0, 1), (0, 0, 1))
    down = from_offset(latent, (0, 0, 7), (0, 0, 7))
    window = jnp.concatenate([latent, up, down])
    far_up = from_offset(window, (0, 0, 3), (0, 0, 3))
    far_down = from_offset(window, (0, 0, 5), (0, 0, 5))[:2]
    column = jnp.concatenate([window, far_up, far_down])
    column, query = lax.optimization_barrier((column, query))
    plane = jnp.concatenate(
        [column] + [from_offset(column, (0, d, 0), (d, 0, 0)) for d in OFFSETS[1:]]
    )
    own = [plane] + [from_offset(plane, (d, 0, 0), (0, d, 0)) for d in OFFSETS[1:]]
    return own, query


def query_kernel(nope_ref, rope_ref, uk_ref, query_ref):
    latent_width = uk_ref.shape[2]
    nope_width = uk_ref.shape[1]
    rope_width = rope_ref.shape[1] // uk_ref.shape[0]
    block = nope_ref.shape[0] // 2
    for head in range(uk_ref.shape[0]):
        lat = jnp.dot(
            nope_ref[:, head * nope_width : (head + 1) * nope_width],
            uk_ref[head],
            preferred_element_type=jnp.float32,
        ).astype(jnp.bfloat16)
        rope = rope_ref[:, head * rope_width : (head + 1) * rope_width]
        for half in range(2):
            rows = slice(half * block, (half + 1) * block)
            to = slice(head * block, (head + 1) * block)
            query_ref[half, to, :latent_width] = lat[rows]
            query_ref[half, to, latent_width:] = rope[rows]


def make_queries(q_nope, q_rope, w_uk):
    rows = q_nope.shape[0]
    heads, nope_width, latent_width = w_uk.shape
    rope_width = q_rope.shape[1] // heads
    at_once = 4
    width = latent_width + rope_width
    return pl.pallas_call(
        query_kernel,
        grid=(heads // at_once,),
        in_specs=[
            pl.BlockSpec((rows, at_once * nope_width), lambda g: (0, g)),
            pl.BlockSpec((rows, at_once * rope_width), lambda g: (0, g)),
            pl.BlockSpec((at_once, nope_width, latent_width), lambda g: (g, 0, 0)),
        ],
        out_specs=pl.BlockSpec((2, at_once * rows // 2, width), lambda g: (0, g, 0)),
        out_shape=jax.ShapeDtypeStruct((2, heads * rows // 2, width), jnp.bfloat16),
        cost_estimate=pl.CostEstimate(
            flops=2 * rows * heads * nope_width * latent_width,
            bytes_accessed=6 * 2**20,
            transcendentals=0,
        ),
        name="make_queries",
    )(q_nope, q_rope, w_uk)


def absorb_kernel(last, finish, starts_ref, query_ref, own_ref, other_ref, *refs):
    state_in = refs[: 3 if last else 0]
    refs = refs[len(state_in) :]
    if finish:
        uv_ref, out_ref, keys, marks, acc, top, total = refs
    else:
        acc, top, total, keys, marks = refs
    ctx, head_group = lax.axis_index("ctx"), lax.axis_index("head")
    x = (head_group // 4) * 2 + ctx // 16
    y, z, core = head_group % 4, (ctx // 2) % 8, ctx % 2
    rows = query_ref.shape[1]
    block, width = 4 * PIECE, query_ref.shape[2]
    latent_width = acc.shape[1]
    factor = math.log2(math.e) / math.sqrt(NOPE + width - latent_width)
    low, high = starts_ref[2 * ctx], starts_ref[2 * ctx + 1]

    def column(owner, middle, first):
        px = (x + jnp.where(owner == 0, OFFSETS[last], OFFSETS[middle])) % 4
        py = (y + jnp.where(owner == 0, OFFSETS[middle], OFFSETS[last])) % 4
        pz = (z + WINDOW[first]) % 8
        return starts_ref[2 * (((px % 2) * 8 + pz) * 2 + owner) + px // 2], py

    pieces = []
    for ref, owner in ((own_ref, core), (other_ref, 1 - core)):
        for middle in range(4):
            for first in range(8):
                start, py = column(owner, middle, first)
                pieces.append((ref, middle * 8 + first, start, py))
    below = sum([jnp.where(p[2] <= low, 1, 0) for p in pieces[1:]], jnp.where(pieces[0][2] <= low, 1, 0))
    keys[...] = jnp.zeros(keys.shape, keys.dtype)
    marks[...] = jnp.full(marks.shape, 64.0, marks.dtype)
    lane = lax.broadcasted_iota(jnp.int32, (PIECE, 128), 1)
    row = lax.broadcasted_iota(jnp.int32, (PIECE, 128), 0)
    next_low, next_high = jnp.int32(0), below
    for ref, at, start, py in pieces:
        is_low = start <= low
        is_high = (start > low) & (start <= high)
        to = pl.multiple_of(
            jnp.where(is_low, next_low, jnp.where(is_high, next_high, len(pieces))) * PIECE, PIECE
        )
        keys[pl.ds(to, PIECE), :] = ref[at]
        mark = jnp.where(lane == 0, start // 64, jnp.where(lane == 1, row + py * PIECE, 0))
        marks[pl.ds(to, PIECE), :] = mark.astype(jnp.float32).astype(jnp.bfloat16)
        next_low = next_low + jnp.where(is_low, 1, 0)
        next_high = next_high + jnp.where(is_high, 1, 0)

    if last:
        for to_ref, from_ref in zip((acc, top, total), state_in):
            to_ref[...] = from_ref[...]
    else:
        top[...] = jnp.full(top.shape, -1e30, jnp.float32)
        total[...] = jnp.zeros(total.shape, jnp.float32)
        acc[...] = jnp.zeros(acc.shape, jnp.float32)

    read_lane = lax.broadcasted_iota(jnp.int32, (PIECE, 128), 1)
    read = jnp.where(read_lane == 0, 64.0, jnp.where(read_lane == 1, 1.0, 0.0)).astype(jnp.bfloat16)
    query_row = lax.broadcasted_iota(jnp.int32, (block, TILE), 0).astype(jnp.float32)
    per_tile = TILE // PIECE
    tiles_low = (below + per_tile - 1) // per_tile
    tiles_high = (next_high + per_tile - 1) // per_tile

    @pl.loop(0, tiles_low + tiles_high)
    def _(step):
        is_high = step >= tiles_low
        half = jnp.where(is_high, 1, 0)
        at = pl.multiple_of((step - half * tiles_low) * TILE, TILE)
        start = jnp.where(is_high, high, low)
        tile = keys[pl.ds(at, TILE), :]
        position = lax.dot_general(
            read, marks[pl.ds(at, TILE), :], (((1,), (1,)), ((), ())),
            preferred_element_type=jnp.float32,
        )
        position = jnp.broadcast_to(position[:1, :], (block, TILE))
        allowed = position - start.astype(jnp.float32) <= query_row
        for c in range(rows // CHUNK):
            s = lax.dot_general(
                query_ref[half, c * CHUNK : (c + 1) * CHUNK, :],
                tile,
                (((1,), (1,)), ((), ())),
                preferred_element_type=jnp.float32,
            )
            s = jnp.where(allowed[None], s.reshape(CHUNK // block, block, TILE), -1e30)
            s = s.reshape(CHUNK, TILE)
            own = pl.ds(pl.multiple_of(half * rows + c * CHUNK, CHUNK), CHUNK)
            left, right = s[:, :128], s[:, 128:]
            old = top[own, :]
            new = jnp.maximum(old, jnp.max(jnp.maximum(left, right), axis=1, keepdims=True))
            scale = jnp.exp2((old - new) * factor)
            left = jnp.exp2((left - new) * factor)
            right = jnp.exp2((right - new) * factor)
            top[own, :] = new
            total[own, :] = total[own, :] * scale + (left + right)
            weights = jnp.concatenate([left, right], axis=1).astype(jnp.bfloat16)
            scales = jnp.concatenate([scale] * (latent_width // 128), axis=1)
            acc[own, :] = acc[own, :] * scales + jnp.dot(
                weights, tile[:, :latent_width], preferred_element_type=jnp.float32
            )

    if finish:
        value_width = uv_ref.shape[2]
        for h in range(uv_ref.shape[0]):
            lat = []
            for half in range(2):
                own = slice(half * rows + h * block, half * rows + (h + 1) * block)
                whole = jnp.sum(total[own, :], axis=1, keepdims=True)
                lat.append((acc[own, :] / whole).astype(jnp.bfloat16))
            out_ref[:, h * value_width : (h + 1) * value_width] = jnp.dot(
                jnp.concatenate(lat), uv_ref[h], preferred_element_type=jnp.float32
            ).astype(jnp.bfloat16)


def absorb(last, block_start, query, own, other, state, w_uv):
    heads, latent_width, value_width = w_uv.shape
    rows, width = query.shape[1:]
    finish = last == len(OFFSETS) - 1
    count = 2 * own.shape[0] * own.shape[1]
    vmem = pl.BlockSpec(memory_space=pltpu.VMEM)
    state_shapes = [(2 * rows, latent_width), (2 * rows, 128), (2 * rows, 128)]
    scratch = [
        pltpu.VMEM((count + PIECE, width), jnp.bfloat16),
        pltpu.VMEM((count + PIECE, 128), jnp.bfloat16),
    ]
    operands = [block_start, query, own, other, *state]
    if finish:
        operands.append(w_uv)
        scratch += [pltpu.VMEM(shape, jnp.float32) for shape in state_shapes]
        out_shape = jax.ShapeDtypeStruct((2 * rows // heads, heads * value_width), jnp.bfloat16)
    else:
        out_shape = [jax.ShapeDtypeStruct(shape, jnp.float32) for shape in state_shapes]
    return pl.pallas_call(
        functools.partial(absorb_kernel, last, finish),
        in_specs=[pl.BlockSpec(memory_space=pltpu.SMEM)] + [vmem] * (len(operands) - 1),
        out_specs=vmem if finish else [vmem] * 3,
        out_shape=out_shape,
        scratch_shapes=scratch,
        compiler_params=pltpu.CompilerParams(vmem_limit_bytes=24 * 2**20),
        cost_estimate=pl.CostEstimate(
            flops=rows * count * width,
            bytes_accessed=2**20,
            transcendentals=0,
        ),
        name=f"absorb_{last}",
    )(*operands)


def shards(q_nope, q_rope, latent, block_start, w_uk, w_uv):
    query = make_queries(q_nope, q_rope, w_uk)
    own, query = gather_own_core(latent, query)
    state = ()
    for last, piece in enumerate(own):
        if last:
            piece, state = lax.optimization_barrier((piece, state))
        state = absorb(last, block_start, query, piece, other_core(piece), state, w_uv)
    return state


def solution(mesh):
    placed = (P("ctx", "head"), P("ctx", "head"), P(BOTH, None), P(), P("head"), P("head"))
    return jax.shard_map(
        shards, mesh=mesh, in_specs=placed, out_specs=P("ctx", "head"), check_vma=False
    )
```

time: 85.6 us -> 92 us (1.075)
  the two profiles are of different devices: /device:TPU:1 before, /device:TPU:4 now
where the time goes in v3:
time: 92 us; the launch traced here: 90.5 us
  Pallas kernels  42.3 us (46%)
  starting transfers between devices  23.7 us (26%)
  waiting for transfers between devices  21.7 us (24%)
  local copies, waits for them, and re-layouts  2.67 us (3%)
    pallas_call x4, Pallas kernels, absorb(): pl.pallas_call(functools.partial(absorb_kernel, last, finish), in_specs=[...  37.7 us
    ppermute x10, starting transfers between devices, from_offset(): return lax.ppermute(value, BOTH, pairs)  21.9 us
    ppermute x10, waiting for transfers between devices, from_offset(): return lax.ppermute(value, BOTH, pairs)  17.7 us
    pallas_call x1, Pallas kernels, make_queries(): pl.pallas_call(query_kernel, grid=(heads // at_once,), in_specs=[pl.Block...  4.59 us
    ppermute x4, waiting for transfers between devices, other_core(): return lax.ppermute(value, 'ctx', [(i, i ^ 1) for i in range(32)])  3.93 us
    unnamed x15, local copies, waits for them, and re-layouts  2.63 us
  transfers between devices with their start and end apart: 14, of which 8 were waited for; matrix products, arithmetic and copies ran while one was open for 1% of the time, Pallas kernels for 33%

profile of v3, /device:TPU:4, one launch (start us, length us, event | category | flops | bytes accessed | tf_op | source)
XLA Modules:
  0.0 90.5 jit_solution(1575846098764030897)
XLA Ops:
  0.0 5.9 %collective-permute-start = (bf16[1,16,576]{2,1,0:T(8,128)(2,1)}, bf16[1,16,576]{2,1,0:T(8,128)(2,1)S(1)}, u32[]{:S(2)}, u32[]{:S(2)}) collective-permute-start(bf16[1,16,576]{2,1,0:T(8,128)(2,1)} %bitcast.2), channel_id=1, source_target_pairs={{16,0},{24,8},{32,16},{40,24},{48,32},{56,40},{64,48},{72,56},{80,... | collective-permute-start | bytes 55304 | tf_op jit(solution)/shard_map/ppermute | solution.py:33
  5.9 0.0 collective-permute-start.1
  5.9 0.8 constant_dynamic-update-slice_fusion.3
  6.7 4.6 %make_queries.1.query_ref = bf16[2,1024,576]{2,1,0:T(8,128)(2,1)} custom-call(bf16[128,2048]{1,0:T(8,128)(2,1)} %nope_ref.1, bf16[128,1024]{1,0:T(8,128)(2,1)} %rope_ref.1, bf16[16,128,512]{2,1,0:T(8,128)(2,1)} %uk_ref.1), custom_call_target="tpu_custom_call" | custom-call | flops 268435456 | bytes 6291456 | tf_op jit(solution)/shard_map/make_queries/pallas_call | solution.py:81
  11.3 0.0 collective-permute-done
  11.3 0.0 collective-permute-done.1
  11.3 3.0 %collective-permute-start.2 = (bf16[3,16,576]{2,1,0:T(8,128)(2,1)S(1)}, bf16[3,16,576]{2,1,0:T(8,128)(2,1)S(1)}, u32[]{:S(2)}, u32[]{:S(2)}) collective-permute-start(bf16[3,16,576]{2,1,0:T(8,128)(2,1)S(1)} %pad_maximum_fusion), channel_id=1, source_target_pairs={{48,0},{56,8},{64,16},{72,24},{80,32},{88,40},{96,48},{104,56},{11... | collective-permute-start | bytes 165896 | tf_op jit(solution)/shard_map/ppermute | solution.py:33
  14.3 0.9 %collective-permute-start.3 = (bf16[3,16,576]{2,1,0:T(8,128)(2,1)S(1)}, bf16[3,16,576]{2,1,0:T(8,128)(2,1)S(1)}, u32[]{:S(2)}, u32[]{:S(2)}) collective-permute-start(bf16[3,16,576]{2,1,0:T(8,128)(2,1)S(1)} %pad_maximum_fusion), channel_id=1, source_target_pairs={{80,0},{88,8},{96,16},{104,24},{112,32},{120,40},{0,48},{8,56},{16... | collective-permute-start | bytes 165896 | tf_op jit(solution)/shard_map/ppermute | solution.py:33
  15.2 3.6 %collective-permute-done.2 = bf16[3,16,576]{2,1,0:T(8,128)(2,1)S(1)} collective-permute-done((bf16[3,16,576]{2,1,0:T(8,128)(2,1)S(1)}, bf16[3,16,576]{2,1,0:T(8,128)(2,1)S(1)}, u32[]{:S(2)}, u32[]{:S(2)}) %collective-permute-start.2) | collective-permute-done | bytes 55328 | tf_op jit(solution)/shard_map/ppermute | solution.py:33
  18.8 4.3 %collective-permute-done.3 = bf16[3,16,576]{2,1,0:T(8,128)(2,1)S(1)} collective-permute-done((bf16[3,16,576]{2,1,0:T(8,128)(2,1)S(1)}, bf16[3,16,576]{2,1,0:T(8,128)(2,1)S(1)}, u32[]{:S(2)}, u32[]{:S(2)}) %collective-permute-start.3) | collective-permute-done | bytes 55328 | tf_op jit(solution)/shard_map/ppermute | solution.py:33
  23.1 3.0 %collective-permute-start.4 = (bf16[8,16,576]{2,1,0:T(8,128)(2,1)S(1)}, bf16[8,16,576]{2,1,0:T(8,128)(2,1)S(1)}, u32[]{:S(2)}, u32[]{:S(2)}) collective-permute-start(bf16[8,16,576]{2,1,0:T(8,128)(2,1)S(1)} %slice_dynamic-update-slice_fusion), channel_id=1, source_target_pairs={{1,0},{136,8},{17,16},{152,24},{33,32},{168,40},{49,48},{184,56},{... | collective-permute-start | bytes 442376 | tf_op jit(solution)/shard_map/ppermute | solution.py:33
  26.1 0.0 collective-permute-start.5
  26.1 2.3 %collective-permute-start.6 = (bf16[8,16,576]{2,1,0:T(8,128)(2,1)S(1)}, bf16[8,16,576]{2,1,0:T(8,128)(2,1)S(1)}, u32[]{:S(2)}, u32[]{:S(2)}) collective-permute-start(bf16[8,16,576]{2,1,0:T(8,128)(2,1)S(1)} %slice_dynamic-update-slice_fusion), channel_id=1, source_target_pairs={{2,0},{12,8},{18,16},{28,24},{34,32},{44,40},{50,48},{60,56},{66,6... | collective-permute-start | bytes 442376 | tf_op jit(solution)/shard_map/ppermute | solution.py:33
  28.4 0.5 collective-permute-done.4
  29.0 5.4 %collective-permute-done.5 = bf16[8,16,576]{2,1,0:T(8,128)(2,1)S(1)} collective-permute-done((bf16[8,16,576]{2,1,0:T(8,128)(2,1)S(1)}, bf16[8,16,576]{2,1,0:T(8,128)(2,1)S(1)}, u32[]{:S(2)}, u32[]{:S(2)}) %collective-permute-start.5) | collective-permute-done | bytes 147488 | tf_op jit(solution)/shard_map/ppermute | solution.py:33
  34.4 0.0 collective-permute-done.6
  34.5 0.1 collective-permute-start.10
  34.6 0.6 collective-permute-start.9
  35.2 1.5 %collective-permute-done.10.other_ref = bf16[32,16,576]{2,1,0:T(8,128)(2,1)S(1)} collective-permute-done((bf16[32,16,576]{2,1,0:T(8,128)(2,1)S(1)}, bf16[32,16,576]{2,1,0:T(8,128)(2,1)S(1)}, u32[]{:S(2)}, u32[]{:S(2)}) %collective-permute-start.10) | collective-permute-done | bytes 589856 | tf_op jit(solution)/shard_map/ppermute | solution.py:37
  36.6 1.7 %copy-done = bf16[2,1024,576]{2,1,0:T(8,128)(2,1)S(1)} copy-done((bf16[2,1024,576]{2,1,0:T(8,128)(2,1)S(1)}, bf16[2,1024,576]{2,1,0:T(8,128)(2,1)}, u32[]{:S(2)}) %copy-start) | copy-done | bytes 2359320
  38.4 7.6 %absorb_0.1 = (f32[2048,512]{1,0:T(8,128)S(1)}, f32[2048,128]{1,0:T(8,128)S(1)}, f32[2048,128]{1,0:T(8,128)S(1)}) custom-call(s32[64]{0:T(128)S(1)} %copy-done.2, bf16[2,1024,576]{2,1,0:T(8,128)(2,1)S(1)} %copy-done, bf16[32,16,576]{2,1,0:T(8,128)(2,1)S(1)} %constant_dynamic-update-slice_fusion.4.own_ref, ...), custom_call_target="tpu_custom_call" | custom-call | flops 603979776 | bytes 1048576 | tf_op jit(solution)/shard_map/absorb_0/pallas_call | solution.py:229
  46.0 0.0 collective-permute-done.9.own_ref
  46.0 1.6 %collective-permute-start.11 = (bf16[32,16,576]{2,1,0:T(8,128)(2,1)S(1)}, bf16[32,16,576]{2,1,0:T(8,128)(2,1)S(1)}, u32[]{:S(2)}, u32[]{:S(2)}) collective-permute-start(bf16[32,16,576]{2,1,0:T(8,128)(2,1)S(1)} %collective-permute-done.9.own_ref), channel_id=1, source_target_pairs={{0,8},{8,0},{16,24},{24,16},{32,40},{40,32},{48,56},{56,48},{64,72... | collective-permute-start | bytes 1769480 | tf_op jit(solution)/shard_map/ppermute | solution.py:37
  47.7 1.3 %collective-permute-start.8 = (bf16[32,16,576]{2,1,0:T(8,128)(2,1)S(1)}, bf16[32,16,576]{2,1,0:T(8,128)(2,1)S(1)}, u32[]{:S(2)}, u32[]{:S(2)}) collective-permute-start(bf16[32,16,576]{2,1,0:T(8,128)(2,1)S(1)} %constant_dynamic-update-slice_fusion.4.own_ref), channel_id=1, source_target_pairs={{132,0},{11,8},{148,16},{27,24},{164,32},{43,40},{180,48},{59,56},... | collective-permute-start | bytes 1769480 | tf_op jit(solution)/shard_map/ppermute | solution.py:33
  49.0 0.4 collective-permute-done.11.other_ref
  49.4 6.2 %absorb_1.1 = (f32[2048,512]{1,0:T(8,128)S(1)}, f32[2048,128]{1,0:T(8,128)S(1)}, f32[2048,128]{1,0:T(8,128)S(1)}) custom-call(s32[64]{0:T(128)S(1)} %copy-done.2, bf16[2,1024,576]{2,1,0:T(8,128)(2,1)S(1)} %copy-done, bf16[32,16,576]{2,1,0:T(8,128)(2,1)S(1)} %collective-permute-done.9.own_ref, bf16[32,16,576]{2,1,0:T(8,128)(2,1)S(1)} %collective-permute-done.11.other_ref, ...), custom_call_target="tpu_custom_call" | custom-call | flops 603979776 | bytes 1048576 | tf_op jit(solution)/shard_map/absorb_1/pallas_call | solution.py:229
  55.6 3.9 %collective-permute-done.8.own_ref = bf16[32,16,576]{2,1,0:T(8,128)(2,1)S(1)} collective-permute-done((bf16[32,16,576]{2,1,0:T(8,128)(2,1)S(1)}, bf16[32,16,576]{2,1,0:T(8,128)(2,1)S(1)}, u32[]{:S(2)}, u32[]{:S(2)}) %collective-permute-start.8) | collective-permute-done | bytes 589856 | tf_op jit(solution)/shard_map/ppermute | solution.py:33
  59.6 4.9 %collective-permute-start.7 = (bf16[32,16,576]{2,1,0:T(8,128)(2,1)S(1)}, bf16[32,16,576]{2,1,0:T(8,128)(2,1)S(1)}, u32[]{:S(2)}, u32[]{:S(2)}) collective-permute-start(bf16[32,16,576]{2,1,0:T(8,128)(2,1)S(1)} %constant_dynamic-update-slice_fusion.4.own_ref), channel_id=1, source_target_pairs={{4,0},{10,8},{20,16},{26,24},{36,32},{42,40},{52,48},{58,56},{68,6... | collective-permute-start | bytes 1769480 | tf_op jit(solution)/shard_map/ppermute | solution.py:33
  64.5 11.8 %absorb_2.1 = (f32[2048,512]{1,0:T(8,128)S(1)}, f32[2048,128]{1,0:T(8,128)S(1)}, f32[2048,128]{1,0:T(8,128)S(1)}) custom-call(s32[64]{0:T(128)S(1)} %copy-done.2, bf16[2,1024,576]{2,1,0:T(8,128)(2,1)S(1)} %copy-done, bf16[32,16,576]{2,1,0:T(8,128)(2,1)S(1)} %collective-permute-done.8.own_ref, bf16[32,16,576]{2,1,0:T(8,128)(2,1)S(1)} %collective-permute-done.12.other_ref, ...), custom_call_target="tpu_custom_call" | custom-call | flops 603979776 | bytes 1048576 | tf_op jit(solution)/shard_map/absorb_2/pallas_call | solution.py:229
  76.3 0.1 collective-permute-start.13
  76.4 2.1 %collective-permute-done.13.other_ref = bf16[32,16,576]{2,1,0:T(8,128)(2,1)S(1)} collective-permute-done((bf16[32,16,576]{2,1,0:T(8,128)(2,1)S(1)}, bf16[32,16,576]{2,1,0:T(8,128)(2,1)S(1)}, u32[]{:S(2)}, u32[]{:S(2)}) %collective-permute-start.13) | collective-permute-done | bytes 589856 | tf_op jit(solution)/shard_map/ppermute | solution.py:37
  78.4 12.0 %absorb_3.1 = bf16[128,2048]{1,0:T(8,128)(2,1)} custom-call(s32[64]{0:T(128)S(1)} %copy-done.2, bf16[2,1024,576]{2,1,0:T(8,128)(2,1)S(1)} %copy-done, bf16[32,16,576]{2,1,0:T(8,128)(2,1)S(1)} %collective-permute-done.7.own_ref, bf16[32,16,576]{2,1,0:T(8,128)(2,1)S(1)} %collective-permute-done.13.other_ref, f32[2048,512]{1,0:T(8,128)S(1)} %get-tuple-element.48.refs_0_, ...), custom_call_target="tpu_custom_call" | custom-call | flops 603979776 | bytes 1048576 | tf_op jit(solution)/shard_map/absorb_3/pallas_call | solution.py:229
  (19 shorter events, 0.2 us)
Async XLA Ops:
  0.0 11.3 %copy-start.3 = (bf16[16,576]{1,0:T(8,128)(2,1)S(1)}, bf16[16,576]{1,0:T(8,128)(2,1)}, u32[]{:S(2)}) copy-start(bf16[16,576]{1,0:T(8,128)(2,1)} %param.8) | copy-start | bytes 55300
  0.0 36.6 %copy-start.2 = (s32[64]{0:T(128)S(1)}, s32[64]{0:T(128)}, u32[]{:S(2)}) copy-start(s32[64]{0:T(128)} %starts_ref.7) | copy-start | bytes 772
  0.0 11.3 %collective-permute-start = (bf16[1,16,576]{2,1,0:T(8,128)(2,1)}, bf16[1,16,576]{2,1,0:T(8,128)(2,1)S(1)}, u32[]{:S(2)}, u32[]{:S(2)}) collective-permute-start(bf16[1,16,576]{2,1,0:T(8,128)(2,1)} %bitcast.2), channel_id=1, source_target_pairs={{16,0},{24,8},{32,16},{40,24},{48,32},{56,40},{64,48},{72,56},{80,... | collective-permute-start | bytes 55304 | tf_op jit(solution)/shard_map/ppermute | solution.py:33
  5.9 5.4 %collective-permute-start.1 = (bf16[1,16,576]{2,1,0:T(8,128)(2,1)}, bf16[1,16,576]{2,1,0:T(8,128)(2,1)S(1)}, u32[]{:S(2)}, u32[]{:S(2)}) collective-permute-start(bf16[1,16,576]{2,1,0:T(8,128)(2,1)} %bitcast.3), channel_id=1, source_target_pairs={{112,0},{120,8},{0,16},{8,24},{16,32},{24,40},{32,48},{40,56},{48,... | collective-permute-start | bytes 55304 | tf_op jit(solution)/shard_map/ppermute | solution.py:33
  11.3 7.5 %collective-permute-start.2 = (bf16[3,16,576]{2,1,0:T(8,128)(2,1)S(1)}, bf16[3,16,576]{2,1,0:T(8,128)(2,1)S(1)}, u32[]{:S(2)}, u32[]{:S(2)}) collective-permute-start(bf16[3,16,576]{2,1,0:T(8,128)(2,1)S(1)} %pad_maximum_fusion), channel_id=1, source_target_pairs={{48,0},{56,8},{64,16},{72,24},{80,32},{88,40},{96,48},{104,56},{11... | collective-permute-start | bytes 165896 | tf_op jit(solution)/shard_map/ppermute | solution.py:33
  14.3 8.8 %collective-permute-start.3 = (bf16[3,16,576]{2,1,0:T(8,128)(2,1)S(1)}, bf16[3,16,576]{2,1,0:T(8,128)(2,1)S(1)}, u32[]{:S(2)}, u32[]{:S(2)}) collective-permute-start(bf16[3,16,576]{2,1,0:T(8,128)(2,1)S(1)} %pad_maximum_fusion), channel_id=1, source_target_pairs={{80,0},{88,8},{96,16},{104,24},{112,32},{120,40},{0,48},{8,56},{16... | collective-permute-start | bytes 165896 | tf_op jit(solution)/shard_map/ppermute | solution.py:33
  23.1 5.8 %collective-permute-start.4 = (bf16[8,16,576]{2,1,0:T(8,128)(2,1)S(1)}, bf16[8,16,576]{2,1,0:T(8,128)(2,1)S(1)}, u32[]{:S(2)}, u32[]{:S(2)}) collective-permute-start(bf16[8,16,576]{2,1,0:T(8,128)(2,1)S(1)} %slice_dynamic-update-slice_fusion), channel_id=1, source_target_pairs={{1,0},{136,8},{17,16},{152,24},{33,32},{168,40},{49,48},{184,56},{... | collective-permute-start | bytes 442376 | tf_op jit(solution)/shard_map/ppermute | solution.py:33
  26.1 8.3 %collective-permute-start.5 = (bf16[8,16,576]{2,1,0:T(8,128)(2,1)S(1)}, bf16[8,16,576]{2,1,0:T(8,128)(2,1)S(1)}, u32[]{:S(2)}, u32[]{:S(2)}) collective-permute-start(bf16[8,16,576]{2,1,0:T(8,128)(2,1)S(1)} %slice_dynamic-update-slice_fusion), channel_id=1, source_target_pairs={{3,0},{140,8},{19,16},{156,24},{35,32},{172,40},{51,48},{188,56},{... | collective-permute-start | bytes 442376 | tf_op jit(solution)/shard_map/ppermute | solution.py:33
  26.1 8.3 %collective-permute-start.6 = (bf16[8,16,576]{2,1,0:T(8,128)(2,1)S(1)}, bf16[8,16,576]{2,1,0:T(8,128)(2,1)S(1)}, u32[]{:S(2)}, u32[]{:S(2)}) collective-permute-start(bf16[8,16,576]{2,1,0:T(8,128)(2,1)S(1)} %slice_dynamic-update-slice_fusion), channel_id=1, source_target_pairs={{2,0},{12,8},{18,16},{28,24},{34,32},{44,40},{50,48},{60,56},{66,6... | collective-permute-start | bytes 442376 | tf_op jit(solution)/shard_map/ppermute | solution.py:33
  34.5 2.2 %collective-permute-start.10 = (bf16[32,16,576]{2,1,0:T(8,128)(2,1)S(1)}, bf16[32,16,576]{2,1,0:T(8,128)(2,1)S(1)}, u32[]{:S(2)}, u32[]{:S(2)}) collective-permute-start(bf16[32,16,576]{2,1,0:T(8,128)(2,1)S(1)} %constant_dynamic-update-slice_fusion.4.own_ref), channel_id=1, source_target_pairs={{0,8},{8,0},{16,24},{24,16},{32,40},{40,32},{48,56},{56,48},{64,72... | collective-permute-start | bytes 1769480 | tf_op jit(solution)/shard_map/ppermute | solution.py:37
  34.6 11.5 %collective-permute-start.9 = (bf16[32,16,576]{2,1,0:T(8,128)(2,1)S(1)}, bf16[32,16,576]{2,1,0:T(8,128)(2,1)S(1)}, u32[]{:S(2)}, u32[]{:S(2)}) collective-permute-start(bf16[32,16,576]{2,1,0:T(8,128)(2,1)S(1)} %constant_dynamic-update-slice_fusion.4.own_ref), channel_id=1, source_target_pairs={{128,0},{9,8},{144,16},{25,24},{160,32},{41,40},{176,48},{57,56},{... | collective-permute-start | bytes 1769480 | tf_op jit(solution)/shard_map/ppermute | solution.py:33
  36.6 1.7 %copy-start = (bf16[2,1024,576]{2,1,0:T(8,128)(2,1)S(1)}, bf16[2,1024,576]{2,1,0:T(8,128)(2,1)}, u32[]{:S(2)}) copy-start(bf16[2,1024,576]{2,1,0:T(8,128)(2,1)} %make_queries.1.query_ref) | copy-start | bytes 7077892
  46.0 3.3 %collective-permute-start.11 = (bf16[32,16,576]{2,1,0:T(8,128)(2,1)S(1)}, bf16[32,16,576]{2,1,0:T(8,128)(2,1)S(1)}, u32[]{:S(2)}, u32[]{:S(2)}) collective-permute-start(bf16[32,16,576]{2,1,0:T(8,128)(2,1)S(1)} %collective-permute-done.9.own_ref), channel_id=1, source_target_pairs={{0,8},{8,0},{16,24},{24,16},{32,40},{40,32},{48,56},{56,48},{64,72... | collective-permute-start | bytes 1769480 | tf_op jit(solution)/shard_map/ppermute | solution.py:37
  47.7 11.9 %collective-permute-start.8 = (bf16[32,16,576]{2,1,0:T(8,128)(2,1)S(1)}, bf16[32,16,576]{2,1,0:T(8,128)(2,1)S(1)}, u32[]{:S(2)}, u32[]{:S(2)}) collective-permute-start(bf16[32,16,576]{2,1,0:T(8,128)(2,1)S(1)} %constant_dynamic-update-slice_fusion.4.own_ref), channel_id=1, source_target_pairs={{132,0},{11,8},{148,16},{27,24},{164,32},{43,40},{180,48},{59,56},... | collective-permute-start | bytes 1769480 | tf_op jit(solution)/shard_map/ppermute | solution.py:33
  59.5 18.9 %copy-start.1 = (bf16[16,512,128]{2,1,0:T(8,128)(2,1)S(1)}, bf16[16,512,128]{2,1,0:T(8,128)(2,1)}, u32[]{:S(2)}) copy-start(bf16[16,512,128]{2,1,0:T(8,128)(2,1)} %refs_3_.1) | copy-start | bytes 6291460
  59.5 4.9 %collective-permute-start.12 = (bf16[32,16,576]{2,1,0:T(8,128)(2,1)S(1)}, bf16[32,16,576]{2,1,0:T(8,128)(2,1)S(1)}, u32[]{:S(2)}, u32[]{:S(2)}) collective-permute-start(bf16[32,16,576]{2,1,0:T(8,128)(2,1)S(1)} %collective-permute-done.8.own_ref), channel_id=1, source_target_pairs={{0,8},{8,0},{16,24},{24,16},{32,40},{40,32},{48,56},{56,48},{64,72... | collective-permute-start | bytes 1769480 | tf_op jit(solution)/shard_map/ppermute | solution.py:37
  59.6 16.7 %collective-permute-start.7 = (bf16[32,16,576]{2,1,0:T(8,128)(2,1)S(1)}, bf16[32,16,576]{2,1,0:T(8,128)(2,1)S(1)}, u32[]{:S(2)}, u32[]{:S(2)}) collective-permute-start(bf16[32,16,576]{2,1,0:T(8,128)(2,1)S(1)} %constant_dynamic-update-slice_fusion.4.own_ref), channel_id=1, source_target_pairs={{4,0},{10,8},{20,16},{26,24},{36,32},{42,40},{52,48},{58,56},{68,6... | collective-permute-start | bytes 1769480 | tf_op jit(solution)/shard_map/ppermute | solution.py:33
  76.3 2.2 %collective-permute-start.13 = (bf16[32,16,576]{2,1,0:T(8,128)(2,1)S(1)}, bf16[32,16,576]{2,1,0:T(8,128)(2,1)S(1)}, u32[]{:S(2)}, u32[]{:S(2)}) collective-permute-start(bf16[32,16,576]{2,1,0:T(8,128)(2,1)S(1)} %collective-permute-done.7.own_ref), channel_id=1, source_target_pairs={{0,8},{8,0},{16,24},{24,16},{32,40},{40,32},{48,56},{56,48},{64,72... | collective-permute-start | bytes 1769480 | tf_op jit(solution)/shard_map/ppermute | solution.py:37

commit v4 on v2

--- a/solution.py
+++ b/solution.py
@@ -10,7 +10,9 @@
 
 BOTH = ("ctx", "head")
 PIECE = 16
-TILE = 512
+TILE = 256
+CHUNK = 1024
+QCHUNK = 1024
 OFFSETS = (0, 1, 3, 2)
 WINDOW = (0, 1, 7, 3, 4, 2, 5, 6)
 
@@ -41,14 +43,14 @@
     down = from_offset(latent, (0, 0, 7), (0, 0, 7))
     window = jnp.concatenate([latent, up, down])
     far_up = from_offset(window, (0, 0, 3), (0, 0, 3))
-    far_down = from_offset(window[:2], (0, 0, 5), (0, 0, 5))
+    far_down = from_offset(window, (0, 0, 5), (0, 0, 5))[:2]
     column = jnp.concatenate([window, far_up, far_down])
     plane = jnp.concatenate(
         [column] + [from_offset(column, (0, d, 0), (d, 0, 0)) for d in OFFSETS[1:]]
     )
-    plane, query = lax.optimization_barrier((plane, query))
-    own = [plane] + [from_offset(plane, (d, 0, 0), (0, d, 0)) for d in OFFSETS[1:]]
-    return own, query
+    lines = [from_offset(plane, (d, 0, 0), (0, d, 0)) for d in OFFSETS[1:]]
+    *lines, query = lax.optimization_barrier((*lines, query))
+    return [plane, *lines], query
 
 
 def query_kernel(nope_ref, rope_ref, uk_ref, query_ref):
@@ -74,18 +76,14 @@
     rows = q_nope.shape[0]
     heads, nope_width, latent_width = w_uk.shape
     rope_width = q_rope.shape[1] // heads
-    at_once = 2
     width = latent_width + rope_width
+    vmem = pl.BlockSpec(memory_space=pltpu.VMEM)
     return pl.pallas_call(
         query_kernel,
-        grid=(heads // at_once,),
-        in_specs=[
-            pl.BlockSpec((rows, at_once * nope_width), lambda g: (0, g)),
-            pl.BlockSpec((rows, at_once * rope_width), lambda g: (0, g)),
-            pl.BlockSpec((at_once, nope_width, latent_width), lambda g: (g, 0, 0)),
-        ],
-        out_specs=pl.BlockSpec((2, at_once * rows // 2, width), lambda g: (0, g, 0)),
+        in_specs=[vmem] * 3,
+        out_specs=vmem,
         out_shape=jax.ShapeDtypeStruct((2, heads * rows // 2, width), jnp.bfloat16),
+        compiler_params=pltpu.CompilerParams(vmem_limit_bytes=12 * 2**20),
         cost_estimate=pl.CostEstimate(
             flops=2 * rows * heads * nope_width * latent_width,
             bytes_accessed=6 * 2**20,
@@ -97,7 +95,7 @@
 
 def attention_kernel(starts_ref, query_ref, *refs):
     pieces = refs[:8]
-    uv_ref, out_ref, keys, scores, top, total, acc = refs[8:]
+    uv_ref, out_ref, keys, even, odd, top, total, acc = refs[8:]
     ctx, head_group = lax.axis_index("ctx"), lax.axis_index("head")
     x = (head_group // 4) * 2 + ctx // 16
     y, z, core = head_group % 4, (ctx // 2) % 8, ctx % 2
@@ -122,58 +120,76 @@
     ahead = lax.broadcasted_iota(jnp.int32, (block, TILE), 0) - lax.broadcasted_iota(
         jnp.int32, (block, TILE), 1
     )
-    chunk = 16 * block
-
-    @pl.loop(0, 2)
-    def _(half):
-        start = starts_ref[2 * ctx + half]
-        tiles = start // TILE + 1
+    chunk = CHUNK
+    start0, start1 = starts_ref[2 * ctx], starts_ref[2 * ctx + 1]
+    steps0, steps1 = start0 // (2 * TILE) + 1, start1 // (2 * TILE) + 1
+
+    def place(step):
+        half = jnp.where(step >= steps0, 1, 0)
+        start = jnp.where(half == 1, start1, start0)
+        return half, start, (step - half * steps0) * (2 * TILE)
+
+    def score(buffer, half, start, at):
+        at = pl.multiple_of(jnp.minimum(at, keys.shape[0] - TILE), TILE)
+        tile = keys[pl.ds(at, TILE), :]
+        allowed = ahead >= at - start
+        for c in range(rows // QCHUNK):
+            own = slice(c * QCHUNK, (c + 1) * QCHUNK)
+            s = lax.dot_general(
+                query_ref[half, own, :],
+                tile,
+                (((1,), (1,)), ((), ())),
+                preferred_element_type=jnp.float32,
+            )
+            s = jnp.where(allowed[None], s.reshape(QCHUNK // block, block, TILE), -1e30)
+            buffer[own, :] = s.reshape(QCHUNK, TILE)
+
+    def absorb(buffer, at):
+        tile = keys[pl.ds(pl.multiple_of(at, TILE), TILE), :latent_width]
+        for c in range(rows // chunk):
+            own = slice(c * chunk, (c + 1) * chunk)
+            left, right = buffer[own, :128], buffer[own, 128:]
+            old = top[own, :]
+            new = jnp.maximum(old, jnp.max(jnp.maximum(left, right), axis=1, keepdims=True))
+            scale = jnp.exp2((old - new) * factor)
+            left = jnp.exp2((left - new) * factor)
+            right = jnp.exp2((right - new) * factor)
+            top[own, :] = new
+            total[own, :] = total[own, :] * scale + (left + right)
+            weights = jnp.concatenate([left, right], axis=1).astype(jnp.bfloat16)
+            scales = jnp.concatenate([scale] * (latent_width // 128), axis=1)
+            acc[own, :] = acc[own, :] * scales + jnp.dot(
+                weights, tile, preferred_element_type=jnp.float32
+            )
+
+    def clear():
         top[...] = jnp.full(top.shape, -1e30, jnp.float32)
-
-        @pl.loop(0, tiles)
-        def _(j):
-            at = pl.multiple_of(j * TILE, TILE)
-            tile = keys[pl.ds(at, TILE), :]
-            allowed = ahead >= at - start
-            for c in range(rows // chunk):
-                own = slice(c * chunk, (c + 1) * chunk)
-                s = lax.dot_general(
-                    query_ref[half, own, :],
-                    tile,
-                    (((1,), (1,)), ((), ())),
-                    preferred_element_type=jnp.float32,
-                )
-                s = jnp.where(allowed[None], s.reshape(chunk // block, block, TILE), -1e30)
-                s = s.reshape(chunk, TILE)
-                scores[own, pl.ds(at, TILE)] = s
-                top[own, :] = functools.reduce(jnp.maximum, [s[:, i:i+128] for i in range(0, TILE, 128)], top[own, :])
-
-        top[...] = jnp.broadcast_to(
-            jnp.max(top[...], axis=1, keepdims=True) * factor, top.shape
-        )
         total[...] = jnp.zeros(total.shape, jnp.float32)
         acc[...] = jnp.zeros(acc.shape, jnp.float32)
 
-        @pl.loop(0, tiles)
-        def _(j):
-            at = pl.multiple_of(j * TILE, TILE)
-            tile = keys[pl.ds(at, TILE), :latent_width]
-            for c in range(rows // chunk):
-                own = slice(c * chunk, (c + 1) * chunk)
-                shift = top[own, :]
-                parts = [jnp.exp2(scores[own, pl.ds(at + i, 128)] * factor - shift) for i in range(0, TILE, 128)]
-                total[own, :] += sum(parts[1:], parts[0])
-                weights = jnp.concatenate(parts, axis=1).astype(jnp.bfloat16)
-                acc[own, :] += jnp.dot(weights, tile, preferred_element_type=jnp.float32)
-
-        to = pl.ds(pl.multiple_of(half * block, block), block)
-        for h in range(count):
-            own = slice(h * block, (h + 1) * block)
-            whole = jnp.sum(total[own, :], axis=1, keepdims=True)
-            lat = (acc[own, :] / whole).astype(jnp.bfloat16)
-            out_ref[to, h * value_width : (h + 1) * value_width] = jnp.dot(
-                lat, uv_ref[h], preferred_element_type=jnp.float32
-            ).astype(jnp.bfloat16)
+    clear()
+    score(even, 0, start0, 0)
+
+    @pl.loop(0, steps0 + steps1)
+    def _(step):
+        half, start, at = place(step)
+        score(odd, half, start, at + TILE)
+        absorb(even, at)
+        half_next, start_next, at_next = place(step + 1)
+        score(even, half_next, start_next, at_next)
+        absorb(odd, at + TILE)
+
+        @pl.when((step == steps0 - 1) | (step == steps0 + steps1 - 1))
+        def _():
+            to = pl.ds(pl.multiple_of(half * block, block), block)
+            for h in range(count):
+                own = slice(h * block, (h + 1) * block)
+                whole = jnp.sum(total[own, :], axis=1, keepdims=True)
+                lat = (acc[own, :] / whole).astype(jnp.bfloat16)
+                out_ref[to, h * value_width : (h + 1) * value_width] = jnp.dot(
+                    lat, uv_ref[h], preferred_element_type=jnp.float32
+                ).astype(jnp.bfloat16)
+            clear()
 
 
 def attend(block_start, query, pieces, w_uv):
@@ -190,12 +206,13 @@
         out_shape=jax.ShapeDtypeStruct((2 * block, heads * value_width), jnp.bfloat16),
         scratch_shapes=[
             pltpu.VMEM((keys, width), jnp.bfloat16),
-            pltpu.VMEM((rows, keys), jnp.float32),
+            pltpu.VMEM((rows, TILE), jnp.float32),
+            pltpu.VMEM((rows, TILE), jnp.float32),
             pltpu.VMEM((rows, 128), jnp.float32),
             pltpu.VMEM((rows, 128), jnp.float32),
             pltpu.VMEM((rows, latent_width), jnp.float32),
         ],
-        compiler_params=pltpu.CompilerParams(vmem_limit_bytes=30 * 2**20),
+        compiler_params=pltpu.CompilerParams(vmem_limit_bytes=20 * 2**20),
         cost_estimate=pl.CostEstimate(
             flops=2 * rows * (keys + 256) * (width + latent_width),
             bytes_accessed=10 * 2**20,

time: 85.6 us -> 83.1 us (0.971)
  Pallas kernels: 27.4 us -> 19.9 us
  starting transfers between devices: 41.7 us -> 43.9 us
  waiting for transfers between devices: 11.8 us -> 13.8 us
  local copies, waits for them, and re-layouts: 2.64 us -> 4.48 us
    pallas_call x1, Pallas kernels: 6.69 us -> 0.76 us  [make_queries(): pl.pallas_call(query_kernel, in_specs=[vmem] * 3, out_specs=vmem, out_sha...]
    ppermute x4, starting transfers between devices: 20.7 us -> 22.9 us  [other_core(): return lax.ppermute(value, 'ctx', [(i, i ^ 1) for i in range(32)])]
    unnamed x12 -> x16, local copies, waits for them, and re-layouts: 2.61 us -> 4.44 us
    pallas_call x1, Pallas kernels: 20.7 us -> 19.2 us  [attend(): pl.pallas_call(attention_kernel, in_specs=[pl.BlockSpec(memory_space=pltp...]
    ppermute x10, waiting for transfers between devices: 9.13 us -> 10.7 us  [from_offset(): return lax.ppermute(value, BOTH, pairs)]
  transfers between devices with their start and end apart: 14 -> 14, of which waited for: 6 -> 7; matrix products, arithmetic and copies ran while one was open for 3% -> 1% of each run, Pallas kernels for 8% -> 1%
where the time goes in v4:
time: 83.1 us; the launch traced here: 82.8 us
  starting transfers between devices  43.9 us (53%)
  Pallas kernels  19.9 us (24%)
  waiting for transfers between devices  13.8 us (17%)
  local copies, waits for them, and re-layouts  4.48 us (5%)
    ppermute x4, starting transfers between devices, other_core(): return lax.ppermute(value, 'ctx', [(i, i ^ 1) for i in range(32)])  22.9 us
    ppermute x10, starting transfers between devices, from_offset(): return lax.ppermute(value, BOTH, pairs)  20.9 us
    pallas_call x1, Pallas kernels, attend(): pl.pallas_call(attention_kernel, in_specs=[pl.BlockSpec(memory_space=pltp...  19.2 us
    ppermute x10, waiting for transfers between devices, from_offset(): return lax.ppermute(value, BOTH, pairs)  10.7 us
    unnamed x16, local copies, waits for them, and re-layouts  4.44 us
    ppermute x4, waiting for transfers between devices, other_core(): return lax.ppermute(value, 'ctx', [(i, i ^ 1) for i in range(32)])  3.09 us
  transfers between devices with their start and end apart: 14, of which 7 were waited for; matrix products, arithmetic and copies ran while one was open for 1% of the time, Pallas kernels for 1%

profile of v4, /device:TPU:1, one launch (start us, length us, event | category | flops | bytes accessed | tf_op | source)
XLA Modules:
  0.0 82.8 jit_solution(6171584314326857100)
XLA Ops:
  0.0 2.5 %collective-permute-start.1 = (bf16[1,16,576]{2,1,0:T(8,128)(2,1)}, bf16[1,16,576]{2,1,0:T(8,128)(2,1)S(1)}, u32[]{:S(2)}, u32[]{:S(2)}) collective-permute-start(bf16[1,16,576]{2,1,0:T(8,128)(2,1)} %bitcast.3), channel_id=1, source_target_pairs={{112,0},{120,8},{0,16},{8,24},{16,32},{24,40},{32,48},{40,56},{48,... | collective-permute-start | bytes 55304 | tf_op jit(solution)/shard_map/ppermute | solution.py:33
  2.5 3.9 %collective-permute-start = (bf16[1,16,576]{2,1,0:T(8,128)(2,1)}, bf16[1,16,576]{2,1,0:T(8,128)(2,1)S(1)}, u32[]{:S(2)}, u32[]{:S(2)}) collective-permute-start(bf16[1,16,576]{2,1,0:T(8,128)(2,1)} %bitcast.4), channel_id=1, source_target_pairs={{16,0},{24,8},{32,16},{40,24},{48,32},{56,40},{64,48},{72,56},{80,... | collective-permute-start | bytes 55304 | tf_op jit(solution)/shard_map/ppermute | solution.py:33
  6.4 0.8 constant_dynamic-update-slice_fusion.3
  7.2 0.6 collective-permute-done.1
  7.8 0.7 pad_maximum_fusion
  8.5 4.4 %collective-permute-start.3 = (bf16[3,16,576]{2,1,0:T(8,128)(2,1)S(1)}, bf16[3,16,576]{2,1,0:T(8,128)(2,1)S(1)}, u32[]{:S(2)}, u32[]{:S(2)}) collective-permute-start(bf16[3,16,576]{2,1,0:T(8,128)(2,1)S(1)} %pad_maximum_fusion), channel_id=1, source_target_pairs={{80,0},{88,8},{96,16},{104,24},{112,32},{120,40},{0,48},{8,56},{16... | collective-permute-start | bytes 165896 | tf_op jit(solution)/shard_map/ppermute | solution.py:33
  12.9 0.2 collective-permute-start.2
  13.1 4.7 %collective-permute-done.2 = bf16[3,16,576]{2,1,0:T(8,128)(2,1)S(1)} collective-permute-done((bf16[3,16,576]{2,1,0:T(8,128)(2,1)S(1)}, bf16[3,16,576]{2,1,0:T(8,128)(2,1)S(1)}, u32[]{:S(2)}, u32[]{:S(2)}) %collective-permute-start.2) | collective-permute-done | bytes 55328 | tf_op jit(solution)/shard_map/ppermute | solution.py:33
  17.8 0.0 collective-permute-done.3
  17.8 2.6 %collective-permute-start.4 = (bf16[8,16,576]{2,1,0:T(8,128)(2,1)S(1)}, bf16[8,16,576]{2,1,0:T(8,128)(2,1)S(1)}, u32[]{:S(2)}, u32[]{:S(2)}) collective-permute-start(bf16[8,16,576]{2,1,0:T(8,128)(2,1)S(1)} %get-tuple-element.13), channel_id=1, source_target_pairs={{1,0},{136,8},{17,16},{152,24},{33,32},{168,40},{49,48},{184,56},{... | collective-permute-start | bytes 442376 | tf_op jit(solution)/shard_map/ppermute | solution.py:33
  20.4 1.7 %collective-permute-start.6 = (bf16[8,16,576]{2,1,0:T(8,128)(2,1)S(1)}, bf16[8,16,576]{2,1,0:T(8,128)(2,1)S(1)}, u32[]{:S(2)}, u32[]{:S(2)}) collective-permute-start(bf16[8,16,576]{2,1,0:T(8,128)(2,1)S(1)} %get-tuple-element.13), channel_id=1, source_target_pairs={{2,0},{12,8},{18,16},{28,24},{34,32},{44,40},{50,48},{60,56},{66,6... | collective-permute-start | bytes 442376 | tf_op jit(solution)/shard_map/ppermute | solution.py:33
  22.1 0.5 collective-permute-done.4
  22.7 4.8 %collective-permute-done.5 = bf16[8,16,576]{2,1,0:T(8,128)(2,1)S(1)} collective-permute-done((bf16[8,16,576]{2,1,0:T(8,128)(2,1)S(1)}, bf16[8,16,576]{2,1,0:T(8,128)(2,1)S(1)}, u32[]{:S(2)}, u32[]{:S(2)}) %collective-permute-start.5) | collective-permute-done | bytes 147488 | tf_op jit(solution)/shard_map/ppermute | solution.py:33
  27.5 0.0 copy-start.4
  27.6 3.0 %collective-permute-start.9 = (bf16[32,16,576]{2,1,0:T(8,128)(2,1)S(1)}, bf16[32,16,576]{2,1,0:T(8,128)(2,1)S(1)}, u32[]{:S(2)}, u32[]{:S(2)}) collective-permute-start(bf16[32,16,576]{2,1,0:T(8,128)(2,1)S(1)} %constant_dynamic-update-slice_fusion.4.refs_0_), channel_id=1, source_target_pairs={{4,0},{10,8},{20,16},{26,24},{36,32},{42,40},{52,48},{58,56},{68,6... | collective-permute-start | bytes 1769480 | tf_op jit(solution)/shard_map/ppermute | solution.py:33
  30.6 0.5 collective-permute-start.8
  31.1 2.2 %collective-permute-start.7 = (bf16[32,16,576]{2,1,0:T(8,128)(2,1)S(1)}, bf16[32,16,576]{2,1,0:T(8,128)(2,1)S(1)}, u32[]{:S(2)}, u32[]{:S(2)}) collective-permute-start(bf16[32,16,576]{2,1,0:T(8,128)(2,1)S(1)} %constant_dynamic-update-slice_fusion.4.refs_0_), channel_id=1, source_target_pairs={{128,0},{9,8},{144,16},{25,24},{160,32},{41,40},{176,48},{57,56},{... | collective-permute-start | bytes 1769480 | tf_op jit(solution)/shard_map/ppermute | solution.py:33
  33.3 1.6 %copy-done = bf16[16,128,512]{2,1,0:T(8,128)(2,1)S(1)} copy-done((bf16[16,128,512]{2,1,0:T(8,128)(2,1)S(1)}, bf16[16,128,512]{2,1,0:T(8,128)(2,1)}, u32[]{:S(2)}) %copy-start) | copy-done | bytes 2097176
  34.9 1.0 %copy-done.1 = bf16[128,2048]{1,0:T(8,128)(2,1)S(1)} copy-done((bf16[128,2048]{1,0:T(8,128)(2,1)S(1)}, bf16[128,2048]{1,0:T(8,128)(2,1)}, u32[]{:S(2)}) %copy-start.1) | copy-done | bytes 524312
  35.9 0.9 %copy-done.2 = bf16[128,1024]{1,0:T(8,128)(2,1)S(1)} copy-done((bf16[128,1024]{1,0:T(8,128)(2,1)S(1)}, bf16[128,1024]{1,0:T(8,128)(2,1)}, u32[]{:S(2)}) %copy-start.2) | copy-done | bytes 262168
  36.9 0.8 make_queries.1.query_ref
  37.6 13.9 %collective-permute-start.10 = (bf16[32,16,576]{2,1,0:T(8,128)(2,1)S(1)}, bf16[32,16,576]{2,1,0:T(8,128)(2,1)S(1)}, u32[]{:S(2)}, u32[]{:S(2)}) collective-permute-start(bf16[32,16,576]{2,1,0:T(8,128)(2,1)S(1)} %constant_dynamic-update-slice_fusion.4.refs_0_), channel_id=1, source_target_pairs={{0,8},{8,0},{16,24},{24,16},{32,40},{40,32},{48,56},{56,48},{64,72... | collective-permute-start | bytes 1769480 | tf_op jit(solution)/shard_map/ppermute | solution.py:37
  51.5 0.0 collective-permute-done.9.refs_3_
  51.5 0.0 collective-permute-done.8.refs_2_
  51.5 0.0 collective-permute-done.7.refs_1_
  51.6 8.5 %collective-permute-start.11 = (bf16[32,16,576]{2,1,0:T(8,128)(2,1)S(1)}, bf16[32,16,576]{2,1,0:T(8,128)(2,1)S(1)}, u32[]{:S(2)}, u32[]{:S(2)}) collective-permute-start(bf16[32,16,576]{2,1,0:T(8,128)(2,1)S(1)} %collective-permute-done.7.refs_1_), channel_id=1, source_target_pairs={{0,8},{8,0},{16,24},{24,16},{32,40},{40,32},{48,56},{56,48},{64,72... | collective-permute-start | bytes 1769480 | tf_op jit(solution)/shard_map/ppermute | solution.py:37
  60.1 0.0 collective-permute-start.12
  60.1 0.5 collective-permute-start.13
  60.6 1.2 %collective-permute-done.11.refs_5_ = bf16[32,16,576]{2,1,0:T(8,128)(2,1)S(1)} collective-permute-done((bf16[32,16,576]{2,1,0:T(8,128)(2,1)S(1)}, bf16[32,16,576]{2,1,0:T(8,128)(2,1)S(1)}, u32[]{:S(2)}, u32[]{:S(2)}) %collective-permute-start.11) | collective-permute-done | bytes 589856 | tf_op jit(solution)/shard_map/ppermute | solution.py:37
  61.8 0.9 %collective-permute-done.12.refs_6_ = bf16[32,16,576]{2,1,0:T(8,128)(2,1)S(1)} collective-permute-done((bf16[32,16,576]{2,1,0:T(8,128)(2,1)S(1)}, bf16[32,16,576]{2,1,0:T(8,128)(2,1)S(1)}, u32[]{:S(2)}, u32[]{:S(2)}) %collective-permute-start.12) | collective-permute-done | bytes 589856 | tf_op jit(solution)/shard_map/ppermute | solution.py:37
  62.7 0.9 %collective-permute-done.13.refs_7_ = bf16[32,16,576]{2,1,0:T(8,128)(2,1)S(1)} collective-permute-done((bf16[32,16,576]{2,1,0:T(8,128)(2,1)S(1)}, bf16[32,16,576]{2,1,0:T(8,128)(2,1)S(1)}, u32[]{:S(2)}, u32[]{:S(2)}) %collective-permute-start.13) | collective-permute-done | bytes 589856 | tf_op jit(solution)/shard_map/ppermute | solution.py:37
  63.7 19.2 %attention.1 = bf16[128,2048]{1,0:T(8,128)(2,1)} custom-call(s32[64]{0:T(128)S(1)} %copy-done.4, bf16[2,1024,576]{2,1,0:T(8,128)(2,1)S(1)} %make_queries.1.query_ref, bf16[32,16,576]{2,1,0:T(8,128)(2,1)S(1)} %constant_dynamic-update-slice_fusion.4.refs_0_, bf16[32,16,576]{2,1,0:T(8,128)(2,1)S(1)} %collective-permute-done.7.refs_1_, ...), custom_call_target="tpu_custom_call" | custom-call | flops 9697230848 | bytes 10485760 | tf_op jit(solution)/shard_map/attention/pallas_call | solution.py:202
  (17 shorter events, 0.1 us)
Async XLA Ops:
  0.0 7.8 %collective-permute-start.1 = (bf16[1,16,576]{2,1,0:T(8,128)(2,1)}, bf16[1,16,576]{2,1,0:T(8,128)(2,1)S(1)}, u32[]{:S(2)}, u32[]{:S(2)}) collective-permute-start(bf16[1,16,576]{2,1,0:T(8,128)(2,1)} %bitcast.3), channel_id=1, source_target_pairs={{112,0},{120,8},{0,16},{8,24},{16,32},{24,40},{32,48},{40,56},{48,... | collective-permute-start | bytes 55304 | tf_op jit(solution)/shard_map/ppermute | solution.py:33
  2.5 5.3 %collective-permute-start = (bf16[1,16,576]{2,1,0:T(8,128)(2,1)}, bf16[1,16,576]{2,1,0:T(8,128)(2,1)S(1)}, u32[]{:S(2)}, u32[]{:S(2)}) collective-permute-start(bf16[1,16,576]{2,1,0:T(8,128)(2,1)} %bitcast.4), channel_id=1, source_target_pairs={{16,0},{24,8},{32,16},{40,24},{48,32},{56,40},{64,48},{72,56},{80,... | collective-permute-start | bytes 55304 | tf_op jit(solution)/shard_map/ppermute | solution.py:33
  8.5 9.3 %collective-permute-start.3 = (bf16[3,16,576]{2,1,0:T(8,128)(2,1)S(1)}, bf16[3,16,576]{2,1,0:T(8,128)(2,1)S(1)}, u32[]{:S(2)}, u32[]{:S(2)}) collective-permute-start(bf16[3,16,576]{2,1,0:T(8,128)(2,1)S(1)} %pad_maximum_fusion), channel_id=1, source_target_pairs={{80,0},{88,8},{96,16},{104,24},{112,32},{120,40},{0,48},{8,56},{16... | collective-permute-start | bytes 165896 | tf_op jit(solution)/shard_map/ppermute | solution.py:33
  12.9 4.9 %collective-permute-start.2 = (bf16[3,16,576]{2,1,0:T(8,128)(2,1)S(1)}, bf16[3,16,576]{2,1,0:T(8,128)(2,1)S(1)}, u32[]{:S(2)}, u32[]{:S(2)}) collective-permute-start(bf16[3,16,576]{2,1,0:T(8,128)(2,1)S(1)} %pad_maximum_fusion), channel_id=1, source_target_pairs={{48,0},{56,8},{64,16},{72,24},{80,32},{88,40},{96,48},{104,56},{11... | collective-permute-start | bytes 165896 | tf_op jit(solution)/shard_map/ppermute | solution.py:33
  17.8 4.8 %collective-permute-start.4 = (bf16[8,16,576]{2,1,0:T(8,128)(2,1)S(1)}, bf16[8,16,576]{2,1,0:T(8,128)(2,1)S(1)}, u32[]{:S(2)}, u32[]{:S(2)}) collective-permute-start(bf16[8,16,576]{2,1,0:T(8,128)(2,1)S(1)} %get-tuple-element.13), channel_id=1, source_target_pairs={{1,0},{136,8},{17,16},{152,24},{33,32},{168,40},{49,48},{184,56},{... | collective-permute-start | bytes 442376 | tf_op jit(solution)/shard_map/ppermute | solution.py:33
  20.4 7.1 %collective-permute-start.5 = (bf16[8,16,576]{2,1,0:T(8,128)(2,1)S(1)}, bf16[8,16,576]{2,1,0:T(8,128)(2,1)S(1)}, u32[]{:S(2)}, u32[]{:S(2)}) collective-permute-start(bf16[8,16,576]{2,1,0:T(8,128)(2,1)S(1)} %get-tuple-element.13), channel_id=1, source_target_pairs={{3,0},{140,8},{19,16},{156,24},{35,32},{172,40},{51,48},{188,56},{... | collective-permute-start | bytes 442376 | tf_op jit(solution)/shard_map/ppermute | solution.py:33
  20.4 7.2 %collective-permute-start.6 = (bf16[8,16,576]{2,1,0:T(8,128)(2,1)S(1)}, bf16[8,16,576]{2,1,0:T(8,128)(2,1)S(1)}, u32[]{:S(2)}, u32[]{:S(2)}) collective-permute-start(bf16[8,16,576]{2,1,0:T(8,128)(2,1)S(1)} %get-tuple-element.13), channel_id=1, source_target_pairs={{2,0},{12,8},{18,16},{28,24},{34,32},{44,40},{50,48},{60,56},{66,6... | collective-permute-start | bytes 442376 | tf_op jit(solution)/shard_map/ppermute | solution.py:33
  27.5 36.1 %copy-start.4 = (s32[64]{0:T(128)S(1)}, s32[64]{0:T(128)}, u32[]{:S(2)}) copy-start(s32[64]{0:T(128)} %starts_ref.1) | copy-start | bytes 772
  27.6 24.0 %collective-permute-start.9 = (bf16[32,16,576]{2,1,0:T(8,128)(2,1)S(1)}, bf16[32,16,576]{2,1,0:T(8,128)(2,1)S(1)}, u32[]{:S(2)}, u32[]{:S(2)}) collective-permute-start(bf16[32,16,576]{2,1,0:T(8,128)(2,1)S(1)} %constant_dynamic-update-slice_fusion.4.refs_0_), channel_id=1, source_target_pairs={{4,0},{10,8},{20,16},{26,24},{36,32},{42,40},{52,48},{58,56},{68,6... | collective-permute-start | bytes 1769480 | tf_op jit(solution)/shard_map/ppermute | solution.py:33
  30.6 21.0 %collective-permute-start.8 = (bf16[32,16,576]{2,1,0:T(8,128)(2,1)S(1)}, bf16[32,16,576]{2,1,0:T(8,128)(2,1)S(1)}, u32[]{:S(2)}, u32[]{:S(2)}) collective-permute-start(bf16[32,16,576]{2,1,0:T(8,128)(2,1)S(1)} %constant_dynamic-update-slice_fusion.4.refs_0_), channel_id=1, source_target_pairs={{132,0},{11,8},{148,16},{27,24},{164,32},{43,40},{180,48},{59,56},... | collective-permute-start | bytes 1769480 | tf_op jit(solution)/shard_map/ppermute | solution.py:33
  31.1 20.5 %collective-permute-start.7 = (bf16[32,16,576]{2,1,0:T(8,128)(2,1)S(1)}, bf16[32,16,576]{2,1,0:T(8,128)(2,1)S(1)}, u32[]{:S(2)}, u32[]{:S(2)}) collective-permute-start(bf16[32,16,576]{2,1,0:T(8,128)(2,1)S(1)} %constant_dynamic-update-slice_fusion.4.refs_0_), channel_id=1, source_target_pairs={{128,0},{9,8},{144,16},{25,24},{160,32},{41,40},{176,48},{57,56},{... | collective-permute-start | bytes 1769480 | tf_op jit(solution)/shard_map/ppermute | solution.py:33
  33.3 1.6 %copy-start = (bf16[16,128,512]{2,1,0:T(8,128)(2,1)S(1)}, bf16[16,128,512]{2,1,0:T(8,128)(2,1)}, u32[]{:S(2)}) copy-start(bf16[16,128,512]{2,1,0:T(8,128)(2,1)} %uk_ref.1) | copy-start | bytes 6291460
  34.9 1.0 %copy-start.1 = (bf16[128,2048]{1,0:T(8,128)(2,1)S(1)}, bf16[128,2048]{1,0:T(8,128)(2,1)}, u32[]{:S(2)}) copy-start(bf16[128,2048]{1,0:T(8,128)(2,1)} %nope_ref.1) | copy-start | bytes 1572868
  35.9 0.9 %copy-start.2 = (bf16[128,1024]{1,0:T(8,128)(2,1)S(1)}, bf16[128,1024]{1,0:T(8,128)(2,1)}, u32[]{:S(2)}) copy-start(bf16[128,1024]{1,0:T(8,128)(2,1)} %rope_ref.1) | copy-start | bytes 786436
  36.9 26.8 %copy-start.3 = (bf16[16,512,128]{2,1,0:T(8,128)(2,1)S(1)}, bf16[16,512,128]{2,1,0:T(8,128)(2,1)}, u32[]{:S(2)}) copy-start(bf16[16,512,128]{2,1,0:T(8,128)(2,1)} %refs_8_.1) | copy-start | bytes 6291460
  37.6 23.0 %collective-permute-start.10 = (bf16[32,16,576]{2,1,0:T(8,128)(2,1)S(1)}, bf16[32,16,576]{2,1,0:T(8,128)(2,1)S(1)}, u32[]{:S(2)}, u32[]{:S(2)}) collective-permute-start(bf16[32,16,576]{2,1,0:T(8,128)(2,1)S(1)} %constant_dynamic-update-slice_fusion.4.refs_0_), channel_id=1, source_target_pairs={{0,8},{8,0},{16,24},{24,16},{32,40},{40,32},{48,56},{56,48},{64,72... | collective-permute-start | bytes 1769480 | tf_op jit(solution)/shard_map/ppermute | solution.py:37
  51.6 10.2 %collective-permute-start.11 = (bf16[32,16,576]{2,1,0:T(8,128)(2,1)S(1)}, bf16[32,16,576]{2,1,0:T(8,128)(2,1)S(1)}, u32[]{:S(2)}, u32[]{:S(2)}) collective-permute-start(bf16[32,16,576]{2,1,0:T(8,128)(2,1)S(1)} %collective-permute-done.7.refs_1_), channel_id=1, source_target_pairs={{0,8},{8,0},{16,24},{24,16},{32,40},{40,32},{48,56},{56,48},{64,72... | collective-permute-start | bytes 1769480 | tf_op jit(solution)/shard_map/ppermute | solution.py:37
  60.1 2.7 %collective-permute-start.12 = (bf16[32,16,576]{2,1,0:T(8,128)(2,1)S(1)}, bf16[32,16,576]{2,1,0:T(8,128)(2,1)S(1)}, u32[]{:S(2)}, u32[]{:S(2)}) collective-permute-start(bf16[32,16,576]{2,1,0:T(8,128)(2,1)S(1)} %collective-permute-done.8.refs_2_), channel_id=1, source_target_pairs={{0,8},{8,0},{16,24},{24,16},{32,40},{40,32},{48,56},{56,48},{64,72... | collective-permute-start | bytes 1769480 | tf_op jit(solution)/shard_map/ppermute | solution.py:37
  60.1 3.6 %collective-permute-start.13 = (bf16[32,16,576]{2,1,0:T(8,128)(2,1)S(1)}, bf16[32,16,576]{2,1,0:T(8,128)(2,1)S(1)}, u32[]{:S(2)}, u32[]{:S(2)}) collective-permute-start(bf16[32,16,576]{2,1,0:T(8,128)(2,1)S(1)} %collective-permute-done.9.refs_3_), channel_id=1, source_target_pairs={{0,8},{8,0},{16,24},{24,16},{32,40},{40,32},{48,56},{56,48},{64,72... | collective-permute-start | bytes 1769480 | tf_op jit(solution)/shard_map/ppermute | solution.py:37

commit v5 on v3

v5 whole, which is shorter than its diff:
```python
import functools
import math

import jax
import jax.numpy as jnp
from jax import lax
from jax.experimental import pallas as pl
from jax.experimental.pallas import tpu as pltpu
from jax.sharding import PartitionSpec as P

BOTH = ("ctx", "head")
PIECE = 16
TILE = 256
NOPE = 128
GROUPS = ((0,), (1, 2), (3,))
OFFSETS = (0, 1, 3, 2)
WINDOW = (0, 1, 7, 3, 4, 2, 5, 6)


def device_index(x, y, z, core):
    return (((x % 2) * 8 + z) * 2 + core) * 8 + (x // 2) * 4 + y


def from_offset(value, first, second):
    pairs = []
    for x in range(4):
        for y in range(4):
            for z in range(8):
                for core in range(2):
                    dx, dy, dz = second if core else first
                    source = device_index((x + dx) % 4, (y + dy) % 4, (z + dz) % 8, core)
                    pairs.append((source, device_index(x, y, z, core)))
    return lax.ppermute(value, BOTH, pairs)


def other_core(value):
    return lax.ppermute(value, "ctx", [(i, i ^ 1) for i in range(32)])


def gather_own_core(latent, query):
    latent = latent[None]
    up = from_offset(latent, (0, 0, 1), (0, 0, 1))
    down = from_offset(latent, (0, 0, 7), (0, 0, 7))
    window = jnp.concatenate([latent, up, down])
    far_up = from_offset(window, (0, 0, 3), (0, 0, 3))
    far_down = from_offset(window, (0, 0, 5), (0, 0, 5))[:2]
    column = jnp.concatenate([window, far_up, far_down])
    column, query = lax.optimization_barrier((column, query))
    plane = jnp.concatenate(
        [column] + [from_offset(column, (0, d, 0), (d, 0, 0)) for d in OFFSETS[1:]]
    )
    lines = [from_offset(plane, (d, 0, 0), (0, d, 0)) for d in OFFSETS[1:]]
    return [plane, *lines], query


def query_kernel(nope_ref, rope_ref, uk_ref, query_ref):
    latent_width = uk_ref.shape[2]
    nope_width = uk_ref.shape[1]
    rope_width = rope_ref.shape[1] // uk_ref.shape[0]
    block = nope_ref.shape[0] // 2
    for head in range(uk_ref.shape[0]):
        lat = jnp.dot(
            nope_ref[:, head * nope_width : (head + 1) * nope_width],
            uk_ref[head],
            preferred_element_type=jnp.float32,
        ).astype(jnp.bfloat16)
        rope = rope_ref[:, head * rope_width : (head + 1) * rope_width]
        for half in range(2):
            rows = slice(half * block, (half + 1) * block)
            to = slice(head * block, (head + 1) * block)
            query_ref[half, to, :latent_width] = lat[rows]
            query_ref[half, to, latent_width:] = rope[rows]


def make_queries(q_nope, q_rope, w_uk):
    rows = q_nope.shape[0]
    heads, nope_width, latent_width = w_uk.shape
    rope_width = q_rope.shape[1] // heads
    width = latent_width + rope_width
    vmem = pl.BlockSpec(memory_space=pltpu.VMEM)
    return pl.pallas_call(
        query_kernel,
        in_specs=[vmem] * 3,
        out_specs=vmem,
        out_shape=jax.ShapeDtypeStruct((2, heads * rows // 2, width), jnp.bfloat16),
        compiler_params=pltpu.CompilerParams(vmem_limit_bytes=12 * 2**20),
        cost_estimate=pl.CostEstimate(
            flops=2 * rows * heads * nope_width * latent_width,
            bytes_accessed=6 * 2**20,
            transcendentals=0,
        ),
        name="make_queries",
    )(q_nope, q_rope, w_uk)


def absorb_kernel(lasts, finish, starts_ref, query_ref, *refs):
    piece_refs, refs = refs[: 2 * len(lasts)], refs[2 * len(lasts) :]
    state_in = refs[: 0 if lasts[0] == 0 else 3]
    refs = refs[len(state_in) :]
    if finish:
        uv_ref, out_ref, keys, marks, even, odd, acc, top, total = refs
    else:
        acc, top, total, keys, marks, even, odd = refs
    ctx, head_group = lax.axis_index("ctx"), lax.axis_index("head")
    x = (head_group // 4) * 2 + ctx // 16
    y, z, core = head_group % 4, (ctx // 2) % 8, ctx % 2
    rows = query_ref.shape[1]
    block, width = 4 * PIECE, query_ref.shape[2]
    latent_width = acc.shape[1]
    factor = math.log2(math.e) / math.sqrt(NOPE + width - latent_width)
    low, high = starts_ref[2 * ctx], starts_ref[2 * ctx + 1]

    if state_in:
        for to_ref, from_ref in zip((acc, top, total), state_in):
            to_ref[...] = from_ref[...]
    else:
        top[...] = jnp.full(top.shape, -1e30, jnp.float32)
        total[...] = jnp.zeros(total.shape, jnp.float32)
        acc[...] = jnp.zeros(acc.shape, jnp.float32)

    pieces = []
    for index, ref in enumerate(piece_refs):
        last, owner = lasts[index // 2], core if index % 2 == 0 else 1 - core
        for middle in range(4):
            px = (x + jnp.where(owner == 0, OFFSETS[last], OFFSETS[middle])) % 4
            py = (y + jnp.where(owner == 0, OFFSETS[middle], OFFSETS[last])) % 4
            for first in range(8):
                pz = (z + WINDOW[first]) % 8
                start = starts_ref[2 * (((px % 2) * 8 + pz) * 2 + owner) + px // 2]
                pieces.append((ref, middle * 8 + first, start, py * PIECE))
    below = jnp.int32(0)
    within = jnp.int32(0)
    for _, _, start, _ in pieces:
        below = below + jnp.where(start <= low, 1, 0)
        within = within + jnp.where(start <= high, 1, 0)
    lane = lax.broadcasted_iota(jnp.int32, (PIECE, 128), 1)
    row = lax.broadcasted_iota(jnp.int32, (PIECE, 128), 0)
    unit, offset = jnp.where(lane == 0, 1, 0), jnp.where(lane == 1, row, 0)
    beside = jnp.where(lane == 1, 1, 0)
    nexts = [jnp.int32(0), below, within]
    for ref, at, start, shift in pieces:
        first, second = start <= low, start <= high
        to = jnp.where(first, nexts[0], jnp.where(second, nexts[1], nexts[2]))
        nexts[0] = nexts[0] + jnp.where(first, 1, 0)
        nexts[1] = nexts[1] + jnp.where(second & (start > low), 1, 0)
        nexts[2] = nexts[2] + jnp.where(second, 0, 1)
        to = pl.ds(pl.multiple_of(to * PIECE, PIECE), PIECE)
        keys[to, :] = ref[at]
        mark = unit * (start // block) + offset + beside * shift
        marks[to, :] = mark.astype(jnp.float32).astype(jnp.bfloat16)

    read = jnp.where(lane == 0, float(block), jnp.where(lane == 1, 1.0, 0.0)).astype(jnp.bfloat16)
    query_row = lax.broadcasted_iota(jnp.int32, (block, TILE), 0).astype(jnp.float32)
    per_tile = TILE // PIECE
    tiles_low = (below + per_tile - 1) // per_tile
    tiles = tiles_low + (within + per_tile - 1) // per_tile

    def place(index):
        is_high = index >= tiles_low
        half = jnp.where(is_high, 1, 0)
        at = jnp.minimum((index - half * tiles_low) * TILE, keys.shape[0] - TILE)
        start = jnp.where(index >= tiles, -block, jnp.where(is_high, high, low))
        return half, pl.multiple_of(at, TILE), start

    def score(buffer, index):
        half, at, start = place(index)
        position = lax.dot_general(
            read,
            marks[pl.ds(at, TILE), :],
            (((1,), (1,)), ((), ())),
            preferred_element_type=jnp.float32,
        )
        position = jnp.broadcast_to(position[:1, :], (block, TILE))
        allowed = position - start.astype(jnp.float32) <= query_row
        s = lax.dot_general(
            query_ref[half],
            keys[pl.ds(at, TILE), :],
            (((1,), (1,)), ((), ())),
            preferred_element_type=jnp.float32,
        )
        s = jnp.where(allowed[None], s.reshape(rows // block, block, TILE), -1e30)
        buffer[...] = s.reshape(rows, TILE)

    def absorb_tile(buffer, index):
        half, at, _ = place(index)
        own = pl.ds(pl.multiple_of(half * rows, rows), rows)
        left, right = buffer[:, :128], buffer[:, 128:]
        old = top[own, :]
        new = jnp.maximum(old, jnp.max(jnp.maximum(left, right), axis=1, keepdims=True))
        scale = jnp.exp2((old - new) * factor)
        left = jnp.exp2((left - new) * factor)
        right = jnp.exp2((right - new) * factor)
        top[own, :] = new
        total[own, :] = total[own, :] * scale + (left + right)
        weights = jnp.concatenate([left, right], axis=1).astype(jnp.bfloat16)
        scales = jnp.concatenate([scale] * (latent_width // 128), axis=1)
        acc[own, :] = acc[own, :] * scales + jnp.dot(
            weights, keys[pl.ds(at, TILE), :latent_width], preferred_element_type=jnp.float32
        )

    score(even, 0)

    @pl.loop(0, (tiles + 1) // 2)
    def _(step):
        score(odd, 2 * step + 1)
        absorb_tile(even, 2 * step)
        score(even, 2 * step + 2)
        absorb_tile(odd, 2 * step + 1)

    if finish:
        value_width = uv_ref.shape[2]
        for h in range(uv_ref.shape[0]):
            lat = []
            for half in range(2):
                own = slice(half * rows + h * block, half * rows + (h + 1) * block)
                whole = jnp.sum(total[own, :], axis=1, keepdims=True)
                lat.append((acc[own, :] / whole).astype(jnp.bfloat16))
            out_ref[:, h * value_width : (h + 1) * value_width] = jnp.dot(
                jnp.concatenate(lat), uv_ref[h], preferred_element_type=jnp.float32
            ).astype(jnp.bfloat16)


def absorb(lasts, finish, block_start, query, pieces, state, w_uv):
    heads, latent_width, value_width = w_uv.shape
    rows, width = query.shape[1:]
    count = sum(p.shape[0] * p.shape[1] for p in pieces)
    vmem = pl.BlockSpec(memory_space=pltpu.VMEM)
    state_shapes = [(2 * rows, latent_width), (2 * rows, 128), (2 * rows, 128)]
    scratch = [
        pltpu.VMEM((count, width), jnp.bfloat16),
        pltpu.VMEM((count, 128), jnp.bfloat16),
        pltpu.VMEM((rows, TILE), jnp.float32),
        pltpu.VMEM((rows, TILE), jnp.float32),
    ]
    operands = [block_start, query, *pieces, *state]
    if finish:
        operands.append(w_uv)
        scratch += [pltpu.VMEM(shape, jnp.float32) for shape in state_shapes]
        out_shape = jax.ShapeDtypeStruct((2 * rows // heads, heads * value_width), jnp.bfloat16)
    else:
        out_shape = [jax.ShapeDtypeStruct(shape, jnp.float32) for shape in state_shapes]
    return pl.pallas_call(
        functools.partial(absorb_kernel, lasts, finish),
        in_specs=[pl.BlockSpec(memory_space=pltpu.SMEM)] + [vmem] * (len(operands) - 1),
        out_specs=vmem if finish else [vmem] * 3,
        out_shape=out_shape,
        scratch_shapes=scratch,
        compiler_params=pltpu.CompilerParams(vmem_limit_bytes=24 * 2**20),
        cost_estimate=pl.CostEstimate(
            flops=2 * rows * count * (width + latent_width),
            bytes_accessed=10 * 2**20,
            transcendentals=rows * count,
        ),
        name=f"absorb_{lasts[0]}",
    )(*operands)


def shards(q_nope, q_rope, latent, block_start, w_uk, w_uv):
    query = make_queries(q_nope, q_rope, w_uk)
    own, query = gather_own_core(latent, query)
    state = ()
    for lasts in GROUPS:
        chunks = [own[last] for last in lasts]
        if state:
            *chunks, state = lax.optimization_barrier((*chunks, state))
        pieces = [piece for chunk in chunks for piece in (chunk, other_core(chunk))]
        finish = lasts[-1] == len(own) - 1
        state = absorb(lasts, finish, block_start, query, pieces, state, w_uv)
    return state


def solution(mesh):
    placed = (P("ctx", "head"), P("ctx", "head"), P(BOTH, None), P(), P("head"), P("head"))
    return jax.shard_map(
        shards, mesh=mesh, in_specs=placed, out_specs=P("ctx", "head"), check_vma=False
    )
```

time: 92 us -> 75 us (0.82)
  the two profiles are of different devices: /device:TPU:4 before, /device:TPU:38 now
where the time goes in v5:
time: 75 us; the launch traced here: 75.5 us
  Pallas kernels  31 us (41%)
  waiting for transfers between devices  21.7 us (29%)
  starting transfers between devices  18.2 us (24%)
  local copies, waits for them, and re-layouts  4.48 us (6%)
    pallas_call x3, Pallas kernels, absorb(): pl.pallas_call(functools.partial(absorb_kernel, lasts, finish), in_specs=...  30.2 us
    ppermute x10, waiting for transfers between devices, from_offset(): return lax.ppermute(value, BOTH, pairs)  18.7 us
    ppermute x10, starting transfers between devices, from_offset(): return lax.ppermute(value, BOTH, pairs)  17.4 us
    unnamed x19, local copies, waits for them, and re-layouts  4.44 us
    ppermute x4, waiting for transfers between devices, other_core(): return lax.ppermute(value, 'ctx', [(i, i ^ 1) for i in range(32)])  3.01 us
  transfers between devices with their start and end apart: 14, of which 8 were waited for; matrix products, arithmetic and copies ran while one was open for 1% of the time, Pallas kernels for 26%

profile of v5, /device:TPU:38, one launch (start us, length us, event | category | flops | bytes accessed | tf_op | source)
XLA Modules:
  0.0 75.5 jit_solution(8216815252249356265)
XLA Ops:
  0.0 1.9 %collective-permute-start.1 = (bf16[1,16,576]{2,1,0:T(8,128)(2,1)}, bf16[1,16,576]{2,1,0:T(8,128)(2,1)S(1)}, u32[]{:S(2)}, u32[]{:S(2)}) collective-permute-start(bf16[1,16,576]{2,1,0:T(8,128)(2,1)} %bitcast.2), channel_id=1, source_target_pairs={{112,0},{120,8},{0,16},{8,24},{16,32},{24,40},{32,48},{40,56},{48,... | collective-permute-start | bytes 55304 | tf_op jit(solution)/shard_map/ppermute | solution.py:33
  1.9 0.1 collective-permute-start
  2.0 0.8 %constant_dynamic-update-slice_fusion.3 = bf16[8,16,576]{2,1,0:T(8,128)(2,1)S(1)} fusion(bf16[16,576]{1,0:T(8,128)(2,1)} %param.8), kind=kLoop, calls=%fused_computation.5 | loop fusion | bytes 38912
  2.8 1.6 %copy-done.1 = bf16[16,128,512]{2,1,0:T(8,128)(2,1)S(1)} copy-done((bf16[16,128,512]{2,1,0:T(8,128)(2,1)S(1)}, bf16[16,128,512]{2,1,0:T(8,128)(2,1)}, u32[]{:S(2)}) %copy-start.1) | copy-done | bytes 2097176
  4.4 1.0 %copy-done.2 = bf16[128,2048]{1,0:T(8,128)(2,1)S(1)} copy-done((bf16[128,2048]{1,0:T(8,128)(2,1)S(1)}, bf16[128,2048]{1,0:T(8,128)(2,1)}, u32[]{:S(2)}) %copy-start.2) | copy-done | bytes 524312
  5.4 0.9 %copy-done.3 = bf16[128,1024]{1,0:T(8,128)(2,1)S(1)} copy-done((bf16[128,1024]{1,0:T(8,128)(2,1)S(1)}, bf16[128,1024]{1,0:T(8,128)(2,1)}, u32[]{:S(2)}) %copy-start.3) | copy-done | bytes 262168
  6.4 0.8 %make_queries.1.query_ref = bf16[2,1024,576]{2,1,0:T(8,128)(2,1)S(1)} custom-call(bf16[128,2048]{1,0:T(8,128)(2,1)S(1)} %copy-done.2, bf16[128,1024]{1,0:T(8,128)(2,1)S(1)} %copy-done.3, bf16[16,128,512]{2,1,0:T(8,128)(2,1)S(1)} %copy-done.1), custom_call_target="tpu_custom_call" | custom-call | flops 268435456 | bytes 6291456 | tf_op jit(solution)/shard_map/make_queries/pallas_call | solution.py:81
  7.2 7.1 %collective-permute-start.3 = (bf16[3,16,576]{2,1,0:T(8,128)(2,1)S(1)}, bf16[3,16,576]{2,1,0:T(8,128)(2,1)S(1)}, u32[]{:S(2)}, u32[]{:S(2)}) collective-permute-start(bf16[3,16,576]{2,1,0:T(8,128)(2,1)S(1)} %pad_maximum_fusion), channel_id=1, source_target_pairs={{80,0},{88,8},{96,16},{104,24},{112,32},{120,40},{0,48},{8,56},{16... | collective-permute-start | bytes 165896 | tf_op jit(solution)/shard_map/ppermute | solution.py:33
  14.3 7.8 %collective-permute-done.2 = bf16[3,16,576]{2,1,0:T(8,128)(2,1)S(1)} collective-permute-done((bf16[3,16,576]{2,1,0:T(8,128)(2,1)S(1)}, bf16[3,16,576]{2,1,0:T(8,128)(2,1)S(1)}, u32[]{:S(2)}, u32[]{:S(2)}) %collective-permute-start.2) | collective-permute-done | bytes 55328 | tf_op jit(solution)/shard_map/ppermute | solution.py:33
  22.2 0.0 collective-permute-done.3
  22.2 3.1 %collective-permute-start.4 = (bf16[8,16,576]{2,1,0:T(8,128)(2,1)S(1)}, bf16[8,16,576]{2,1,0:T(8,128)(2,1)S(1)}, u32[]{:S(2)}, u32[]{:S(2)}) collective-permute-start(bf16[8,16,576]{2,1,0:T(8,128)(2,1)S(1)} %slice_dynamic-update-slice_fusion), channel_id=1, source_target_pairs={{1,0},{136,8},{17,16},{152,24},{33,32},{168,40},{49,48},{184,56},{... | collective-permute-start | bytes 442376 | tf_op jit(solution)/shard_map/ppermute | solution.py:33
  25.3 0.6 collective-permute-start.6
  25.9 1.0 %collective-permute-start.5 = (bf16[8,16,576]{2,1,0:T(8,128)(2,1)S(1)}, bf16[8,16,576]{2,1,0:T(8,128)(2,1)S(1)}, u32[]{:S(2)}, u32[]{:S(2)}) collective-permute-start(bf16[8,16,576]{2,1,0:T(8,128)(2,1)S(1)} %slice_dynamic-update-slice_fusion), channel_id=1, source_target_pairs={{3,0},{140,8},{19,16},{156,24},{35,32},{172,40},{51,48},{188,56},{... | collective-permute-start | bytes 442376 | tf_op jit(solution)/shard_map/ppermute | solution.py:33
  26.9 3.0 %collective-permute-done.4 = bf16[8,16,576]{2,1,0:T(8,128)(2,1)S(1)} collective-permute-done((bf16[8,16,576]{2,1,0:T(8,128)(2,1)S(1)}, bf16[8,16,576]{2,1,0:T(8,128)(2,1)S(1)}, u32[]{:S(2)}, u32[]{:S(2)}) %collective-permute-start.4) | collective-permute-done | bytes 147488 | tf_op jit(solution)/shard_map/ppermute | solution.py:33
  29.9 3.9 %collective-permute-done.5 = bf16[8,16,576]{2,1,0:T(8,128)(2,1)S(1)} collective-permute-done((bf16[8,16,576]{2,1,0:T(8,128)(2,1)S(1)}, bf16[8,16,576]{2,1,0:T(8,128)(2,1)S(1)}, u32[]{:S(2)}, u32[]{:S(2)}) %collective-permute-start.5) | collective-permute-done | bytes 147488 | tf_op jit(solution)/shard_map/ppermute | solution.py:33
  33.9 0.0 collective-permute-done.6
  33.9 0.1 collective-permute-start.10
  34.0 0.6 collective-permute-start.9
  34.6 1.5 %collective-permute-start.8 = (bf16[32,16,576]{2,1,0:T(8,128)(2,1)S(1)}, bf16[32,16,576]{2,1,0:T(8,128)(2,1)S(1)}, u32[]{:S(2)}, u32[]{:S(2)}) collective-permute-start(bf16[32,16,576]{2,1,0:T(8,128)(2,1)S(1)} %constant_dynamic-update-slice_fusion.4.refs_0_), channel_id=1, source_target_pairs={{128,0},{9,8},{144,16},{25,24},{160,32},{41,40},{176,48},{57,56},{... | collective-permute-start | bytes 1769480 | tf_op jit(solution)/shard_map/ppermute | solution.py:33
  36.1 0.0 collective-permute-done.10.refs_1_
  36.2 6.3 %absorb_0.1 = (f32[2048,512]{1,0:T(8,128)S(1)}, f32[2048,128]{1,0:T(8,128)S(1)}, f32[2048,128]{1,0:T(8,128)S(1)}) custom-call(s32[64]{0:T(128)S(1)} %copy-done.4, bf16[2,1024,576]{2,1,0:T(8,128)(2,1)S(1)} %make_queries.1.query_ref, bf16[32,16,576]{2,1,0:T(8,128)(2,1)S(1)} %constant_dynamic-update-slice_fusion.4.refs_0_, ...), custom_call_target="tpu_custom_call" | custom-call | flops 2281701376 | bytes 10485760 | tf_op jit(solution)/shard_map/absorb_0/pallas_call | solution.py:242
  42.5 2.2 %collective-permute-done.9.refs_2_ = bf16[32,16,576]{2,1,0:T(8,128)(2,1)S(1)} collective-permute-done((bf16[32,16,576]{2,1,0:T(8,128)(2,1)S(1)}, bf16[32,16,576]{2,1,0:T(8,128)(2,1)S(1)}, u32[]{:S(2)}, u32[]{:S(2)}) %collective-permute-start.9) | collective-permute-done | bytes 589856 | tf_op jit(solution)/shard_map/ppermute | solution.py:33
  44.7 1.7 %collective-permute-done.8.refs_0_ = bf16[32,16,576]{2,1,0:T(8,128)(2,1)S(1)} collective-permute-done((bf16[32,16,576]{2,1,0:T(8,128)(2,1)S(1)}, bf16[32,16,576]{2,1,0:T(8,128)(2,1)S(1)}, u32[]{:S(2)}, u32[]{:S(2)}) %collective-permute-start.8) | collective-permute-done | bytes 589856 | tf_op jit(solution)/shard_map/ppermute | solution.py:33
  46.4 0.0 collective-permute-start.11
  46.4 0.5 collective-permute-start.12
  46.9 1.5 %collective-permute-start.7 = (bf16[32,16,576]{2,1,0:T(8,128)(2,1)S(1)}, bf16[32,16,576]{2,1,0:T(8,128)(2,1)S(1)}, u32[]{:S(2)}, u32[]{:S(2)}) collective-permute-start(bf16[32,16,576]{2,1,0:T(8,128)(2,1)S(1)} %constant_dynamic-update-slice_fusion.4.refs_0_), channel_id=1, source_target_pairs={{4,0},{10,8},{20,16},{26,24},{36,32},{42,40},{52,48},{58,56},{68,6... | collective-permute-start | bytes 1769480 | tf_op jit(solution)/shard_map/ppermute | solution.py:33
  48.4 0.1 collective-permute-done.11.refs_1_
  48.5 0.9 %collective-permute-done.12.refs_3_ = bf16[32,16,576]{2,1,0:T(8,128)(2,1)S(1)} collective-permute-done((bf16[32,16,576]{2,1,0:T(8,128)(2,1)S(1)}, bf16[32,16,576]{2,1,0:T(8,128)(2,1)S(1)}, u32[]{:S(2)}, u32[]{:S(2)}) %collective-permute-start.12) | collective-permute-done | bytes 589856 | tf_op jit(solution)/shard_map/ppermute | solution.py:37
  49.4 12.7 %absorb_1.1 = (f32[2048,512]{1,0:T(8,128)S(1)}, f32[2048,128]{1,0:T(8,128)S(1)}, f32[2048,128]{1,0:T(8,128)S(1)}) custom-call(s32[64]{0:T(128)S(1)} %copy-done.4, bf16[2,1024,576]{2,1,0:T(8,128)(2,1)S(1)} %make_queries.1.query_ref, bf16[32,16,576]{2,1,0:T(8,128)(2,1)S(1)} %collective-permute-done.8.refs_0_, ...), custom_call_target="tpu_custom_call" | custom-call | flops 4563402752 | bytes 10485760 | tf_op jit(solution)/shard_map/absorb_1/pallas_call | solution.py:242
  62.1 0.2 collective-permute-start.13
  62.3 2.0 %collective-permute-done.13.refs_1_ = bf16[32,16,576]{2,1,0:T(8,128)(2,1)S(1)} collective-permute-done((bf16[32,16,576]{2,1,0:T(8,128)(2,1)S(1)}, bf16[32,16,576]{2,1,0:T(8,128)(2,1)S(1)}, u32[]{:S(2)}, u32[]{:S(2)}) %collective-permute-start.13) | collective-permute-done | bytes 589856 | tf_op jit(solution)/shard_map/ppermute | solution.py:37
  64.3 11.2 %absorb_3.1 = bf16[128,2048]{1,0:T(8,128)(2,1)} custom-call(s32[64]{0:T(128)S(1)} %copy-done.4, bf16[2,1024,576]{2,1,0:T(8,128)(2,1)S(1)} %make_queries.1.query_ref, bf16[32,16,576]{2,1,0:T(8,128)(2,1)S(1)} %collective-permute-done.7.refs_0_, bf16[32,16,576]{2,1,0:T(8,128)(2,1)S(1)} %collective-permute-done.13.refs_1_, ...), custom_call_target="tpu_custom_call" | custom-call | flops 2281701376 | bytes 10485760 | tf_op jit(solution)/shard_map/absorb_3/pallas_call | solution.py:242
  (22 shorter events, 0.2 us)
Async XLA Ops:
  0.0 7.1 %collective-permute-start.1 = (bf16[1,16,576]{2,1,0:T(8,128)(2,1)}, bf16[1,16,576]{2,1,0:T(8,128)(2,1)S(1)}, u32[]{:S(2)}, u32[]{:S(2)}) collective-permute-start(bf16[1,16,576]{2,1,0:T(8,128)(2,1)} %bitcast.2), channel_id=1, source_target_pairs={{112,0},{120,8},{0,16},{8,24},{16,32},{24,40},{32,48},{40,56},{48,... | collective-permute-start | bytes 55304 | tf_op jit(solution)/shard_map/ppermute | solution.py:33
  1.9 5.2 %collective-permute-start = (bf16[1,16,576]{2,1,0:T(8,128)(2,1)}, bf16[1,16,576]{2,1,0:T(8,128)(2,1)S(1)}, u32[]{:S(2)}, u32[]{:S(2)}) collective-permute-start(bf16[1,16,576]{2,1,0:T(8,128)(2,1)} %bitcast.3), channel_id=1, source_target_pairs={{16,0},{24,8},{32,16},{40,24},{48,32},{56,40},{64,48},{72,56},{80,... | collective-permute-start | bytes 55304 | tf_op jit(solution)/shard_map/ppermute | solution.py:33
  2.8 1.6 %copy-start.1 = (bf16[16,128,512]{2,1,0:T(8,128)(2,1)S(1)}, bf16[16,128,512]{2,1,0:T(8,128)(2,1)}, u32[]{:S(2)}) copy-start(bf16[16,128,512]{2,1,0:T(8,128)(2,1)} %uk_ref.1) | copy-start | bytes 6291460
  4.4 1.0 %copy-start.2 = (bf16[128,2048]{1,0:T(8,128)(2,1)S(1)}, bf16[128,2048]{1,0:T(8,128)(2,1)}, u32[]{:S(2)}) copy-start(bf16[128,2048]{1,0:T(8,128)(2,1)} %nope_ref.1) | copy-start | bytes 1572868
  5.4 0.9 %copy-start.3 = (bf16[128,1024]{1,0:T(8,128)(2,1)S(1)}, bf16[128,1024]{1,0:T(8,128)(2,1)}, u32[]{:S(2)}) copy-start(bf16[128,1024]{1,0:T(8,128)(2,1)} %rope_ref.1) | copy-start | bytes 786436
  6.4 0.8 %copy-start.5 = (bf16[16,576]{1,0:T(8,128)(2,1)S(1)}, bf16[16,576]{1,0:T(8,128)(2,1)}, u32[]{:S(2)}) copy-start(bf16[16,576]{1,0:T(8,128)(2,1)} %param.8) | copy-start | bytes 55300
  6.4 29.8 %copy-start.4 = (s32[64]{0:T(128)S(1)}, s32[64]{0:T(128)}, u32[]{:S(2)}) copy-start(s32[64]{0:T(128)} %starts_ref.5) | copy-start | bytes 772
  7.2 15.0 %collective-permute-start.3 = (bf16[3,16,576]{2,1,0:T(8,128)(2,1)S(1)}, bf16[3,16,576]{2,1,0:T(8,128)(2,1)S(1)}, u32[]{:S(2)}, u32[]{:S(2)}) collective-permute-start(bf16[3,16,576]{2,1,0:T(8,128)(2,1)S(1)} %pad_maximum_fusion), channel_id=1, source_target_pairs={{80,0},{88,8},{96,16},{104,24},{112,32},{120,40},{0,48},{8,56},{16... | collective-permute-start | bytes 165896 | tf_op jit(solution)/shard_map/ppermute | solution.py:33
  14.3 7.8 %collective-permute-start.2 = (bf16[3,16,576]{2,1,0:T(8,128)(2,1)S(1)}, bf16[3,16,576]{2,1,0:T(8,128)(2,1)S(1)}, u32[]{:S(2)}, u32[]{:S(2)}) collective-permute-start(bf16[3,16,576]{2,1,0:T(8,128)(2,1)S(1)} %pad_maximum_fusion), channel_id=1, source_target_pairs={{48,0},{56,8},{64,16},{72,24},{80,32},{88,40},{96,48},{104,56},{11... | collective-permute-start | bytes 165896 | tf_op jit(solution)/shard_map/ppermute | solution.py:33
  22.2 7.7 %collective-permute-start.4 = (bf16[8,16,576]{2,1,0:T(8,128)(2,1)S(1)}, bf16[8,16,576]{2,1,0:T(8,128)(2,1)S(1)}, u32[]{:S(2)}, u32[]{:S(2)}) collective-permute-start(bf16[8,16,576]{2,1,0:T(8,128)(2,1)S(1)} %slice_dynamic-update-slice_fusion), channel_id=1, source_target_pairs={{1,0},{136,8},{17,16},{152,24},{33,32},{168,40},{49,48},{184,56},{... | collective-permute-start | bytes 442376 | tf_op jit(solution)/shard_map/ppermute | solution.py:33
  25.3 8.6 %collective-permute-start.6 = (bf16[8,16,576]{2,1,0:T(8,128)(2,1)S(1)}, bf16[8,16,576]{2,1,0:T(8,128)(2,1)S(1)}, u32[]{:S(2)}, u32[]{:S(2)}) collective-permute-start(bf16[8,16,576]{2,1,0:T(8,128)(2,1)S(1)} %slice_dynamic-update-slice_fusion), channel_id=1, source_target_pairs={{2,0},{12,8},{18,16},{28,24},{34,32},{44,40},{50,48},{60,56},{66,6... | collective-permute-start | bytes 442376 | tf_op jit(solution)/shard_map/ppermute | solution.py:33
  25.9 7.9 %collective-permute-start.5 = (bf16[8,16,576]{2,1,0:T(8,128)(2,1)S(1)}, bf16[8,16,576]{2,1,0:T(8,128)(2,1)S(1)}, u32[]{:S(2)}, u32[]{:S(2)}) collective-permute-start(bf16[8,16,576]{2,1,0:T(8,128)(2,1)S(1)} %slice_dynamic-update-slice_fusion), channel_id=1, source_target_pairs={{3,0},{140,8},{19,16},{156,24},{35,32},{172,40},{51,48},{188,56},{... | collective-permute-start | bytes 442376 | tf_op jit(solution)/shard_map/ppermute | solution.py:33
  33.9 2.2 %collective-permute-start.10 = (bf16[32,16,576]{2,1,0:T(8,128)(2,1)S(1)}, bf16[32,16,576]{2,1,0:T(8,128)(2,1)S(1)}, u32[]{:S(2)}, u32[]{:S(2)}) collective-permute-start(bf16[32,16,576]{2,1,0:T(8,128)(2,1)S(1)} %constant_dynamic-update-slice_fusion.4.refs_0_), channel_id=1, source_target_pairs={{0,8},{8,0},{16,24},{24,16},{32,40},{40,32},{48,56},{56,48},{64,72... | collective-permute-start | bytes 1769480 | tf_op jit(solution)/shard_map/ppermute | solution.py:37
  34.0 10.7 %collective-permute-start.9 = (bf16[32,16,576]{2,1,0:T(8,128)(2,1)S(1)}, bf16[32,16,576]{2,1,0:T(8,128)(2,1)S(1)}, u32[]{:S(2)}, u32[]{:S(2)}) collective-permute-start(bf16[32,16,576]{2,1,0:T(8,128)(2,1)S(1)} %constant_dynamic-update-slice_fusion.4.refs_0_), channel_id=1, source_target_pairs={{132,0},{11,8},{148,16},{27,24},{164,32},{43,40},{180,48},{59,56},... | collective-permute-start | bytes 1769480 | tf_op jit(solution)/shard_map/ppermute | solution.py:33
  34.6 11.8 %collective-permute-start.8 = (bf16[32,16,576]{2,1,0:T(8,128)(2,1)S(1)}, bf16[32,16,576]{2,1,0:T(8,128)(2,1)S(1)}, u32[]{:S(2)}, u32[]{:S(2)}) collective-permute-start(bf16[32,16,576]{2,1,0:T(8,128)(2,1)S(1)} %constant_dynamic-update-slice_fusion.4.refs_0_), channel_id=1, source_target_pairs={{128,0},{9,8},{144,16},{25,24},{160,32},{41,40},{176,48},{57,56},{... | collective-permute-start | bytes 1769480 | tf_op jit(solution)/shard_map/ppermute | solution.py:33
  46.4 17.9 %copy-start = (bf16[16,512,128]{2,1,0:T(8,128)(2,1)S(1)}, bf16[16,512,128]{2,1,0:T(8,128)(2,1)}, u32[]{:S(2)}) copy-start(bf16[16,512,128]{2,1,0:T(8,128)(2,1)} %refs_5_.1) | copy-start | bytes 6291460
  46.4 2.1 %collective-permute-start.11 = (bf16[32,16,576]{2,1,0:T(8,128)(2,1)S(1)}, bf16[32,16,576]{2,1,0:T(8,128)(2,1)S(1)}, u32[]{:S(2)}, u32[]{:S(2)}) collective-permute-start(bf16[32,16,576]{2,1,0:T(8,128)(2,1)S(1)} %collective-permute-done.8.refs_0_), channel_id=1, source_target_pairs={{0,8},{8,0},{16,24},{24,16},{32,40},{40,32},{48,56},{56,48},{64,72... | collective-permute-start | bytes 1769480 | tf_op jit(solution)/shard_map/ppermute | solution.py:37
  46.4 3.0 %collective-permute-start.12 = (bf16[32,16,576]{2,1,0:T(8,128)(2,1)S(1)}, bf16[32,16,576]{2,1,0:T(8,128)(2,1)S(1)}, u32[]{:S(2)}, u32[]{:S(2)}) collective-permute-start(bf16[32,16,576]{2,1,0:T(8,128)(2,1)S(1)} %collective-permute-done.9.refs_2_), channel_id=1, source_target_pairs={{0,8},{8,0},{16,24},{24,16},{32,40},{40,32},{48,56},{56,48},{64,72... | collective-permute-start | bytes 1769480 | tf_op jit(solution)/shard_map/ppermute | solution.py:37
  46.9 15.2 %collective-permute-start.7 = (bf16[32,16,576]{2,1,0:T(8,128)(2,1)S(1)}, bf16[32,16,576]{2,1,0:T(8,128)(2,1)S(1)}, u32[]{:S(2)}, u32[]{:S(2)}) collective-permute-start(bf16[32,16,576]{2,1,0:T(8,128)(2,1)S(1)} %constant_dynamic-update-slice_fusion.4.refs_0_), channel_id=1, source_target_pairs={{4,0},{10,8},{20,16},{26,24},{36,32},{42,40},{52,48},{58,56},{68,6... | collective-permute-start | bytes 1769480 | tf_op jit(solution)/shard_map/ppermute | solution.py:33
  62.1 2.2 %collective-permute-start.13 = (bf16[32,16,576]{2,1,0:T(8,128)(2,1)S(1)}, bf16[32,16,576]{2,1,0:T(8,128)(2,1)S(1)}, u32[]{:S(2)}, u32[]{:S(2)}) collective-permute-start(bf16[32,16,576]{2,1,0:T(8,128)(2,1)S(1)} %collective-permute-done.7.refs_0_), channel_id=1, source_target_pairs={{0,8},{8,0},{16,24},{24,16},{32,40},{40,32},{48,56},{56,48},{64,72... | collective-permute-start | bytes 1769480 | tf_op jit(solution)/shard_map/ppermute | solution.py:37

commit v6 on v5

--- a/solution.py
+++ b/solution.py
@@ -12,7 +12,7 @@
 PIECE = 16
 TILE = 256
 NOPE = 128
-GROUPS = ((0,), (1, 2), (3,))
+GROUPS = ((0,), (1, 2, 3))
 OFFSETS = (0, 1, 3, 2)
 WINDOW = (0, 1, 7, 3, 4, 2, 5, 6)
 
@@ -102,8 +102,8 @@
     else:
         acc, top, total, keys, marks, even, odd = refs
     ctx, head_group = lax.axis_index("ctx"), lax.axis_index("head")
-    x = (head_group // 4) * 2 + ctx // 16
-    y, z, core = head_group % 4, (ctx // 2) % 8, ctx % 2
+    x = (head_group >> 2) * 2 + (ctx >> 4)
+    y, z, core = head_group & 3, (ctx >> 1) & 7, ctx & 1
     rows = query_ref.shape[1]
     block, width = 4 * PIECE, query_ref.shape[2]
     latent_width = acc.shape[1]
@@ -122,11 +122,11 @@
     for index, ref in enumerate(piece_refs):
         last, owner = lasts[index // 2], core if index % 2 == 0 else 1 - core
         for middle in range(4):
-            px = (x + jnp.where(owner == 0, OFFSETS[last], OFFSETS[middle])) % 4
-            py = (y + jnp.where(owner == 0, OFFSETS[middle], OFFSETS[last])) % 4
+            px = (x + jnp.where(owner == 0, OFFSETS[last], OFFSETS[middle])) & 3
+            py = (y + jnp.where(owner == 0, OFFSETS[middle], OFFSETS[last])) & 3
             for first in range(8):
-                pz = (z + WINDOW[first]) % 8
-                start = starts_ref[2 * (((px % 2) * 8 + pz) * 2 + owner) + px // 2]
+                pz = (z + WINDOW[first]) & 7
+                start = starts_ref[((px & 1) << 5) + (pz << 2) + (owner << 1) + (px >> 1)]
                 pieces.append((ref, middle * 8 + first, start, py * PIECE))
     below = jnp.int32(0)
     within = jnp.int32(0)
@@ -146,14 +146,14 @@
         nexts[2] = nexts[2] + jnp.where(second, 0, 1)
         to = pl.ds(pl.multiple_of(to * PIECE, PIECE), PIECE)
         keys[to, :] = ref[at]
-        mark = unit * (start // block) + offset + beside * shift
+        mark = unit * (start >> 6) + offset + beside * shift
         marks[to, :] = mark.astype(jnp.float32).astype(jnp.bfloat16)
 
     read = jnp.where(lane == 0, float(block), jnp.where(lane == 1, 1.0, 0.0)).astype(jnp.bfloat16)
     query_row = lax.broadcasted_iota(jnp.int32, (block, TILE), 0).astype(jnp.float32)
     per_tile = TILE // PIECE
-    tiles_low = (below + per_tile - 1) // per_tile
-    tiles = tiles_low + (within + per_tile - 1) // per_tile
+    tiles_low = (below + per_tile - 1) >> 4
+    tiles = tiles_low + ((within + per_tile - 1) >> 4)
 
     def place(index):
         is_high = index >= tiles_low
@@ -200,7 +200,7 @@
 
     score(even, 0)
 
-    @pl.loop(0, (tiles + 1) // 2)
+    @pl.loop(0, (tiles + 1) >> 1)
     def _(step):
         score(odd, 2 * step + 1)
         absorb_tile(even, 2 * step)
@@ -261,8 +261,8 @@
     state = ()
     for lasts in GROUPS:
         chunks = [own[last] for last in lasts]
-        if state:
-            *chunks, state = lax.optimization_barrier((*chunks, state))
+        for i in range(len(chunks) if state else 0):
+            chunks[i], state = lax.optimization_barrier((chunks[i], state))
         pieces = [piece for chunk in chunks for piece in (chunk, other_core(chunk))]
         finish = lasts[-1] == len(own) - 1
         state = absorb(lasts, finish, block_start, query, pieces, state, w_uv)

time: 75 us -> 77.7 us (1.036)
  the two profiles are of different devices: /device:TPU:38 before, /device:TPU:32 now
where the time goes in v6:
time: 77.7 us; the launch traced here: 77.5 us
  waiting for transfers between devices  26.8 us (34%)
  Pallas kernels  26.4 us (34%)
  starting transfers between devices  19.6 us (25%)
  local copies, waits for them, and re-layouts  4.48 us (6%)
    pallas_call x2, Pallas kernels, absorb(): pl.pallas_call(functools.partial(absorb_kernel, lasts, finish), in_specs=...  25.7 us
    ppermute x10, waiting for transfers between devices, from_offset(): return lax.ppermute(value, BOTH, pairs)  23.4 us
    ppermute x10, starting transfers between devices, from_offset(): return lax.ppermute(value, BOTH, pairs)  19 us
    unnamed x19, local copies, waits for them, and re-layouts  4.45 us
    ppermute x4, waiting for transfers between devices, other_core(): return lax.ppermute(value, 'ctx', [(i, i ^ 1) for i in range(32)])  3.46 us
  transfers between devices with their start and end apart: 14, of which 8 were waited for; matrix products, arithmetic and copies ran while one was open for 1% of the time, Pallas kernels for 11%

profile of v6, /device:TPU:32, one launch (start us, length us, event | category | flops | bytes accessed | tf_op | source)
XLA Modules:
  0.0 77.5 jit_solution(3091064782937014655)
XLA Ops:
  0.0 1.9 %collective-permute-start.1 = (bf16[1,16,576]{2,1,0:T(8,128)(2,1)}, bf16[1,16,576]{2,1,0:T(8,128)(2,1)S(1)}, u32[]{:S(2)}, u32[]{:S(2)}) collective-permute-start(bf16[1,16,576]{2,1,0:T(8,128)(2,1)} %bitcast.2), channel_id=1, source_target_pairs={{112,0},{120,8},{0,16},{8,24},{16,32},{24,40},{32,48},{40,56},{48,... | collective-permute-start | bytes 55304 | tf_op jit(solution)/shard_map/ppermute | solution.py:33
  1.9 0.1 collective-permute-start
  2.0 0.8 constant_dynamic-update-slice_fusion.3
  2.8 1.6 %copy-done = bf16[16,128,512]{2,1,0:T(8,128)(2,1)S(1)} copy-done((bf16[16,128,512]{2,1,0:T(8,128)(2,1)S(1)}, bf16[16,128,512]{2,1,0:T(8,128)(2,1)}, u32[]{:S(2)}) %copy-start) | copy-done | bytes 2097176
  4.4 1.0 %copy-done.1 = bf16[128,2048]{1,0:T(8,128)(2,1)S(1)} copy-done((bf16[128,2048]{1,0:T(8,128)(2,1)S(1)}, bf16[128,2048]{1,0:T(8,128)(2,1)}, u32[]{:S(2)}) %copy-start.1) | copy-done | bytes 524312
  5.4 0.9 %copy-done.2 = bf16[128,1024]{1,0:T(8,128)(2,1)S(1)} copy-done((bf16[128,1024]{1,0:T(8,128)(2,1)S(1)}, bf16[128,1024]{1,0:T(8,128)(2,1)}, u32[]{:S(2)}) %copy-start.2) | copy-done | bytes 262168
  6.4 0.8 make_queries.1.query_ref
  7.1 0.0 collective-permute-done.1
  7.2 0.0 collective-permute-done
  7.2 7.1 %collective-permute-start.3 = (bf16[3,16,576]{2,1,0:T(8,128)(2,1)S(1)}, bf16[3,16,576]{2,1,0:T(8,128)(2,1)S(1)}, u32[]{:S(2)}, u32[]{:S(2)}) collective-permute-start(bf16[3,16,576]{2,1,0:T(8,128)(2,1)S(1)} %pad_maximum_fusion), channel_id=1, source_target_pairs={{80,0},{88,8},{96,16},{104,24},{112,32},{120,40},{0,48},{8,56},{16... | collective-permute-start | bytes 165896 | tf_op jit(solution)/shard_map/ppermute | solution.py:33
  14.3 0.0 collective-permute-start.2
  14.3 7.8 %collective-permute-done.2 = bf16[3,16,576]{2,1,0:T(8,128)(2,1)S(1)} collective-permute-done((bf16[3,16,576]{2,1,0:T(8,128)(2,1)S(1)}, bf16[3,16,576]{2,1,0:T(8,128)(2,1)S(1)}, u32[]{:S(2)}, u32[]{:S(2)}) %collective-permute-start.2) | collective-permute-done | bytes 55328 | tf_op jit(solution)/shard_map/ppermute | solution.py:33
  22.2 0.0 collective-permute-done.3
  22.2 3.1 %collective-permute-start.4 = (bf16[8,16,576]{2,1,0:T(8,128)(2,1)S(1)}, bf16[8,16,576]{2,1,0:T(8,128)(2,1)S(1)}, u32[]{:S(2)}, u32[]{:S(2)}) collective-permute-start(bf16[8,16,576]{2,1,0:T(8,128)(2,1)S(1)} %slice_dynamic-update-slice_fusion), channel_id=1, source_target_pairs={{1,0},{136,8},{17,16},{152,24},{33,32},{168,40},{49,48},{184,56},{... | collective-permute-start | bytes 442376 | tf_op jit(solution)/shard_map/ppermute | solution.py:33
  25.3 0.6 collective-permute-start.6
  25.9 1.0 %collective-permute-start.5 = (bf16[8,16,576]{2,1,0:T(8,128)(2,1)S(1)}, bf16[8,16,576]{2,1,0:T(8,128)(2,1)S(1)}, u32[]{:S(2)}, u32[]{:S(2)}) collective-permute-start(bf16[8,16,576]{2,1,0:T(8,128)(2,1)S(1)} %slice_dynamic-update-slice_fusion), channel_id=1, source_target_pairs={{3,0},{140,8},{19,16},{156,24},{35,32},{172,40},{51,48},{188,56},{... | collective-permute-start | bytes 442376 | tf_op jit(solution)/shard_map/ppermute | solution.py:33
  26.9 3.0 %collective-permute-done.4 = bf16[8,16,576]{2,1,0:T(8,128)(2,1)S(1)} collective-permute-done((bf16[8,16,576]{2,1,0:T(8,128)(2,1)S(1)}, bf16[8,16,576]{2,1,0:T(8,128)(2,1)S(1)}, u32[]{:S(2)}, u32[]{:S(2)}) %collective-permute-start.4) | collective-permute-done | bytes 147488 | tf_op jit(solution)/shard_map/ppermute | solution.py:33
  30.0 3.9 %collective-permute-done.5 = bf16[8,16,576]{2,1,0:T(8,128)(2,1)S(1)} collective-permute-done((bf16[8,16,576]{2,1,0:T(8,128)(2,1)S(1)}, bf16[8,16,576]{2,1,0:T(8,128)(2,1)S(1)}, u32[]{:S(2)}, u32[]{:S(2)}) %collective-permute-start.5) | collective-permute-done | bytes 147488 | tf_op jit(solution)/shard_map/ppermute | solution.py:33
  33.9 0.0 copy-start.3
  34.0 0.1 collective-permute-start.8
  34.1 2.8 %collective-permute-start.7 = (bf16[32,16,576]{2,1,0:T(8,128)(2,1)S(1)}, bf16[32,16,576]{2,1,0:T(8,128)(2,1)S(1)}, u32[]{:S(2)}, u32[]{:S(2)}) collective-permute-start(bf16[32,16,576]{2,1,0:T(8,128)(2,1)S(1)} %constant_dynamic-update-slice_fusion.4.refs_0_), channel_id=1, source_target_pairs={{128,0},{9,8},{144,16},{25,24},{160,32},{41,40},{176,48},{57,56},{... | collective-permute-start | bytes 1769480 | tf_op jit(solution)/shard_map/ppermute | solution.py:33
  36.9 2.3 %collective-permute-start.12 = (bf16[32,16,576]{2,1,0:T(8,128)(2,1)S(1)}, bf16[32,16,576]{2,1,0:T(8,128)(2,1)S(1)}, u32[]{:S(2)}, u32[]{:S(2)}) collective-permute-start(bf16[32,16,576]{2,1,0:T(8,128)(2,1)S(1)} %constant_dynamic-update-slice_fusion.4.refs_0_), channel_id=1, source_target_pairs={{4,0},{10,8},{20,16},{26,24},{36,32},{42,40},{52,48},{58,56},{68,6... | collective-permute-start | bytes 1769480 | tf_op jit(solution)/shard_map/ppermute | solution.py:33
  39.2 7.9 %absorb_0.1 = (f32[2048,512]{1,0:T(8,128)S(1)}, f32[2048,128]{1,0:T(8,128)S(1)}, f32[2048,128]{1,0:T(8,128)S(1)}) custom-call(s32[64]{0:T(128)S(1)} %copy-done.4, bf16[2,1024,576]{2,1,0:T(8,128)(2,1)S(1)} %make_queries.1.query_ref, bf16[32,16,576]{2,1,0:T(8,128)(2,1)S(1)} %constant_dynamic-update-slice_fusion.4.refs_0_, ...), custom_call_target="tpu_custom_call" | custom-call | flops 2281701376 | bytes 10485760 | tf_op jit(solution)/shard_map/absorb_0/pallas_call | solution.py:242
  47.1 5.0 %collective-permute-done.7.refs_0_ = bf16[32,16,576]{2,1,0:T(8,128)(2,1)S(1)} collective-permute-done((bf16[32,16,576]{2,1,0:T(8,128)(2,1)S(1)}, bf16[32,16,576]{2,1,0:T(8,128)(2,1)S(1)}, u32[]{:S(2)}, u32[]{:S(2)}) %collective-permute-start.7) | collective-permute-done | bytes 589856 | tf_op jit(solution)/shard_map/ppermute | solution.py:33
  52.1 3.7 %collective-permute-done.10.refs_2_ = bf16[32,16,576]{2,1,0:T(8,128)(2,1)S(1)} collective-permute-done((bf16[32,16,576]{2,1,0:T(8,128)(2,1)S(1)}, bf16[32,16,576]{2,1,0:T(8,128)(2,1)S(1)}, u32[]{:S(2)}, u32[]{:S(2)}) %collective-permute-start.10) | collective-permute-done | bytes 589856 | tf_op jit(solution)/shard_map/ppermute | solution.py:33
  55.7 0.0 collective-permute-start.13
  55.7 0.5 collective-permute-start.11
  56.2 0.0 collective-permute-start.9
  56.2 1.6 %collective-permute-done.13.refs_5_ = bf16[32,16,576]{2,1,0:T(8,128)(2,1)S(1)} collective-permute-done((bf16[32,16,576]{2,1,0:T(8,128)(2,1)S(1)}, bf16[32,16,576]{2,1,0:T(8,128)(2,1)S(1)}, u32[]{:S(2)}, u32[]{:S(2)}) %collective-permute-start.13) | collective-permute-done | bytes 589856 | tf_op jit(solution)/shard_map/ppermute | solution.py:37
  57.8 0.9 %collective-permute-done.11.refs_3_ = bf16[32,16,576]{2,1,0:T(8,128)(2,1)S(1)} collective-permute-done((bf16[32,16,576]{2,1,0:T(8,128)(2,1)S(1)}, bf16[32,16,576]{2,1,0:T(8,128)(2,1)S(1)}, u32[]{:S(2)}, u32[]{:S(2)}) %collective-permute-start.11) | collective-permute-done | bytes 589856 | tf_op jit(solution)/shard_map/ppermute | solution.py:37
  58.8 0.9 %collective-permute-done.9.refs_1_ = bf16[32,16,576]{2,1,0:T(8,128)(2,1)S(1)} collective-permute-done((bf16[32,16,576]{2,1,0:T(8,128)(2,1)S(1)}, bf16[32,16,576]{2,1,0:T(8,128)(2,1)S(1)}, u32[]{:S(2)}, u32[]{:S(2)}) %collective-permute-start.9) | collective-permute-done | bytes 589856 | tf_op jit(solution)/shard_map/ppermute | solution.py:37
  59.7 17.8 %absorb_1.1 = bf16[128,2048]{1,0:T(8,128)(2,1)} custom-call(s32[64]{0:T(128)S(1)} %copy-done.4, bf16[2,1024,576]{2,1,0:T(8,128)(2,1)S(1)} %make_queries.1.query_ref, bf16[32,16,576]{2,1,0:T(8,128)(2,1)S(1)} %collective-permute-done.7.refs_0_, bf16[32,16,576]{2,1,0:T(8,128)(2,1)S(1)} %collective-permute-done.9.refs_1_, ...), custom_call_target="tpu_custom_call" | custom-call | flops 6845104128 | bytes 10485760 | tf_op jit(solution)/shard_map/absorb_1/pallas_call | solution.py:242
  (21 shorter events, 0.2 us)
Async XLA Ops:
  0.0 7.1 %collective-permute-start.1 = (bf16[1,16,576]{2,1,0:T(8,128)(2,1)}, bf16[1,16,576]{2,1,0:T(8,128)(2,1)S(1)}, u32[]{:S(2)}, u32[]{:S(2)}) collective-permute-start(bf16[1,16,576]{2,1,0:T(8,128)(2,1)} %bitcast.2), channel_id=1, source_target_pairs={{112,0},{120,8},{0,16},{8,24},{16,32},{24,40},{32,48},{40,56},{48,... | collective-permute-start | bytes 55304 | tf_op jit(solution)/shard_map/ppermute | solution.py:33
  1.9 5.2 %collective-permute-start = (bf16[1,16,576]{2,1,0:T(8,128)(2,1)}, bf16[1,16,576]{2,1,0:T(8,128)(2,1)S(1)}, u32[]{:S(2)}, u32[]{:S(2)}) collective-permute-start(bf16[1,16,576]{2,1,0:T(8,128)(2,1)} %bitcast.3), channel_id=1, source_target_pairs={{16,0},{24,8},{32,16},{40,24},{48,32},{56,40},{64,48},{72,56},{80,... | collective-permute-start | bytes 55304 | tf_op jit(solution)/shard_map/ppermute | solution.py:33
  2.8 1.6 %copy-start = (bf16[16,128,512]{2,1,0:T(8,128)(2,1)S(1)}, bf16[16,128,512]{2,1,0:T(8,128)(2,1)}, u32[]{:S(2)}) copy-start(bf16[16,128,512]{2,1,0:T(8,128)(2,1)} %uk_ref.1) | copy-start | bytes 6291460
  4.4 1.0 %copy-start.1 = (bf16[128,2048]{1,0:T(8,128)(2,1)S(1)}, bf16[128,2048]{1,0:T(8,128)(2,1)}, u32[]{:S(2)}) copy-start(bf16[128,2048]{1,0:T(8,128)(2,1)} %nope_ref.1) | copy-start | bytes 1572868
  5.4 0.9 %copy-start.2 = (bf16[128,1024]{1,0:T(8,128)(2,1)S(1)}, bf16[128,1024]{1,0:T(8,128)(2,1)}, u32[]{:S(2)}) copy-start(bf16[128,1024]{1,0:T(8,128)(2,1)} %rope_ref.1) | copy-start | bytes 786436
  6.4 0.8 %copy-start.5 = (bf16[16,576]{1,0:T(8,128)(2,1)S(1)}, bf16[16,576]{1,0:T(8,128)(2,1)}, u32[]{:S(2)}) copy-start(bf16[16,576]{1,0:T(8,128)(2,1)} %param.8) | copy-start | bytes 55300
  6.4 32.8 %copy-start.4 = (s32[64]{0:T(128)S(1)}, s32[64]{0:T(128)}, u32[]{:S(2)}) copy-start(s32[64]{0:T(128)} %starts_ref.3) | copy-start | bytes 772
  7.2 15.0 %collective-permute-start.3 = (bf16[3,16,576]{2,1,0:T(8,128)(2,1)S(1)}, bf16[3,16,576]{2,1,0:T(8,128)(2,1)S(1)}, u32[]{:S(2)}, u32[]{:S(2)}) collective-permute-start(bf16[3,16,576]{2,1,0:T(8,128)(2,1)S(1)} %pad_maximum_fusion), channel_id=1, source_target_pairs={{80,0},{88,8},{96,16},{104,24},{112,32},{120,40},{0,48},{8,56},{16... | collective-permute-start | bytes 165896 | tf_op jit(solution)/shard_map/ppermute | solution.py:33
  14.3 7.8 %collective-permute-start.2 = (bf16[3,16,576]{2,1,0:T(8,128)(2,1)S(1)}, bf16[3,16,576]{2,1,0:T(8,128)(2,1)S(1)}, u32[]{:S(2)}, u32[]{:S(2)}) collective-permute-start(bf16[3,16,576]{2,1,0:T(8,128)(2,1)S(1)} %pad_maximum_fusion), channel_id=1, source_target_pairs={{48,0},{56,8},{64,16},{72,24},{80,32},{88,40},{96,48},{104,56},{11... | collective-permute-start | bytes 165896 | tf_op jit(solution)/shard_map/ppermute | solution.py:33
  22.2 7.7 %collective-permute-start.4 = (bf16[8,16,576]{2,1,0:T(8,128)(2,1)S(1)}, bf16[8,16,576]{2,1,0:T(8,128)(2,1)S(1)}, u32[]{:S(2)}, u32[]{:S(2)}) collective-permute-start(bf16[8,16,576]{2,1,0:T(8,128)(2,1)S(1)} %slice_dynamic-update-slice_fusion), channel_id=1, source_target_pairs={{1,0},{136,8},{17,16},{152,24},{33,32},{168,40},{49,48},{184,56},{... | collective-permute-start | bytes 442376 | tf_op jit(solution)/shard_map/ppermute | solution.py:33
  25.3 8.6 %collective-permute-start.6 = (bf16[8,16,576]{2,1,0:T(8,128)(2,1)S(1)}, bf16[8,16,576]{2,1,0:T(8,128)(2,1)S(1)}, u32[]{:S(2)}, u32[]{:S(2)}) collective-permute-start(bf16[8,16,576]{2,1,0:T(8,128)(2,1)S(1)} %slice_dynamic-update-slice_fusion), channel_id=1, source_target_pairs={{2,0},{12,8},{18,16},{28,24},{34,32},{44,40},{50,48},{60,56},{66,6... | collective-permute-start | bytes 442376 | tf_op jit(solution)/shard_map/ppermute | solution.py:33
  25.9 8.0 %collective-permute-start.5 = (bf16[8,16,576]{2,1,0:T(8,128)(2,1)S(1)}, bf16[8,16,576]{2,1,0:T(8,128)(2,1)S(1)}, u32[]{:S(2)}, u32[]{:S(2)}) collective-permute-start(bf16[8,16,576]{2,1,0:T(8,128)(2,1)S(1)} %slice_dynamic-update-slice_fusion), channel_id=1, source_target_pairs={{3,0},{140,8},{19,16},{156,24},{35,32},{172,40},{51,48},{188,56},{... | collective-permute-start | bytes 442376 | tf_op jit(solution)/shard_map/ppermute | solution.py:33
  33.9 25.7 %copy-start.3 = (bf16[16,512,128]{2,1,0:T(8,128)(2,1)S(1)}, bf16[16,512,128]{2,1,0:T(8,128)(2,1)}, u32[]{:S(2)}) copy-start(bf16[16,512,128]{2,1,0:T(8,128)(2,1)} %refs_9_.1) | copy-start | bytes 6291460
  34.0 5.2 %collective-permute-start.8 = (bf16[32,16,576]{2,1,0:T(8,128)(2,1)S(1)}, bf16[32,16,576]{2,1,0:T(8,128)(2,1)S(1)}, u32[]{:S(2)}, u32[]{:S(2)}) collective-permute-start(bf16[32,16,576]{2,1,0:T(8,128)(2,1)S(1)} %constant_dynamic-update-slice_fusion.4.refs_0_), channel_id=1, source_target_pairs={{0,8},{8,0},{16,24},{24,16},{32,40},{40,32},{48,56},{56,48},{64,72... | collective-permute-start | bytes 1769480 | tf_op jit(solution)/shard_map/ppermute | solution.py:37
  34.1 18.0 %collective-permute-start.7 = (bf16[32,16,576]{2,1,0:T(8,128)(2,1)S(1)}, bf16[32,16,576]{2,1,0:T(8,128)(2,1)S(1)}, u32[]{:S(2)}, u32[]{:S(2)}) collective-permute-start(bf16[32,16,576]{2,1,0:T(8,128)(2,1)S(1)} %constant_dynamic-update-slice_fusion.4.refs_0_), channel_id=1, source_target_pairs={{128,0},{9,8},{144,16},{25,24},{160,32},{41,40},{176,48},{57,56},{... | collective-permute-start | bytes 1769480 | tf_op jit(solution)/shard_map/ppermute | solution.py:33
  36.9 18.8 %collective-permute-start.10 = (bf16[32,16,576]{2,1,0:T(8,128)(2,1)S(1)}, bf16[32,16,576]{2,1,0:T(8,128)(2,1)S(1)}, u32[]{:S(2)}, u32[]{:S(2)}) collective-permute-start(bf16[32,16,576]{2,1,0:T(8,128)(2,1)S(1)} %constant_dynamic-update-slice_fusion.4.refs_0_), channel_id=1, source_target_pairs={{132,0},{11,8},{148,16},{27,24},{164,32},{43,40},{180,48},{59,56},... | collective-permute-start | bytes 1769480 | tf_op jit(solution)/shard_map/ppermute | solution.py:33
  36.9 18.8 %collective-permute-start.12 = (bf16[32,16,576]{2,1,0:T(8,128)(2,1)S(1)}, bf16[32,16,576]{2,1,0:T(8,128)(2,1)S(1)}, u32[]{:S(2)}, u32[]{:S(2)}) collective-permute-start(bf16[32,16,576]{2,1,0:T(8,128)(2,1)S(1)} %constant_dynamic-update-slice_fusion.4.refs_0_), channel_id=1, source_target_pairs={{4,0},{10,8},{20,16},{26,24},{36,32},{42,40},{52,48},{58,56},{68,6... | collective-permute-start | bytes 1769480 | tf_op jit(solution)/shard_map/ppermute | solution.py:33
  55.7 2.1 %collective-permute-start.13 = (bf16[32,16,576]{2,1,0:T(8,128)(2,1)S(1)}, bf16[32,16,576]{2,1,0:T(8,128)(2,1)S(1)}, u32[]{:S(2)}, u32[]{:S(2)}) collective-permute-start(bf16[32,16,576]{2,1,0:T(8,128)(2,1)S(1)} %collective-permute-done.12.refs_4_), channel_id=1, source_target_pairs={{0,8},{8,0},{16,24},{24,16},{32,40},{40,32},{48,56},{56,48},{64,72... | collective-permute-start | bytes 1769480 | tf_op jit(solution)/shard_map/ppermute | solution.py:37
  55.7 3.0 %collective-permute-start.11 = (bf16[32,16,576]{2,1,0:T(8,128)(2,1)S(1)}, bf16[32,16,576]{2,1,0:T(8,128)(2,1)S(1)}, u32[]{:S(2)}, u32[]{:S(2)}) collective-permute-start(bf16[32,16,576]{2,1,0:T(8,128)(2,1)S(1)} %collective-permute-done.10.refs_2_), channel_id=1, source_target_pairs={{0,8},{8,0},{16,24},{24,16},{32,40},{40,32},{48,56},{56,48},{64,72... | collective-permute-start | bytes 1769480 | tf_op jit(solution)/shard_map/ppermute | solution.py:37
  56.2 3.5 %collective-permute-start.9 = (bf16[32,16,576]{2,1,0:T(8,128)(2,1)S(1)}, bf16[32,16,576]{2,1,0:T(8,128)(2,1)S(1)}, u32[]{:S(2)}, u32[]{:S(2)}) collective-permute-start(bf16[32,16,576]{2,1,0:T(8,128)(2,1)S(1)} %collective-permute-done.7.refs_0_), channel_id=1, source_target_pairs={{0,8},{8,0},{16,24},{24,16},{32,40},{40,32},{48,56},{56,48},{64,72... | collective-permute-start | bytes 1769480 | tf_op jit(solution)/shard_map/ppermute | solution.py:37

commit v7 on v6

--- a/solution.py
+++ b/solution.py
@@ -12,7 +12,7 @@
 PIECE = 16
 TILE = 256
 NOPE = 128
-GROUPS = ((0,), (1, 2, 3))
+GROUPS = ((0,), (1, 2), (3,))
 OFFSETS = (0, 1, 3, 2)
 WINDOW = (0, 1, 7, 3, 4, 2, 5, 6)
 
@@ -159,7 +159,7 @@
         is_high = index >= tiles_low
         half = jnp.where(is_high, 1, 0)
         at = jnp.minimum((index - half * tiles_low) * TILE, keys.shape[0] - TILE)
-        start = jnp.where(index >= tiles, -block, jnp.where(is_high, high, low))
+        start = jnp.where(is_high, high, low)
         return half, pl.multiple_of(at, TILE), start
 
     def score(buffer, index):
@@ -200,12 +200,25 @@
 
     score(even, 0)
 
-    @pl.loop(0, (tiles + 1) >> 1)
-    def _(step):
-        score(odd, 2 * step + 1)
-        absorb_tile(even, 2 * step)
-        score(even, 2 * step + 2)
-        absorb_tile(odd, 2 * step + 1)
+    @pl.loop(0, tiles - 1)
+    def _(index):
+        @pl.when((index & 1) == 0)
+        def _():
+            score(odd, index + 1)
+            absorb_tile(even, index)
+
+        @pl.when((index & 1) == 1)
+        def _():
+            score(even, index + 1)
+            absorb_tile(odd, index)
+
+    @pl.when((tiles & 1) == 1)
+    def _():
+        absorb_tile(even, tiles - 1)
+
+    @pl.when((tiles & 1) == 0)
+    def _():
+        absorb_tile(odd, tiles - 1)
 
     if finish:
         value_width = uv_ref.shape[2]
@@ -261,8 +274,8 @@
     state = ()
     for lasts in GROUPS:
         chunks = [own[last] for last in lasts]
-        for i in range(len(chunks) if state else 0):
-            chunks[i], state = lax.optimization_barrier((chunks[i], state))
+        if state:
+            *chunks, state = lax.optimization_barrier((*chunks, state))
         pieces = [piece for chunk in chunks for piece in (chunk, other_core(chunk))]
         finish = lasts[-1] == len(own) - 1
         state = absorb(lasts, finish, block_start, query, pieces, state, w_uv)

time: 77.7 us -> 73.6 us (0.947)
  the two profiles are of different devices: /device:TPU:32 before, /device:TPU:38 now
where the time goes in v7:
time: 73.6 us; the launch traced here: 73.2 us
  Pallas kernels  27.4 us (37%)
  waiting for transfers between devices  23.2 us (32%)
  starting transfers between devices  18 us (24%)
  local copies, waits for them, and re-layouts  4.48 us (6%)
    pallas_call x3, Pallas kernels, absorb(): pl.pallas_call(functools.partial(absorb_kernel, lasts, finish), in_specs=...  26.7 us
    ppermute x10, waiting for transfers between devices, from_offset(): return lax.ppermute(value, BOTH, pairs)  19.9 us
    ppermute x10, starting transfers between devices, from_offset(): return lax.ppermute(value, BOTH, pairs)  17.2 us
    unnamed x19, local copies, waits for them, and re-layouts  4.44 us
    ppermute x4, waiting for transfers between devices, other_core(): return lax.ppermute(value, 'ctx', [(i, i ^ 1) for i in range(32)])  3.28 us
  transfers between devices with their start and end apart: 14, of which 8 were waited for; matrix products, arithmetic and copies ran while one was open for 1% of the time, Pallas kernels for 24%

profile of v7, /device:TPU:38, one launch (start us, length us, event | category | flops | bytes accessed | tf_op | source)
XLA Modules:
  0.0 73.2 jit_solution(5354231062605812307)
XLA Ops:
  0.0 1.9 %collective-permute-start.1 = (bf16[1,16,576]{2,1,0:T(8,128)(2,1)}, bf16[1,16,576]{2,1,0:T(8,128)(2,1)S(1)}, u32[]{:S(2)}, u32[]{:S(2)}) collective-permute-start(bf16[1,16,576]{2,1,0:T(8,128)(2,1)} %bitcast.2), channel_id=1, source_target_pairs={{112,0},{120,8},{0,16},{8,24},{16,32},{24,40},{32,48},{40,56},{48,... | collective-permute-start | bytes 55304 | tf_op jit(solution)/shard_map/ppermute | solution.py:33
  1.9 0.1 collective-permute-start
  2.0 0.8 %constant_dynamic-update-slice_fusion.3 = bf16[8,16,576]{2,1,0:T(8,128)(2,1)S(1)} fusion(bf16[16,576]{1,0:T(8,128)(2,1)} %param.8), kind=kLoop, calls=%fused_computation.5 | loop fusion | bytes 38912
  2.8 1.6 %copy-done.1 = bf16[16,128,512]{2,1,0:T(8,128)(2,1)S(1)} copy-done((bf16[16,128,512]{2,1,0:T(8,128)(2,1)S(1)}, bf16[16,128,512]{2,1,0:T(8,128)(2,1)}, u32[]{:S(2)}) %copy-start.1) | copy-done | bytes 2097176
  4.4 1.0 %copy-done.2 = bf16[128,2048]{1,0:T(8,128)(2,1)S(1)} copy-done((bf16[128,2048]{1,0:T(8,128)(2,1)S(1)}, bf16[128,2048]{1,0:T(8,128)(2,1)}, u32[]{:S(2)}) %copy-start.2) | copy-done | bytes 524312
  5.4 0.9 %copy-done.3 = bf16[128,1024]{1,0:T(8,128)(2,1)S(1)} copy-done((bf16[128,1024]{1,0:T(8,128)(2,1)S(1)}, bf16[128,1024]{1,0:T(8,128)(2,1)}, u32[]{:S(2)}) %copy-start.3) | copy-done | bytes 262168
  6.4 0.8 %make_queries.1.query_ref = bf16[2,1024,576]{2,1,0:T(8,128)(2,1)S(1)} custom-call(bf16[128,2048]{1,0:T(8,128)(2,1)S(1)} %copy-done.2, bf16[128,1024]{1,0:T(8,128)(2,1)S(1)} %copy-done.3, bf16[16,128,512]{2,1,0:T(8,128)(2,1)S(1)} %copy-done.1), custom_call_target="tpu_custom_call" | custom-call | flops 268435456 | bytes 6291456 | tf_op jit(solution)/shard_map/make_queries/pallas_call | solution.py:81
  7.1 0.0 collective-permute-done.1
  7.2 7.1 %collective-permute-start.3 = (bf16[3,16,576]{2,1,0:T(8,128)(2,1)S(1)}, bf16[3,16,576]{2,1,0:T(8,128)(2,1)S(1)}, u32[]{:S(2)}, u32[]{:S(2)}) collective-permute-start(bf16[3,16,576]{2,1,0:T(8,128)(2,1)S(1)} %pad_maximum_fusion), channel_id=1, source_target_pairs={{80,0},{88,8},{96,16},{104,24},{112,32},{120,40},{0,48},{8,56},{16... | collective-permute-start | bytes 165896 | tf_op jit(solution)/shard_map/ppermute | solution.py:33
  14.3 7.8 %collective-permute-done.2 = bf16[3,16,576]{2,1,0:T(8,128)(2,1)S(1)} collective-permute-done((bf16[3,16,576]{2,1,0:T(8,128)(2,1)S(1)}, bf16[3,16,576]{2,1,0:T(8,128)(2,1)S(1)}, u32[]{:S(2)}, u32[]{:S(2)}) %collective-permute-start.2) | collective-permute-done | bytes 55328 | tf_op jit(solution)/shard_map/ppermute | solution.py:33
  22.2 0.0 collective-permute-done.3
  22.2 3.1 %collective-permute-start.4 = (bf16[8,16,576]{2,1,0:T(8,128)(2,1)S(1)}, bf16[8,16,576]{2,1,0:T(8,128)(2,1)S(1)}, u32[]{:S(2)}, u32[]{:S(2)}) collective-permute-start(bf16[8,16,576]{2,1,0:T(8,128)(2,1)S(1)} %slice_dynamic-update-slice_fusion), channel_id=1, source_target_pairs={{1,0},{136,8},{17,16},{152,24},{33,32},{168,40},{49,48},{184,56},{... | collective-permute-start | bytes 442376 | tf_op jit(solution)/shard_map/ppermute | solution.py:33
  25.3 0.6 collective-permute-start.6
  25.9 1.0 %collective-permute-start.5 = (bf16[8,16,576]{2,1,0:T(8,128)(2,1)S(1)}, bf16[8,16,576]{2,1,0:T(8,128)(2,1)S(1)}, u32[]{:S(2)}, u32[]{:S(2)}) collective-permute-start(bf16[8,16,576]{2,1,0:T(8,128)(2,1)S(1)} %slice_dynamic-update-slice_fusion), channel_id=1, source_target_pairs={{3,0},{140,8},{19,16},{156,24},{35,32},{172,40},{51,48},{188,56},{... | collective-permute-start | bytes 442376 | tf_op jit(solution)/shard_map/ppermute | solution.py:33
  26.9 3.0 %collective-permute-done.4 = bf16[8,16,576]{2,1,0:T(8,128)(2,1)S(1)} collective-permute-done((bf16[8,16,576]{2,1,0:T(8,128)(2,1)S(1)}, bf16[8,16,576]{2,1,0:T(8,128)(2,1)S(1)}, u32[]{:S(2)}, u32[]{:S(2)}) %collective-permute-start.4) | collective-permute-done | bytes 147488 | tf_op jit(solution)/shard_map/ppermute | solution.py:33
  29.9 3.9 %collective-permute-done.5 = bf16[8,16,576]{2,1,0:T(8,128)(2,1)S(1)} collective-permute-done((bf16[8,16,576]{2,1,0:T(8,128)(2,1)S(1)}, bf16[8,16,576]{2,1,0:T(8,128)(2,1)S(1)}, u32[]{:S(2)}, u32[]{:S(2)}) %collective-permute-start.5) | collective-permute-done | bytes 147488 | tf_op jit(solution)/shard_map/ppermute | solution.py:33
  33.9 0.1 collective-permute-start.10
  34.0 0.6 collective-permute-start.9
  34.6 1.5 %collective-permute-start.8 = (bf16[32,16,576]{2,1,0:T(8,128)(2,1)S(1)}, bf16[32,16,576]{2,1,0:T(8,128)(2,1)S(1)}, u32[]{:S(2)}, u32[]{:S(2)}) collective-permute-start(bf16[32,16,576]{2,1,0:T(8,128)(2,1)S(1)} %constant_dynamic-update-slice_fusion.4.refs_0_), channel_id=1, source_target_pairs={{128,0},{9,8},{144,16},{25,24},{160,32},{41,40},{176,48},{57,56},{... | collective-permute-start | bytes 1769480 | tf_op jit(solution)/shard_map/ppermute | solution.py:33
  36.1 0.0 collective-permute-done.10.refs_1_
  36.2 5.1 %absorb_0.1 = (f32[2048,512]{1,0:T(8,128)S(1)}, f32[2048,128]{1,0:T(8,128)S(1)}, f32[2048,128]{1,0:T(8,128)S(1)}) custom-call(s32[64]{0:T(128)S(1)} %copy-done.4, bf16[2,1024,576]{2,1,0:T(8,128)(2,1)S(1)} %make_queries.1.query_ref, bf16[32,16,576]{2,1,0:T(8,128)(2,1)S(1)} %constant_dynamic-update-slice_fusion.4.refs_0_, ...), custom_call_target="tpu_custom_call" | custom-call | flops 2281701376 | bytes 10485760 | tf_op jit(solution)/shard_map/absorb_0/pallas_call | solution.py:255
  41.3 3.4 %collective-permute-done.9.refs_2_ = bf16[32,16,576]{2,1,0:T(8,128)(2,1)S(1)} collective-permute-done((bf16[32,16,576]{2,1,0:T(8,128)(2,1)S(1)}, bf16[32,16,576]{2,1,0:T(8,128)(2,1)S(1)}, u32[]{:S(2)}, u32[]{:S(2)}) %collective-permute-start.9) | collective-permute-done | bytes 589856 | tf_op jit(solution)/shard_map/ppermute | solution.py:33
  44.7 1.7 %collective-permute-done.8.refs_0_ = bf16[32,16,576]{2,1,0:T(8,128)(2,1)S(1)} collective-permute-done((bf16[32,16,576]{2,1,0:T(8,128)(2,1)S(1)}, bf16[32,16,576]{2,1,0:T(8,128)(2,1)S(1)}, u32[]{:S(2)}, u32[]{:S(2)}) %collective-permute-start.8) | collective-permute-done | bytes 589856 | tf_op jit(solution)/shard_map/ppermute | solution.py:33
  46.4 0.0 collective-permute-start.11
  46.4 0.5 collective-permute-start.12
  46.9 1.2 %collective-permute-start.7 = (bf16[32,16,576]{2,1,0:T(8,128)(2,1)S(1)}, bf16[32,16,576]{2,1,0:T(8,128)(2,1)S(1)}, u32[]{:S(2)}, u32[]{:S(2)}) collective-permute-start(bf16[32,16,576]{2,1,0:T(8,128)(2,1)S(1)} %constant_dynamic-update-slice_fusion.4.refs_0_), channel_id=1, source_target_pairs={{4,0},{10,8},{20,16},{26,24},{36,32},{42,40},{52,48},{58,56},{68,6... | collective-permute-start | bytes 1769480 | tf_op jit(solution)/shard_map/ppermute | solution.py:33
  48.1 0.4 collective-permute-done.11.refs_1_
  48.5 0.9 %collective-permute-done.12.refs_3_ = bf16[32,16,576]{2,1,0:T(8,128)(2,1)S(1)} collective-permute-done((bf16[32,16,576]{2,1,0:T(8,128)(2,1)S(1)}, bf16[32,16,576]{2,1,0:T(8,128)(2,1)S(1)}, u32[]{:S(2)}, u32[]{:S(2)}) %collective-permute-start.12) | collective-permute-done | bytes 589856 | tf_op jit(solution)/shard_map/ppermute | solution.py:37
  49.4 11.5 %absorb_1.1 = (f32[2048,512]{1,0:T(8,128)S(1)}, f32[2048,128]{1,0:T(8,128)S(1)}, f32[2048,128]{1,0:T(8,128)S(1)}) custom-call(s32[64]{0:T(128)S(1)} %copy-done.4, bf16[2,1024,576]{2,1,0:T(8,128)(2,1)S(1)} %make_queries.1.query_ref, bf16[32,16,576]{2,1,0:T(8,128)(2,1)S(1)} %collective-permute-done.8.refs_0_, ...), custom_call_target="tpu_custom_call" | custom-call | flops 4563402752 | bytes 10485760 | tf_op jit(solution)/shard_map/absorb_1/pallas_call | solution.py:255
  60.9 0.2 collective-permute-start.13
  61.2 2.0 %collective-permute-done.13.refs_1_ = bf16[32,16,576]{2,1,0:T(8,128)(2,1)S(1)} collective-permute-done((bf16[32,16,576]{2,1,0:T(8,128)(2,1)S(1)}, bf16[32,16,576]{2,1,0:T(8,128)(2,1)S(1)}, u32[]{:S(2)}, u32[]{:S(2)}) %collective-permute-start.13) | collective-permute-done | bytes 589856 | tf_op jit(solution)/shard_map/ppermute | solution.py:37
  63.1 10.1 %absorb_3.1 = bf16[128,2048]{1,0:T(8,128)(2,1)} custom-call(s32[64]{0:T(128)S(1)} %copy-done.4, bf16[2,1024,576]{2,1,0:T(8,128)(2,1)S(1)} %make_queries.1.query_ref, bf16[32,16,576]{2,1,0:T(8,128)(2,1)S(1)} %collective-permute-done.7.refs_0_, bf16[32,16,576]{2,1,0:T(8,128)(2,1)S(1)} %collective-permute-done.13.refs_1_, ...), custom_call_target="tpu_custom_call" | custom-call | flops 2281701376 | bytes 10485760 | tf_op jit(solution)/shard_map/absorb_3/pallas_call | solution.py:255
  (22 shorter events, 0.2 us)
Async XLA Ops:
  0.0 7.1 %collective-permute-start.1 = (bf16[1,16,576]{2,1,0:T(8,128)(2,1)}, bf16[1,16,576]{2,1,0:T(8,128)(2,1)S(1)}, u32[]{:S(2)}, u32[]{:S(2)}) collective-permute-start(bf16[1,16,576]{2,1,0:T(8,128)(2,1)} %bitcast.2), channel_id=1, source_target_pairs={{112,0},{120,8},{0,16},{8,24},{16,32},{24,40},{32,48},{40,56},{48,... | collective-permute-start | bytes 55304 | tf_op jit(solution)/shard_map/ppermute | solution.py:33
  1.9 5.2 %collective-permute-start = (bf16[1,16,576]{2,1,0:T(8,128)(2,1)}, bf16[1,16,576]{2,1,0:T(8,128)(2,1)S(1)}, u32[]{:S(2)}, u32[]{:S(2)}) collective-permute-start(bf16[1,16,576]{2,1,0:T(8,128)(2,1)} %bitcast.3), channel_id=1, source_target_pairs={{16,0},{24,8},{32,16},{40,24},{48,32},{56,40},{64,48},{72,56},{80,... | collective-permute-start | bytes 55304 | tf_op jit(solution)/shard_map/ppermute | solution.py:33
  2.8 1.6 %copy-start.1 = (bf16[16,128,512]{2,1,0:T(8,128)(2,1)S(1)}, bf16[16,128,512]{2,1,0:T(8,128)(2,1)}, u32[]{:S(2)}) copy-start(bf16[16,128,512]{2,1,0:T(8,128)(2,1)} %uk_ref.1) | copy-start | bytes 6291460
  4.4 1.0 %copy-start.2 = (bf16[128,2048]{1,0:T(8,128)(2,1)S(1)}, bf16[128,2048]{1,0:T(8,128)(2,1)}, u32[]{:S(2)}) copy-start(bf16[128,2048]{1,0:T(8,128)(2,1)} %nope_ref.1) | copy-start | bytes 1572868
  5.4 0.9 %copy-start.3 = (bf16[128,1024]{1,0:T(8,128)(2,1)S(1)}, bf16[128,1024]{1,0:T(8,128)(2,1)}, u32[]{:S(2)}) copy-start(bf16[128,1024]{1,0:T(8,128)(2,1)} %rope_ref.1) | copy-start | bytes 786436
  6.4 0.8 %copy-start.5 = (bf16[16,576]{1,0:T(8,128)(2,1)S(1)}, bf16[16,576]{1,0:T(8,128)(2,1)}, u32[]{:S(2)}) copy-start(bf16[16,576]{1,0:T(8,128)(2,1)} %param.8) | copy-start | bytes 55300
  6.4 29.8 %copy-start.4 = (s32[64]{0:T(128)S(1)}, s32[64]{0:T(128)}, u32[]{:S(2)}) copy-start(s32[64]{0:T(128)} %starts_ref.5) | copy-start | bytes 772
  7.2 15.0 %collective-permute-start.3 = (bf16[3,16,576]{2,1,0:T(8,128)(2,1)S(1)}, bf16[3,16,576]{2,1,0:T(8,128)(2,1)S(1)}, u32[]{:S(2)}, u32[]{:S(2)}) collective-permute-start(bf16[3,16,576]{2,1,0:T(8,128)(2,1)S(1)} %pad_maximum_fusion), channel_id=1, source_target_pairs={{80,0},{88,8},{96,16},{104,24},{112,32},{120,40},{0,48},{8,56},{16... | collective-permute-start | bytes 165896 | tf_op jit(solution)/shard_map/ppermute | solution.py:33
  14.3 7.8 %collective-permute-start.2 = (bf16[3,16,576]{2,1,0:T(8,128)(2,1)S(1)}, bf16[3,16,576]{2,1,0:T(8,128)(2,1)S(1)}, u32[]{:S(2)}, u32[]{:S(2)}) collective-permute-start(bf16[3,16,576]{2,1,0:T(8,128)(2,1)S(1)} %pad_maximum_fusion), channel_id=1, source_target_pairs={{48,0},{56,8},{64,16},{72,24},{80,32},{88,40},{96,48},{104,56},{11... | collective-permute-start | bytes 165896 | tf_op jit(solution)/shard_map/ppermute | solution.py:33
  22.2 7.7 %collective-permute-start.4 = (bf16[8,16,576]{2,1,0:T(8,128)(2,1)S(1)}, bf16[8,16,576]{2,1,0:T(8,128)(2,1)S(1)}, u32[]{:S(2)}, u32[]{:S(2)}) collective-permute-start(bf16[8,16,576]{2,1,0:T(8,128)(2,1)S(1)} %slice_dynamic-update-slice_fusion), channel_id=1, source_target_pairs={{1,0},{136,8},{17,16},{152,24},{33,32},{168,40},{49,48},{184,56},{... | collective-permute-start | bytes 442376 | tf_op jit(solution)/shard_map/ppermute | solution.py:33
  25.3 8.6 %collective-permute-start.6 = (bf16[8,16,576]{2,1,0:T(8,128)(2,1)S(1)}, bf16[8,16,576]{2,1,0:T(8,128)(2,1)S(1)}, u32[]{:S(2)}, u32[]{:S(2)}) collective-permute-start(bf16[8,16,576]{2,1,0:T(8,128)(2,1)S(1)} %slice_dynamic-update-slice_fusion), channel_id=1, source_target_pairs={{2,0},{12,8},{18,16},{28,24},{34,32},{44,40},{50,48},{60,56},{66,6... | collective-permute-start | bytes 442376 | tf_op jit(solution)/shard_map/ppermute | solution.py:33
  25.9 7.9 %collective-permute-start.5 = (bf16[8,16,576]{2,1,0:T(8,128)(2,1)S(1)}, bf16[8,16,576]{2,1,0:T(8,128)(2,1)S(1)}, u32[]{:S(2)}, u32[]{:S(2)}) collective-permute-start(bf16[8,16,576]{2,1,0:T(8,128)(2,1)S(1)} %slice_dynamic-update-slice_fusion), channel_id=1, source_target_pairs={{3,0},{140,8},{19,16},{156,24},{35,32},{172,40},{51,48},{188,56},{... | collective-permute-start | bytes 442376 | tf_op jit(solution)/shard_map/ppermute | solution.py:33
  33.9 2.2 %collective-permute-start.10 = (bf16[32,16,576]{2,1,0:T(8,128)(2,1)S(1)}, bf16[32,16,576]{2,1,0:T(8,128)(2,1)S(1)}, u32[]{:S(2)}, u32[]{:S(2)}) collective-permute-start(bf16[32,16,576]{2,1,0:T(8,128)(2,1)S(1)} %constant_dynamic-update-slice_fusion.4.refs_0_), channel_id=1, source_target_pairs={{0,8},{8,0},{16,24},{24,16},{32,40},{40,32},{48,56},{56,48},{64,72... | collective-permute-start | bytes 1769480 | tf_op jit(solution)/shard_map/ppermute | solution.py:37
  34.0 10.7 %collective-permute-start.9 = (bf16[32,16,576]{2,1,0:T(8,128)(2,1)S(1)}, bf16[32,16,576]{2,1,0:T(8,128)(2,1)S(1)}, u32[]{:S(2)}, u32[]{:S(2)}) collective-permute-start(bf16[32,16,576]{2,1,0:T(8,128)(2,1)S(1)} %constant_dynamic-update-slice_fusion.4.refs_0_), channel_id=1, source_target_pairs={{132,0},{11,8},{148,16},{27,24},{164,32},{43,40},{180,48},{59,56},... | collective-permute-start | bytes 1769480 | tf_op jit(solution)/shard_map/ppermute | solution.py:33
  34.6 11.8 %collective-permute-start.8 = (bf16[32,16,576]{2,1,0:T(8,128)(2,1)S(1)}, bf16[32,16,576]{2,1,0:T(8,128)(2,1)S(1)}, u32[]{:S(2)}, u32[]{:S(2)}) collective-permute-start(bf16[32,16,576]{2,1,0:T(8,128)(2,1)S(1)} %constant_dynamic-update-slice_fusion.4.refs_0_), channel_id=1, source_target_pairs={{128,0},{9,8},{144,16},{25,24},{160,32},{41,40},{176,48},{57,56},{... | collective-permute-start | bytes 1769480 | tf_op jit(solution)/shard_map/ppermute | solution.py:33
  46.4 16.7 %copy-start = (bf16[16,512,128]{2,1,0:T(8,128)(2,1)S(1)}, bf16[16,512,128]{2,1,0:T(8,128)(2,1)}, u32[]{:S(2)}) copy-start(bf16[16,512,128]{2,1,0:T(8,128)(2,1)} %refs_5_.1) | copy-start | bytes 6291460
  46.4 2.1 %collective-permute-start.11 = (bf16[32,16,576]{2,1,0:T(8,128)(2,1)S(1)}, bf16[32,16,576]{2,1,0:T(8,128)(2,1)S(1)}, u32[]{:S(2)}, u32[]{:S(2)}) collective-permute-start(bf16[32,16,576]{2,1,0:T(8,128)(2,1)S(1)} %collective-permute-done.8.refs_0_), channel_id=1, source_target_pairs={{0,8},{8,0},{16,24},{24,16},{32,40},{40,32},{48,56},{56,48},{64,72... | collective-permute-start | bytes 1769480 | tf_op jit(solution)/shard_map/ppermute | solution.py:37
  46.4 3.0 %collective-permute-start.12 = (bf16[32,16,576]{2,1,0:T(8,128)(2,1)S(1)}, bf16[32,16,576]{2,1,0:T(8,128)(2,1)S(1)}, u32[]{:S(2)}, u32[]{:S(2)}) collective-permute-start(bf16[32,16,576]{2,1,0:T(8,128)(2,1)S(1)} %collective-permute-done.9.refs_2_), channel_id=1, source_target_pairs={{0,8},{8,0},{16,24},{24,16},{32,40},{40,32},{48,56},{56,48},{64,72... | collective-permute-start | bytes 1769480 | tf_op jit(solution)/shard_map/ppermute | solution.py:37
  46.9 14.0 %collective-permute-start.7 = (bf16[32,16,576]{2,1,0:T(8,128)(2,1)S(1)}, bf16[32,16,576]{2,1,0:T(8,128)(2,1)S(1)}, u32[]{:S(2)}, u32[]{:S(2)}) collective-permute-start(bf16[32,16,576]{2,1,0:T(8,128)(2,1)S(1)} %constant_dynamic-update-slice_fusion.4.refs_0_), channel_id=1, source_target_pairs={{4,0},{10,8},{20,16},{26,24},{36,32},{42,40},{52,48},{58,56},{68,6... | collective-permute-start | bytes 1769480 | tf_op jit(solution)/shard_map/ppermute | solution.py:33
  60.9 2.2 %collective-permute-start.13 = (bf16[32,16,576]{2,1,0:T(8,128)(2,1)S(1)}, bf16[32,16,576]{2,1,0:T(8,128)(2,1)S(1)}, u32[]{:S(2)}, u32[]{:S(2)}) collective-permute-start(bf16[32,16,576]{2,1,0:T(8,128)(2,1)S(1)} %collective-permute-done.7.refs_0_), channel_id=1, source_target_pairs={{0,8},{8,0},{16,24},{24,16},{32,40},{40,32},{48,56},{56,48},{64,72... | collective-permute-start | bytes 1769480 | tf_op jit(solution)/shard_map/ppermute | solution.py:37

commit v8 on v7

--- a/solution.py
+++ b/solution.py
@@ -45,10 +45,9 @@
     far_up = from_offset(window, (0, 0, 3), (0, 0, 3))
     far_down = from_offset(window, (0, 0, 5), (0, 0, 5))[:2]
     column = jnp.concatenate([window, far_up, far_down])
-    column, query = lax.optimization_barrier((column, query))
-    plane = jnp.concatenate(
-        [column] + [from_offset(column, (0, d, 0), (d, 0, 0)) for d in OFFSETS[1:]]
-    )
+    lines = [from_offset(column, (0, d, 0), (d, 0, 0)) for d in OFFSETS[1:]]
+    *lines, query = lax.optimization_barrier((*lines, query))
+    plane = jnp.concatenate([column, *lines])
     lines = [from_offset(plane, (d, 0, 0), (0, d, 0)) for d in OFFSETS[1:]]
     return [plane, *lines], query
 

time: 73.6 us -> 70 us (0.951)
  the two profiles are of different devices: /device:TPU:38 before, /device:TPU:1 now
where the time goes in v8:
time: 70 us; the launch traced here: 69.3 us
  Pallas kernels  27.5 us (39%)
  starting transfers between devices  26.5 us (38%)
  waiting for transfers between devices  9.9 us (14%)
  local copies, waits for them, and re-layouts  4.48 us (6%)
  other arithmetic  0.74 us (1%)
    pallas_call x3, Pallas kernels, absorb(): pl.pallas_call(functools.partial(absorb_kernel, lasts, finish), in_specs=...  26.8 us
    ppermute x10, starting transfers between devices, from_offset(): return lax.ppermute(value, BOTH, pairs)  20 us
    ppermute x4, starting transfers between devices, other_core(): return lax.ppermute(value, 'ctx', [(i, i ^ 1) for i in range(32)])  6.57 us
    ppermute x10, waiting for transfers between devices, from_offset(): return lax.ppermute(value, BOTH, pairs)  6.33 us
    unnamed x17, local copies, waits for them, and re-layouts  4.46 us
    ppermute x4, waiting for transfers between devices, other_core(): return lax.ppermute(value, 'ctx', [(i, i ^ 1) for i in range(32)])  3.56 us
  transfers between devices with their start and end apart: 14, of which 6 were waited for; matrix products, arithmetic and copies ran while one was open for 1% of the time, Pallas kernels for 28%

profile of v8, /device:TPU:1, one launch (start us, length us, event | category | flops | bytes accessed | tf_op | source)
XLA Modules:
  0.0 69.3 jit_solution(7305533871032316782)
XLA Ops:
  0.0 2.5 %collective-permute-start.1 = (bf16[1,16,576]{2,1,0:T(8,128)(2,1)}, bf16[1,16,576]{2,1,0:T(8,128)(2,1)S(1)}, u32[]{:S(2)}, u32[]{:S(2)}) collective-permute-start(bf16[1,16,576]{2,1,0:T(8,128)(2,1)} %bitcast.3), channel_id=1, source_target_pairs={{112,0},{120,8},{0,16},{8,24},{16,32},{24,40},{32,48},{40,56},{48,... | collective-permute-start | bytes 55304 | tf_op jit(solution)/shard_map/ppermute | solution.py:33
  2.5 3.9 %collective-permute-start = (bf16[1,16,576]{2,1,0:T(8,128)(2,1)}, bf16[1,16,576]{2,1,0:T(8,128)(2,1)S(1)}, u32[]{:S(2)}, u32[]{:S(2)}) collective-permute-start(bf16[1,16,576]{2,1,0:T(8,128)(2,1)} %bitcast.4), channel_id=1, source_target_pairs={{16,0},{24,8},{32,16},{40,24},{48,32},{56,40},{64,48},{72,56},{80,... | collective-permute-start | bytes 55304 | tf_op jit(solution)/shard_map/ppermute | solution.py:33
  6.4 0.8 %constant_dynamic-update-slice_fusion.10 = (bf16[32,16,576]{2,1,0:T(8,128)(2,1)S(1)}, bf16[8,16,576]{2,1,0:T(8,128)(2,1)S(1)}) fusion(bf16[16,576]{1,0:T(8,128)(2,1)} %param.8), kind=kLoop, calls=%fused_computation.13 | loop fusion | bytes 59392
  7.2 0.6 collective-permute-done.1
  7.8 0.0 collective-permute-done
  7.8 0.7 %pad_maximum_fusion = bf16[3,16,576]{2,1,0:T(8,128)(2,1)S(1)} fusion(bf16[1,16,576]{2,1,0:T(8,128)(2,1)S(1)} %collective-permute-done.1, bf16[1,16,576]{2,1,0:T(8,128)(2,1)S(1)} %collective-permute-done, bf16[1,16,576]{2,1,0:T(8,128)(2,1)} %bitcast.5), kind=kLoop, calls=%fused_computation | loop fusion | flops 55296 | bytes 110592 | tf_op jit(solution)/shard_map/concatenate | solution.py:44
  8.5 4.4 %collective-permute-start.3 = (bf16[3,16,576]{2,1,0:T(8,128)(2,1)S(1)}, bf16[3,16,576]{2,1,0:T(8,128)(2,1)S(1)}, u32[]{:S(2)}, u32[]{:S(2)}) collective-permute-start(bf16[3,16,576]{2,1,0:T(8,128)(2,1)S(1)} %pad_maximum_fusion), channel_id=1, source_target_pairs={{80,0},{88,8},{96,16},{104,24},{112,32},{120,40},{0,48},{8,56},{16... | collective-permute-start | bytes 165896 | tf_op jit(solution)/shard_map/ppermute | solution.py:33
  12.9 0.2 collective-permute-start.2
  13.1 4.7 %collective-permute-done.2 = bf16[3,16,576]{2,1,0:T(8,128)(2,1)S(1)} collective-permute-done((bf16[3,16,576]{2,1,0:T(8,128)(2,1)S(1)}, bf16[3,16,576]{2,1,0:T(8,128)(2,1)S(1)}, u32[]{:S(2)}, u32[]{:S(2)}) %collective-permute-start.2) | collective-permute-done | bytes 55328 | tf_op jit(solution)/shard_map/ppermute | solution.py:33
  17.8 0.0 copy-start.4
  17.8 2.8 %collective-permute-start.6 = (bf16[8,16,576]{2,1,0:T(8,128)(2,1)S(1)}, bf16[8,16,576]{2,1,0:T(8,128)(2,1)S(1)}, u32[]{:S(2)}, u32[]{:S(2)}) collective-permute-start(bf16[8,16,576]{2,1,0:T(8,128)(2,1)S(1)} %get-tuple-element.44), channel_id=1, source_target_pairs={{2,0},{12,8},{18,16},{28,24},{34,32},{44,40},{50,48},{60,56},{66,6... | collective-permute-start | bytes 442376 | tf_op jit(solution)/shard_map/ppermute | solution.py:33
  20.7 0.3 collective-permute-start.5
  21.0 2.4 %collective-permute-start.4 = (bf16[8,16,576]{2,1,0:T(8,128)(2,1)S(1)}, bf16[8,16,576]{2,1,0:T(8,128)(2,1)S(1)}, u32[]{:S(2)}, u32[]{:S(2)}) collective-permute-start(bf16[8,16,576]{2,1,0:T(8,128)(2,1)S(1)} %get-tuple-element.44), channel_id=1, source_target_pairs={{1,0},{136,8},{17,16},{152,24},{33,32},{168,40},{49,48},{184,56},{... | collective-permute-start | bytes 442376 | tf_op jit(solution)/shard_map/ppermute | solution.py:33
  23.3 1.6 %copy-done.1 = bf16[16,128,512]{2,1,0:T(8,128)(2,1)S(1)} copy-done((bf16[16,128,512]{2,1,0:T(8,128)(2,1)S(1)}, bf16[16,128,512]{2,1,0:T(8,128)(2,1)}, u32[]{:S(2)}) %copy-start.1) | copy-done | bytes 2097176
  24.9 1.0 %copy-done.2 = bf16[128,2048]{1,0:T(8,128)(2,1)S(1)} copy-done((bf16[128,2048]{1,0:T(8,128)(2,1)S(1)}, bf16[128,2048]{1,0:T(8,128)(2,1)}, u32[]{:S(2)}) %copy-start.2) | copy-done | bytes 524312
  26.0 0.9 %copy-done.3 = bf16[128,1024]{1,0:T(8,128)(2,1)S(1)} copy-done((bf16[128,1024]{1,0:T(8,128)(2,1)S(1)}, bf16[128,1024]{1,0:T(8,128)(2,1)}, u32[]{:S(2)}) %copy-start.3) | copy-done | bytes 262168
  26.9 0.8 %make_queries.1.query_ref = bf16[2,1024,576]{2,1,0:T(8,128)(2,1)S(1)} custom-call(bf16[128,2048]{1,0:T(8,128)(2,1)S(1)} %copy-done.2, bf16[128,1024]{1,0:T(8,128)(2,1)S(1)} %copy-done.3, bf16[16,128,512]{2,1,0:T(8,128)(2,1)S(1)} %copy-done.1), custom_call_target="tpu_custom_call" | custom-call | flops 268435456 | bytes 6291456 | tf_op jit(solution)/shard_map/make_queries/pallas_call | solution.py:80
  27.7 0.0 collective-permute-done.6
  27.7 0.0 collective-permute-done.4
  27.8 4.7 %collective-permute-start.10 = (bf16[32,16,576]{2,1,0:T(8,128)(2,1)S(1)}, bf16[32,16,576]{2,1,0:T(8,128)(2,1)S(1)}, u32[]{:S(2)}, u32[]{:S(2)}) collective-permute-start(bf16[32,16,576]{2,1,0:T(8,128)(2,1)S(1)} %constant_dynamic-update-slice_fusion.4.refs_0_), channel_id=1, source_target_pairs={{0,8},{8,0},{16,24},{24,16},{32,40},{40,32},{48,56},{56,48},{64,72... | collective-permute-start | bytes 1769480 | tf_op jit(solution)/shard_map/ppermute | solution.py:37
  32.5 2.7 %collective-permute-start.8 = (bf16[32,16,576]{2,1,0:T(8,128)(2,1)S(1)}, bf16[32,16,576]{2,1,0:T(8,128)(2,1)S(1)}, u32[]{:S(2)}, u32[]{:S(2)}) collective-permute-start(bf16[32,16,576]{2,1,0:T(8,128)(2,1)S(1)} %constant_dynamic-update-slice_fusion.4.refs_0_), channel_id=1, source_target_pairs={{128,0},{9,8},{144,16},{25,24},{160,32},{41,40},{176,48},{57,56},{... | collective-permute-start | bytes 1769480 | tf_op jit(solution)/shard_map/ppermute | solution.py:33
  35.2 7.2 %absorb_0.1 = (f32[2048,512]{1,0:T(8,128)S(1)}, f32[2048,128]{1,0:T(8,128)S(1)}, f32[2048,128]{1,0:T(8,128)S(1)}) custom-call(s32[64]{0:T(128)S(1)} %copy-done.4, bf16[2,1024,576]{2,1,0:T(8,128)(2,1)S(1)} %make_queries.1.query_ref, bf16[32,16,576]{2,1,0:T(8,128)(2,1)S(1)} %constant_dynamic-update-slice_fusion.4.refs_0_, ...), custom_call_target="tpu_custom_call" | custom-call | flops 2281701376 | bytes 10485760 | tf_op jit(solution)/shard_map/absorb_0/pallas_call | solution.py:254
  42.4 1.0 %collective-permute-done.9.refs_2_ = bf16[32,16,576]{2,1,0:T(8,128)(2,1)S(1)} collective-permute-done((bf16[32,16,576]{2,1,0:T(8,128)(2,1)S(1)}, bf16[32,16,576]{2,1,0:T(8,128)(2,1)S(1)}, u32[]{:S(2)}, u32[]{:S(2)}) %collective-permute-start.9) | collective-permute-done | bytes 589856 | tf_op jit(solution)/shard_map/ppermute | solution.py:33
  43.5 1.2 %collective-permute-start.11 = (bf16[32,16,576]{2,1,0:T(8,128)(2,1)S(1)}, bf16[32,16,576]{2,1,0:T(8,128)(2,1)S(1)}, u32[]{:S(2)}, u32[]{:S(2)}) collective-permute-start(bf16[32,16,576]{2,1,0:T(8,128)(2,1)S(1)} %collective-permute-done.8.refs_0_), channel_id=1, source_target_pairs={{0,8},{8,0},{16,24},{24,16},{32,40},{40,32},{48,56},{56,48},{64,72... | collective-permute-start | bytes 1769480 | tf_op jit(solution)/shard_map/ppermute | solution.py:37
  44.7 0.0 collective-permute-start.12
  44.7 0.8 %collective-permute-start.7 = (bf16[32,16,576]{2,1,0:T(8,128)(2,1)S(1)}, bf16[32,16,576]{2,1,0:T(8,128)(2,1)S(1)}, u32[]{:S(2)}, u32[]{:S(2)}) collective-permute-start(bf16[32,16,576]{2,1,0:T(8,128)(2,1)S(1)} %constant_dynamic-update-slice_fusion.4.refs_0_), channel_id=1, source_target_pairs={{4,0},{10,8},{20,16},{26,24},{36,32},{42,40},{52,48},{58,56},{68,6... | collective-permute-start | bytes 1769480 | tf_op jit(solution)/shard_map/ppermute | solution.py:33
  45.5 0.9 %collective-permute-done.11.refs_1_ = bf16[32,16,576]{2,1,0:T(8,128)(2,1)S(1)} collective-permute-done((bf16[32,16,576]{2,1,0:T(8,128)(2,1)S(1)}, bf16[32,16,576]{2,1,0:T(8,128)(2,1)S(1)}, u32[]{:S(2)}, u32[]{:S(2)}) %collective-permute-start.11) | collective-permute-done | bytes 589856 | tf_op jit(solution)/shard_map/ppermute | solution.py:37
  46.4 0.9 %collective-permute-done.12.refs_3_ = bf16[32,16,576]{2,1,0:T(8,128)(2,1)S(1)} collective-permute-done((bf16[32,16,576]{2,1,0:T(8,128)(2,1)S(1)}, bf16[32,16,576]{2,1,0:T(8,128)(2,1)S(1)}, u32[]{:S(2)}, u32[]{:S(2)}) %collective-permute-start.12) | collective-permute-done | bytes 589856 | tf_op jit(solution)/shard_map/ppermute | solution.py:37
  47.3 11.5 %absorb_1.1 = (f32[2048,512]{1,0:T(8,128)S(1)}, f32[2048,128]{1,0:T(8,128)S(1)}, f32[2048,128]{1,0:T(8,128)S(1)}) custom-call(s32[64]{0:T(128)S(1)} %copy-done.4, bf16[2,1024,576]{2,1,0:T(8,128)(2,1)S(1)} %make_queries.1.query_ref, bf16[32,16,576]{2,1,0:T(8,128)(2,1)S(1)} %collective-permute-done.8.refs_0_, ...), custom_call_target="tpu_custom_call" | custom-call | flops 4563402752 | bytes 10485760 | tf_op jit(solution)/shard_map/absorb_1/pallas_call | solution.py:254
  58.8 0.7 collective-permute-start.13
  59.5 1.7 %collective-permute-done.13.refs_1_ = bf16[32,16,576]{2,1,0:T(8,128)(2,1)S(1)} collective-permute-done((bf16[32,16,576]{2,1,0:T(8,128)(2,1)S(1)}, bf16[32,16,576]{2,1,0:T(8,128)(2,1)S(1)}, u32[]{:S(2)}, u32[]{:S(2)}) %collective-permute-start.13) | collective-permute-done | bytes 589856 | tf_op jit(solution)/shard_map/ppermute | solution.py:37
  61.2 8.1 %absorb_3.1 = bf16[128,2048]{1,0:T(8,128)(2,1)} custom-call(s32[64]{0:T(128)S(1)} %copy-done.4, bf16[2,1024,576]{2,1,0:T(8,128)(2,1)S(1)} %make_queries.1.query_ref, bf16[32,16,576]{2,1,0:T(8,128)(2,1)S(1)} %collective-permute-done.7.refs_0_, bf16[32,16,576]{2,1,0:T(8,128)(2,1)S(1)} %collective-permute-done.13.refs_1_, ...), custom_call_target="tpu_custom_call" | custom-call | flops 2281701376 | bytes 10485760 | tf_op jit(solution)/shard_map/absorb_3/pallas_call | solution.py:254
  (19 shorter events, 0.2 us)
Async XLA Ops:
  0.0 7.8 %collective-permute-start.1 = (bf16[1,16,576]{2,1,0:T(8,128)(2,1)}, bf16[1,16,576]{2,1,0:T(8,128)(2,1)S(1)}, u32[]{:S(2)}, u32[]{:S(2)}) collective-permute-start(bf16[1,16,576]{2,1,0:T(8,128)(2,1)} %bitcast.3), channel_id=1, source_target_pairs={{112,0},{120,8},{0,16},{8,24},{16,32},{24,40},{32,48},{40,56},{48,... | collective-permute-start | bytes 55304 | tf_op jit(solution)/shard_map/ppermute | solution.py:33
  2.5 5.3 %collective-permute-start = (bf16[1,16,576]{2,1,0:T(8,128)(2,1)}, bf16[1,16,576]{2,1,0:T(8,128)(2,1)S(1)}, u32[]{:S(2)}, u32[]{:S(2)}) collective-permute-start(bf16[1,16,576]{2,1,0:T(8,128)(2,1)} %bitcast.4), channel_id=1, source_target_pairs={{16,0},{24,8},{32,16},{40,24},{48,32},{56,40},{64,48},{72,56},{80,... | collective-permute-start | bytes 55304 | tf_op jit(solution)/shard_map/ppermute | solution.py:33
  8.5 9.3 %collective-permute-start.3 = (bf16[3,16,576]{2,1,0:T(8,128)(2,1)S(1)}, bf16[3,16,576]{2,1,0:T(8,128)(2,1)S(1)}, u32[]{:S(2)}, u32[]{:S(2)}) collective-permute-start(bf16[3,16,576]{2,1,0:T(8,128)(2,1)S(1)} %pad_maximum_fusion), channel_id=1, source_target_pairs={{80,0},{88,8},{96,16},{104,24},{112,32},{120,40},{0,48},{8,56},{16... | collective-permute-start | bytes 165896 | tf_op jit(solution)/shard_map/ppermute | solution.py:33
  12.9 4.9 %collective-permute-start.2 = (bf16[3,16,576]{2,1,0:T(8,128)(2,1)S(1)}, bf16[3,16,576]{2,1,0:T(8,128)(2,1)S(1)}, u32[]{:S(2)}, u32[]{:S(2)}) collective-permute-start(bf16[3,16,576]{2,1,0:T(8,128)(2,1)S(1)} %pad_maximum_fusion), channel_id=1, source_target_pairs={{48,0},{56,8},{64,16},{72,24},{80,32},{88,40},{96,48},{104,56},{11... | collective-permute-start | bytes 165896 | tf_op jit(solution)/shard_map/ppermute | solution.py:33
  17.8 17.4 %copy-start.4 = (s32[64]{0:T(128)S(1)}, s32[64]{0:T(128)}, u32[]{:S(2)}) copy-start(s32[64]{0:T(128)} %starts_ref.5) | copy-start | bytes 772
  17.8 9.9 %collective-permute-start.6 = (bf16[8,16,576]{2,1,0:T(8,128)(2,1)S(1)}, bf16[8,16,576]{2,1,0:T(8,128)(2,1)S(1)}, u32[]{:S(2)}, u32[]{:S(2)}) collective-permute-start(bf16[8,16,576]{2,1,0:T(8,128)(2,1)S(1)} %get-tuple-element.44), channel_id=1, source_target_pairs={{2,0},{12,8},{18,16},{28,24},{34,32},{44,40},{50,48},{60,56},{66,6... | collective-permute-start | bytes 442376 | tf_op jit(solution)/shard_map/ppermute | solution.py:33
  20.7 7.0 %collective-permute-start.5 = (bf16[8,16,576]{2,1,0:T(8,128)(2,1)S(1)}, bf16[8,16,576]{2,1,0:T(8,128)(2,1)S(1)}, u32[]{:S(2)}, u32[]{:S(2)}) collective-permute-start(bf16[8,16,576]{2,1,0:T(8,128)(2,1)S(1)} %get-tuple-element.44), channel_id=1, source_target_pairs={{3,0},{140,8},{19,16},{156,24},{35,32},{172,40},{51,48},{188,56},{... | collective-permute-start | bytes 442376 | tf_op jit(solution)/shard_map/ppermute | solution.py:33
  21.0 6.7 %collective-permute-start.4 = (bf16[8,16,576]{2,1,0:T(8,128)(2,1)S(1)}, bf16[8,16,576]{2,1,0:T(8,128)(2,1)S(1)}, u32[]{:S(2)}, u32[]{:S(2)}) collective-permute-start(bf16[8,16,576]{2,1,0:T(8,128)(2,1)S(1)} %get-tuple-element.44), channel_id=1, source_target_pairs={{1,0},{136,8},{17,16},{152,24},{33,32},{168,40},{49,48},{184,56},{... | collective-permute-start | bytes 442376 | tf_op jit(solution)/shard_map/ppermute | solution.py:33
  23.3 1.6 %copy-start.1 = (bf16[16,128,512]{2,1,0:T(8,128)(2,1)S(1)}, bf16[16,128,512]{2,1,0:T(8,128)(2,1)}, u32[]{:S(2)}) copy-start(bf16[16,128,512]{2,1,0:T(8,128)(2,1)} %uk_ref.1) | copy-start | bytes 6291460
  24.9 1.0 %copy-start.2 = (bf16[128,2048]{1,0:T(8,128)(2,1)S(1)}, bf16[128,2048]{1,0:T(8,128)(2,1)}, u32[]{:S(2)}) copy-start(bf16[128,2048]{1,0:T(8,128)(2,1)} %nope_ref.1) | copy-start | bytes 1572868
  26.0 0.9 %copy-start.3 = (bf16[128,1024]{1,0:T(8,128)(2,1)S(1)}, bf16[128,1024]{1,0:T(8,128)(2,1)}, u32[]{:S(2)}) copy-start(bf16[128,1024]{1,0:T(8,128)(2,1)} %rope_ref.1) | copy-start | bytes 786436
  27.8 7.4 %collective-permute-start.10 = (bf16[32,16,576]{2,1,0:T(8,128)(2,1)S(1)}, bf16[32,16,576]{2,1,0:T(8,128)(2,1)S(1)}, u32[]{:S(2)}, u32[]{:S(2)}) collective-permute-start(bf16[32,16,576]{2,1,0:T(8,128)(2,1)S(1)} %constant_dynamic-update-slice_fusion.4.refs_0_), channel_id=1, source_target_pairs={{0,8},{8,0},{16,24},{24,16},{32,40},{40,32},{48,56},{56,48},{64,72... | collective-permute-start | bytes 1769480 | tf_op jit(solution)/shard_map/ppermute | solution.py:37
  32.5 10.9 %collective-permute-start.9 = (bf16[32,16,576]{2,1,0:T(8,128)(2,1)S(1)}, bf16[32,16,576]{2,1,0:T(8,128)(2,1)S(1)}, u32[]{:S(2)}, u32[]{:S(2)}) collective-permute-start(bf16[32,16,576]{2,1,0:T(8,128)(2,1)S(1)} %constant_dynamic-update-slice_fusion.4.refs_0_), channel_id=1, source_target_pairs={{132,0},{11,8},{148,16},{27,24},{164,32},{43,40},{180,48},{59,56},... | collective-permute-start | bytes 1769480 | tf_op jit(solution)/shard_map/ppermute | solution.py:33
  32.5 10.9 %collective-permute-start.8 = (bf16[32,16,576]{2,1,0:T(8,128)(2,1)S(1)}, bf16[32,16,576]{2,1,0:T(8,128)(2,1)S(1)}, u32[]{:S(2)}, u32[]{:S(2)}) collective-permute-start(bf16[32,16,576]{2,1,0:T(8,128)(2,1)S(1)} %constant_dynamic-update-slice_fusion.4.refs_0_), channel_id=1, source_target_pairs={{128,0},{9,8},{144,16},{25,24},{160,32},{41,40},{176,48},{57,56},{... | collective-permute-start | bytes 1769480 | tf_op jit(solution)/shard_map/ppermute | solution.py:33
  43.5 17.8 %copy-start = (bf16[16,512,128]{2,1,0:T(8,128)(2,1)S(1)}, bf16[16,512,128]{2,1,0:T(8,128)(2,1)}, u32[]{:S(2)}) copy-start(bf16[16,512,128]{2,1,0:T(8,128)(2,1)} %refs_5_.1) | copy-start | bytes 6291460
  43.5 2.9 %collective-permute-start.11 = (bf16[32,16,576]{2,1,0:T(8,128)(2,1)S(1)}, bf16[32,16,576]{2,1,0:T(8,128)(2,1)S(1)}, u32[]{:S(2)}, u32[]{:S(2)}) collective-permute-start(bf16[32,16,576]{2,1,0:T(8,128)(2,1)S(1)} %collective-permute-done.8.refs_0_), channel_id=1, source_target_pairs={{0,8},{8,0},{16,24},{24,16},{32,40},{40,32},{48,56},{56,48},{64,72... | collective-permute-start | bytes 1769480 | tf_op jit(solution)/shard_map/ppermute | solution.py:37
  44.7 2.7 %collective-permute-start.12 = (bf16[32,16,576]{2,1,0:T(8,128)(2,1)S(1)}, bf16[32,16,576]{2,1,0:T(8,128)(2,1)S(1)}, u32[]{:S(2)}, u32[]{:S(2)}) collective-permute-start(bf16[32,16,576]{2,1,0:T(8,128)(2,1)S(1)} %collective-permute-done.9.refs_2_), channel_id=1, source_target_pairs={{0,8},{8,0},{16,24},{24,16},{32,40},{40,32},{48,56},{56,48},{64,72... | collective-permute-start | bytes 1769480 | tf_op jit(solution)/shard_map/ppermute | solution.py:37
  44.7 14.2 %collective-permute-start.7 = (bf16[32,16,576]{2,1,0:T(8,128)(2,1)S(1)}, bf16[32,16,576]{2,1,0:T(8,128)(2,1)S(1)}, u32[]{:S(2)}, u32[]{:S(2)}) collective-permute-start(bf16[32,16,576]{2,1,0:T(8,128)(2,1)S(1)} %constant_dynamic-update-slice_fusion.4.refs_0_), channel_id=1, source_target_pairs={{4,0},{10,8},{20,16},{26,24},{36,32},{42,40},{52,48},{58,56},{68,6... | collective-permute-start | bytes 1769480 | tf_op jit(solution)/shard_map/ppermute | solution.py:33
  58.8 2.4 %collective-permute-start.13 = (bf16[32,16,576]{2,1,0:T(8,128)(2,1)S(1)}, bf16[32,16,576]{2,1,0:T(8,128)(2,1)S(1)}, u32[]{:S(2)}, u32[]{:S(2)}) collective-permute-start(bf16[32,16,576]{2,1,0:T(8,128)(2,1)S(1)} %collective-permute-done.7.refs_0_), channel_id=1, source_target_pairs={{0,8},{8,0},{16,24},{24,16},{32,40},{40,32},{48,56},{56,48},{64,72... | collective-permute-start | bytes 1769480 | tf_op jit(solution)/shard_map/ppermute | solution.py:37

commit v9 on v8

--- a/solution.py
+++ b/solution.py
@@ -57,6 +57,12 @@
     nope_width = uk_ref.shape[1]
     rope_width = rope_ref.shape[1] // uk_ref.shape[0]
     block = nope_ref.shape[0] // 2
+    rest = jnp.zeros((block, query_ref.shape[2] - latent_width - rope_ref.shape[1] // uk_ref.shape[0]), jnp.bfloat16)
+    lane = lax.broadcasted_iota(jnp.int32, (PIECE, 128), 1)
+    read = jnp.where(lane == 64, float(block), jnp.where(lane == 65, 1.0, 0.0))
+    for half in range(2):
+        query_ref[half, :PIECE, :latent_width] = jnp.zeros((PIECE, latent_width), jnp.bfloat16)
+        query_ref[half, :PIECE, latent_width:] = read.astype(jnp.bfloat16)
     for head in range(uk_ref.shape[0]):
         lat = jnp.dot(
             nope_ref[:, head * nope_width : (head + 1) * nope_width],
@@ -66,22 +72,22 @@
         rope = rope_ref[:, head * rope_width : (head + 1) * rope_width]
         for half in range(2):
             rows = slice(half * block, (half + 1) * block)
-            to = slice(head * block, (head + 1) * block)
+            to = slice(PIECE + head * block, PIECE + (head + 1) * block)
             query_ref[half, to, :latent_width] = lat[rows]
-            query_ref[half, to, latent_width:] = rope[rows]
+            query_ref[half, to, latent_width:] = jnp.concatenate([rope[rows], rest], axis=1)
 
 
 def make_queries(q_nope, q_rope, w_uk):
     rows = q_nope.shape[0]
     heads, nope_width, latent_width = w_uk.shape
     rope_width = q_rope.shape[1] // heads
-    width = latent_width + rope_width
+    width = latent_width + 2 * rope_width
     vmem = pl.BlockSpec(memory_space=pltpu.VMEM)
     return pl.pallas_call(
         query_kernel,
         in_specs=[vmem] * 3,
         out_specs=vmem,
-        out_shape=jax.ShapeDtypeStruct((2, heads * rows // 2, width), jnp.bfloat16),
+        out_shape=jax.ShapeDtypeStruct((2, PIECE + heads * rows // 2, width), jnp.bfloat16),
         compiler_params=pltpu.CompilerParams(vmem_limit_bytes=12 * 2**20),
         cost_estimate=pl.CostEstimate(
             flops=2 * rows * heads * nope_width * latent_width,
@@ -97,14 +103,14 @@
     state_in = refs[: 0 if lasts[0] == 0 else 3]
     refs = refs[len(state_in) :]
     if finish:
-        uv_ref, out_ref, keys, marks, even, odd, acc, top, total = refs
+        uv_ref, out_ref, keys, even, odd, acc, top, total = refs
     else:
-        acc, top, total, keys, marks, even, odd = refs
+        acc, top, total, keys, even, odd = refs
     ctx, head_group = lax.axis_index("ctx"), lax.axis_index("head")
     x = (head_group >> 2) * 2 + (ctx >> 4)
     y, z, core = head_group & 3, (ctx >> 1) & 7, ctx & 1
-    rows = query_ref.shape[1]
-    block, width = 4 * PIECE, query_ref.shape[2]
+    rows = query_ref.shape[1] - PIECE
+    block, width = 4 * PIECE, piece_refs[0].shape[2]
     latent_width = acc.shape[1]
     factor = math.log2(math.e) / math.sqrt(NOPE + width - latent_width)
     low, high = starts_ref[2 * ctx], starts_ref[2 * ctx + 1]
@@ -132,8 +138,8 @@
     for _, _, start, _ in pieces:
         below = below + jnp.where(start <= low, 1, 0)
         within = within + jnp.where(start <= high, 1, 0)
-    lane = lax.broadcasted_iota(jnp.int32, (PIECE, 128), 1)
-    row = lax.broadcasted_iota(jnp.int32, (PIECE, 128), 0)
+    lane = lax.broadcasted_iota(jnp.int32, (PIECE, 64), 1)
+    row = lax.broadcasted_iota(jnp.int32, (PIECE, 64), 0)
     unit, offset = jnp.where(lane == 0, 1, 0), jnp.where(lane == 1, row, 0)
     beside = jnp.where(lane == 1, 1, 0)
     nexts = [jnp.int32(0), below, within]
@@ -144,11 +150,10 @@
         nexts[1] = nexts[1] + jnp.where(second & (start > low), 1, 0)
         nexts[2] = nexts[2] + jnp.where(second, 0, 1)
         to = pl.ds(pl.multiple_of(to * PIECE, PIECE), PIECE)
-        keys[to, :] = ref[at]
+        keys[to, :width] = ref[at]
         mark = unit * (start >> 6) + offset + beside * shift
-        marks[to, :] = mark.astype(jnp.float32).astype(jnp.bfloat16)
-
-    read = jnp.where(lane == 0, float(block), jnp.where(lane == 1, 1.0, 0.0)).astype(jnp.bfloat16)
+        keys[to, width:] = mark.astype(jnp.float32).astype(jnp.bfloat16)
+
     query_row = lax.broadcasted_iota(jnp.int32, (block, TILE), 0).astype(jnp.float32)
     per_tile = TILE // PIECE
     tiles_low = (below + per_tile - 1) >> 4
@@ -163,20 +168,15 @@
 
     def score(buffer, index):
         half, at, start = place(index)
-        position = lax.dot_general(
-            read,
-            marks[pl.ds(at, TILE), :],
-            (((1,), (1,)), ((), ())),
-            preferred_element_type=jnp.float32,
-        )
-        position = jnp.broadcast_to(position[:1, :], (block, TILE))
-        allowed = position - start.astype(jnp.float32) <= query_row
         s = lax.dot_general(
             query_ref[half],
             keys[pl.ds(at, TILE), :],
             (((1,), (1,)), ((), ())),
             preferred_element_type=jnp.float32,
         )
+        position = jnp.broadcast_to(s[:1, :], (block, TILE))
+        allowed = position - start.astype(jnp.float32) <= query_row
+        s = s[PIECE:, :]
         s = jnp.where(allowed[None], s.reshape(rows // block, block, TILE), -1e30)
         buffer[...] = s.reshape(rows, TILE)
 
@@ -234,13 +234,12 @@
 
 def absorb(lasts, finish, block_start, query, pieces, state, w_uv):
     heads, latent_width, value_width = w_uv.shape
-    rows, width = query.shape[1:]
+    rows, width = query.shape[1] - PIECE, query.shape[2]
     count = sum(p.shape[0] * p.shape[1] for p in pieces)
     vmem = pl.BlockSpec(memory_space=pltpu.VMEM)
     state_shapes = [(2 * rows, latent_width), (2 * rows, 128), (2 * rows, 128)]
     scratch = [
         pltpu.VMEM((count, width), jnp.bfloat16),
-        pltpu.VMEM((count, 128), jnp.bfloat16),
         pltpu.VMEM((rows, TILE), jnp.float32),
         pltpu.VMEM((rows, TILE), jnp.float32),
     ]

time: 70 us -> 71 us (1.014)
  the two profiles are of different devices: /device:TPU:1 before, /device:TPU:7 now
where the time goes in v9:
time: 71 us; the launch traced here: 69.8 us
  Pallas kernels  27.8 us (39%)
  starting transfers between devices  24.3 us (34%)
  waiting for transfers between devices  12.5 us (18%)
  local copies, waits for them, and re-layouts  4.48 us (6%)
  other arithmetic  0.74 us (1%)
    pallas_call x3, Pallas kernels, absorb(): pl.pallas_call(functools.partial(absorb_kernel, lasts, finish), in_specs=...  27.1 us
    ppermute x10, starting transfers between devices, from_offset(): return lax.ppermute(value, BOTH, pairs)  16.5 us
    ppermute x10, waiting for transfers between devices, from_offset(): return lax.ppermute(value, BOTH, pairs)  8.78 us
    ppermute x4, starting transfers between devices, other_core(): return lax.ppermute(value, 'ctx', [(i, i ^ 1) for i in range(32)])  7.74 us
    unnamed x17, local copies, waits for them, and re-layouts  4.46 us
    ppermute x4, waiting for transfers between devices, other_core(): return lax.ppermute(value, 'ctx', [(i, i ^ 1) for i in range(32)])  3.71 us
  transfers between devices with their start and end apart: 14, of which 7 were waited for; matrix products, arithmetic and copies ran while one was open for 1% of the time, Pallas kernels for 27%

profile of v9, /device:TPU:7, one launch (start us, length us, event | category | flops | bytes accessed | tf_op | source)
XLA Modules:
  0.0 69.8 jit_solution(1720464116808289068)
XLA Ops:
  0.0 1.6 %collective-permute-start.1 = (bf16[1,16,576]{2,1,0:T(8,128)(2,1)}, bf16[1,16,576]{2,1,0:T(8,128)(2,1)S(1)}, u32[]{:S(2)}, u32[]{:S(2)}) collective-permute-start(bf16[1,16,576]{2,1,0:T(8,128)(2,1)} %bitcast.3), channel_id=1, source_target_pairs={{112,0},{120,8},{0,16},{8,24},{16,32},{24,40},{32,48},{40,56},{48,... | collective-permute-start | bytes 55304 | tf_op jit(solution)/shard_map/ppermute | solution.py:33
  1.6 3.9 %collective-permute-start = (bf16[1,16,576]{2,1,0:T(8,128)(2,1)}, bf16[1,16,576]{2,1,0:T(8,128)(2,1)S(1)}, u32[]{:S(2)}, u32[]{:S(2)}) collective-permute-start(bf16[1,16,576]{2,1,0:T(8,128)(2,1)} %bitcast.4), channel_id=1, source_target_pairs={{16,0},{24,8},{32,16},{40,24},{48,32},{56,40},{64,48},{72,56},{80,... | collective-permute-start | bytes 55304 | tf_op jit(solution)/shard_map/ppermute | solution.py:33
  5.6 0.8 %constant_dynamic-update-slice_fusion.10 = (bf16[32,16,576]{2,1,0:T(8,128)(2,1)S(1)}, bf16[8,16,576]{2,1,0:T(8,128)(2,1)S(1)}) fusion(bf16[16,576]{1,0:T(8,128)(2,1)} %param.8), kind=kLoop, calls=%fused_computation.13 | loop fusion | bytes 59392
  6.3 0.6 collective-permute-done.1
  7.0 0.0 collective-permute-done
  7.0 0.7 %pad_maximum_fusion = bf16[3,16,576]{2,1,0:T(8,128)(2,1)S(1)} fusion(bf16[1,16,576]{2,1,0:T(8,128)(2,1)S(1)} %collective-permute-done.1, bf16[1,16,576]{2,1,0:T(8,128)(2,1)S(1)} %collective-permute-done, bf16[1,16,576]{2,1,0:T(8,128)(2,1)} %bitcast.5), kind=kLoop, calls=%fused_computation | loop fusion | flops 55296 | bytes 110592 | tf_op jit(solution)/shard_map/concatenate | solution.py:44
  7.7 4.4 %collective-permute-start.3 = (bf16[3,16,576]{2,1,0:T(8,128)(2,1)S(1)}, bf16[3,16,576]{2,1,0:T(8,128)(2,1)S(1)}, u32[]{:S(2)}, u32[]{:S(2)}) collective-permute-start(bf16[3,16,576]{2,1,0:T(8,128)(2,1)S(1)} %pad_maximum_fusion), channel_id=1, source_target_pairs={{80,0},{88,8},{96,16},{104,24},{112,32},{120,40},{0,48},{8,56},{16... | collective-permute-start | bytes 165896 | tf_op jit(solution)/shard_map/ppermute | solution.py:33
  12.1 0.2 collective-permute-start.2
  12.3 4.7 %collective-permute-done.2 = bf16[3,16,576]{2,1,0:T(8,128)(2,1)S(1)} collective-permute-done((bf16[3,16,576]{2,1,0:T(8,128)(2,1)S(1)}, bf16[3,16,576]{2,1,0:T(8,128)(2,1)S(1)}, u32[]{:S(2)}, u32[]{:S(2)}) %collective-permute-start.2) | collective-permute-done | bytes 55328 | tf_op jit(solution)/shard_map/ppermute | solution.py:33
  17.0 0.0 copy-start.4
  17.0 1.2 %collective-permute-start.6 = (bf16[8,16,576]{2,1,0:T(8,128)(2,1)S(1)}, bf16[8,16,576]{2,1,0:T(8,128)(2,1)S(1)}, u32[]{:S(2)}, u32[]{:S(2)}) collective-permute-start(bf16[8,16,576]{2,1,0:T(8,128)(2,1)S(1)} %get-tuple-element.44), channel_id=1, source_target_pairs={{2,0},{12,8},{18,16},{28,24},{34,32},{44,40},{50,48},{60,56},{66,6... | collective-permute-start | bytes 442376 | tf_op jit(solution)/shard_map/ppermute | solution.py:33
  18.2 1.8 %collective-permute-start.5 = (bf16[8,16,576]{2,1,0:T(8,128)(2,1)S(1)}, bf16[8,16,576]{2,1,0:T(8,128)(2,1)S(1)}, u32[]{:S(2)}, u32[]{:S(2)}) collective-permute-start(bf16[8,16,576]{2,1,0:T(8,128)(2,1)S(1)} %get-tuple-element.44), channel_id=1, source_target_pairs={{3,0},{140,8},{19,16},{156,24},{35,32},{172,40},{51,48},{188,56},{... | collective-permute-start | bytes 442376 | tf_op jit(solution)/shard_map/ppermute | solution.py:33
  20.0 0.0 collective-permute-start.4
  20.0 1.6 %copy-done = bf16[16,128,512]{2,1,0:T(8,128)(2,1)S(1)} copy-done((bf16[16,128,512]{2,1,0:T(8,128)(2,1)S(1)}, bf16[16,128,512]{2,1,0:T(8,128)(2,1)}, u32[]{:S(2)}) %copy-start) | copy-done | bytes 2097176
  21.6 1.0 %copy-done.2 = bf16[128,2048]{1,0:T(8,128)(2,1)S(1)} copy-done((bf16[128,2048]{1,0:T(8,128)(2,1)S(1)}, bf16[128,2048]{1,0:T(8,128)(2,1)}, u32[]{:S(2)}) %copy-start.2) | copy-done | bytes 524312
  22.7 0.9 %copy-done.3 = bf16[128,1024]{1,0:T(8,128)(2,1)S(1)} copy-done((bf16[128,1024]{1,0:T(8,128)(2,1)S(1)}, bf16[128,1024]{1,0:T(8,128)(2,1)}, u32[]{:S(2)}) %copy-start.3) | copy-done | bytes 262168
  23.6 0.7 %make_queries.1.query_ref = bf16[2,1040,640]{2,1,0:T(8,128)(2,1)S(1)} custom-call(bf16[128,2048]{1,0:T(8,128)(2,1)S(1)} %copy-done.2, bf16[128,1024]{1,0:T(8,128)(2,1)S(1)} %copy-done.3, bf16[16,128,512]{2,1,0:T(8,128)(2,1)S(1)} %copy-done), custom_call_target="tpu_custom_call" | custom-call | flops 268435456 | bytes 6291456 | tf_op jit(solution)/shard_map/make_queries/pallas_call | solution.py:86
  24.3 0.0 collective-permute-done.6
  24.3 1.4 %collective-permute-done.4 = bf16[8,16,576]{2,1,0:T(8,128)(2,1)S(1)} collective-permute-done((bf16[8,16,576]{2,1,0:T(8,128)(2,1)S(1)}, bf16[8,16,576]{2,1,0:T(8,128)(2,1)S(1)}, u32[]{:S(2)}, u32[]{:S(2)}) %collective-permute-start.4) | collective-permute-done | bytes 147488 | tf_op jit(solution)/shard_map/ppermute | solution.py:33
  25.8 5.8 %collective-permute-start.10 = (bf16[32,16,576]{2,1,0:T(8,128)(2,1)S(1)}, bf16[32,16,576]{2,1,0:T(8,128)(2,1)S(1)}, u32[]{:S(2)}, u32[]{:S(2)}) collective-permute-start(bf16[32,16,576]{2,1,0:T(8,128)(2,1)S(1)} %constant_dynamic-update-slice_fusion.4.refs_0_), channel_id=1, source_target_pairs={{0,8},{8,0},{16,24},{24,16},{32,40},{40,32},{48,56},{56,48},{64,72... | collective-permute-start | bytes 1769480 | tf_op jit(solution)/shard_map/ppermute | solution.py:37
  31.6 2.7 %collective-permute-start.8 = (bf16[32,16,576]{2,1,0:T(8,128)(2,1)S(1)}, bf16[32,16,576]{2,1,0:T(8,128)(2,1)S(1)}, u32[]{:S(2)}, u32[]{:S(2)}) collective-permute-start(bf16[32,16,576]{2,1,0:T(8,128)(2,1)S(1)} %constant_dynamic-update-slice_fusion.4.refs_0_), channel_id=1, source_target_pairs={{128,0},{9,8},{144,16},{25,24},{160,32},{41,40},{176,48},{57,56},{... | collective-permute-start | bytes 1769480 | tf_op jit(solution)/shard_map/ppermute | solution.py:33
  34.3 6.1 %absorb_0.1 = (f32[2048,512]{1,0:T(8,128)S(1)}, f32[2048,128]{1,0:T(8,128)S(1)}, f32[2048,128]{1,0:T(8,128)S(1)}) custom-call(s32[64]{0:T(128)S(1)} %copy-done.4, bf16[2,1040,640]{2,1,0:T(8,128)(2,1)S(1)} %make_queries.1.query_ref, bf16[32,16,576]{2,1,0:T(8,128)(2,1)S(1)} %constant_dynamic-update-slice_fusion.4.refs_0_, ...), custom_call_target="tpu_custom_call" | custom-call | flops 2415919104 | bytes 10485760 | tf_op jit(solution)/shard_map/absorb_0/pallas_call | solution.py:253
  40.4 2.1 %collective-permute-done.9.refs_2_ = bf16[32,16,576]{2,1,0:T(8,128)(2,1)S(1)} collective-permute-done((bf16[32,16,576]{2,1,0:T(8,128)(2,1)S(1)}, bf16[32,16,576]{2,1,0:T(8,128)(2,1)S(1)}, u32[]{:S(2)}, u32[]{:S(2)}) %collective-permute-start.9) | collective-permute-done | bytes 589856 | tf_op jit(solution)/shard_map/ppermute | solution.py:33
  42.5 1.4 %collective-permute-start.11 = (bf16[32,16,576]{2,1,0:T(8,128)(2,1)S(1)}, bf16[32,16,576]{2,1,0:T(8,128)(2,1)S(1)}, u32[]{:S(2)}, u32[]{:S(2)}) collective-permute-start(bf16[32,16,576]{2,1,0:T(8,128)(2,1)S(1)} %collective-permute-done.8.refs_0_), channel_id=1, source_target_pairs={{0,8},{8,0},{16,24},{24,16},{32,40},{40,32},{48,56},{56,48},{64,72... | collective-permute-start | bytes 1769480 | tf_op jit(solution)/shard_map/ppermute | solution.py:37
  44.0 0.0 collective-permute-start.12
  44.0 0.7 collective-permute-start.7
  44.7 1.0 %collective-permute-done.11.refs_1_ = bf16[32,16,576]{2,1,0:T(8,128)(2,1)S(1)} collective-permute-done((bf16[32,16,576]{2,1,0:T(8,128)(2,1)S(1)}, bf16[32,16,576]{2,1,0:T(8,128)(2,1)S(1)}, u32[]{:S(2)}, u32[]{:S(2)}) %collective-permute-start.11) | collective-permute-done | bytes 589856 | tf_op jit(solution)/shard_map/ppermute | solution.py:37
  45.7 0.9 %collective-permute-done.12.refs_3_ = bf16[32,16,576]{2,1,0:T(8,128)(2,1)S(1)} collective-permute-done((bf16[32,16,576]{2,1,0:T(8,128)(2,1)S(1)}, bf16[32,16,576]{2,1,0:T(8,128)(2,1)S(1)}, u32[]{:S(2)}, u32[]{:S(2)}) %collective-permute-start.12) | collective-permute-done | bytes 589856 | tf_op jit(solution)/shard_map/ppermute | solution.py:37
  46.6 11.7 %absorb_1.1 = (f32[2048,512]{1,0:T(8,128)S(1)}, f32[2048,128]{1,0:T(8,128)S(1)}, f32[2048,128]{1,0:T(8,128)S(1)}) custom-call(s32[64]{0:T(128)S(1)} %copy-done.4, bf16[2,1040,640]{2,1,0:T(8,128)(2,1)S(1)} %make_queries.1.query_ref, bf16[32,16,576]{2,1,0:T(8,128)(2,1)S(1)} %collective-permute-done.8.refs_0_, ...), custom_call_target="tpu_custom_call" | custom-call | flops 4831838208 | bytes 10485760 | tf_op jit(solution)/shard_map/absorb_1/pallas_call | solution.py:253
  58.4 0.5 collective-permute-start.13
  58.9 1.7 %collective-permute-done.13.refs_1_ = bf16[32,16,576]{2,1,0:T(8,128)(2,1)S(1)} collective-permute-done((bf16[32,16,576]{2,1,0:T(8,128)(2,1)S(1)}, bf16[32,16,576]{2,1,0:T(8,128)(2,1)S(1)}, u32[]{:S(2)}, u32[]{:S(2)}) %collective-permute-start.13) | collective-permute-done | bytes 589856 | tf_op jit(solution)/shard_map/ppermute | solution.py:37
  60.6 9.2 %absorb_3.1 = bf16[128,2048]{1,0:T(8,128)(2,1)} custom-call(s32[64]{0:T(128)S(1)} %copy-done.4, bf16[2,1040,640]{2,1,0:T(8,128)(2,1)S(1)} %make_queries.1.query_ref, bf16[32,16,576]{2,1,0:T(8,128)(2,1)S(1)} %collective-permute-done.7.refs_0_, bf16[32,16,576]{2,1,0:T(8,128)(2,1)S(1)} %collective-permute-done.13.refs_1_, ...), custom_call_target="tpu_custom_call" | custom-call | flops 2415919104 | bytes 10485760 | tf_op jit(solution)/shard_map/absorb_3/pallas_call | solution.py:253
  (19 shorter events, 0.1 us)
Async XLA Ops:
  0.0 7.0 %collective-permute-start.1 = (bf16[1,16,576]{2,1,0:T(8,128)(2,1)}, bf16[1,16,576]{2,1,0:T(8,128)(2,1)S(1)}, u32[]{:S(2)}, u32[]{:S(2)}) collective-permute-start(bf16[1,16,576]{2,1,0:T(8,128)(2,1)} %bitcast.3), channel_id=1, source_target_pairs={{112,0},{120,8},{0,16},{8,24},{16,32},{24,40},{32,48},{40,56},{48,... | collective-permute-start | bytes 55304 | tf_op jit(solution)/shard_map/ppermute | solution.py:33
  1.6 5.3 %collective-permute-start = (bf16[1,16,576]{2,1,0:T(8,128)(2,1)}, bf16[1,16,576]{2,1,0:T(8,128)(2,1)S(1)}, u32[]{:S(2)}, u32[]{:S(2)}) collective-permute-start(bf16[1,16,576]{2,1,0:T(8,128)(2,1)} %bitcast.4), channel_id=1, source_target_pairs={{16,0},{24,8},{32,16},{40,24},{48,32},{56,40},{64,48},{72,56},{80,... | collective-permute-start | bytes 55304 | tf_op jit(solution)/shard_map/ppermute | solution.py:33
  7.7 9.3 %collective-permute-start.3 = (bf16[3,16,576]{2,1,0:T(8,128)(2,1)S(1)}, bf16[3,16,576]{2,1,0:T(8,128)(2,1)S(1)}, u32[]{:S(2)}, u32[]{:S(2)}) collective-permute-start(bf16[3,16,576]{2,1,0:T(8,128)(2,1)S(1)} %pad_maximum_fusion), channel_id=1, source_target_pairs={{80,0},{88,8},{96,16},{104,24},{112,32},{120,40},{0,48},{8,56},{16... | collective-permute-start | bytes 165896 | tf_op jit(solution)/shard_map/ppermute | solution.py:33
  12.1 4.9 %collective-permute-start.2 = (bf16[3,16,576]{2,1,0:T(8,128)(2,1)S(1)}, bf16[3,16,576]{2,1,0:T(8,128)(2,1)S(1)}, u32[]{:S(2)}, u32[]{:S(2)}) collective-permute-start(bf16[3,16,576]{2,1,0:T(8,128)(2,1)S(1)} %pad_maximum_fusion), channel_id=1, source_target_pairs={{48,0},{56,8},{64,16},{72,24},{80,32},{88,40},{96,48},{104,56},{11... | collective-permute-start | bytes 165896 | tf_op jit(solution)/shard_map/ppermute | solution.py:33
  17.0 17.3 %copy-start.4 = (s32[64]{0:T(128)S(1)}, s32[64]{0:T(128)}, u32[]{:S(2)}) copy-start(s32[64]{0:T(128)} %starts_ref.5) | copy-start | bytes 772
  17.0 7.3 %collective-permute-start.6 = (bf16[8,16,576]{2,1,0:T(8,128)(2,1)S(1)}, bf16[8,16,576]{2,1,0:T(8,128)(2,1)S(1)}, u32[]{:S(2)}, u32[]{:S(2)}) collective-permute-start(bf16[8,16,576]{2,1,0:T(8,128)(2,1)S(1)} %get-tuple-element.44), channel_id=1, source_target_pairs={{2,0},{12,8},{18,16},{28,24},{34,32},{44,40},{50,48},{60,56},{66,6... | collective-permute-start | bytes 442376 | tf_op jit(solution)/shard_map/ppermute | solution.py:33
  18.2 6.1 %collective-permute-start.5 = (bf16[8,16,576]{2,1,0:T(8,128)(2,1)S(1)}, bf16[8,16,576]{2,1,0:T(8,128)(2,1)S(1)}, u32[]{:S(2)}, u32[]{:S(2)}) collective-permute-start(bf16[8,16,576]{2,1,0:T(8,128)(2,1)S(1)} %get-tuple-element.44), channel_id=1, source_target_pairs={{3,0},{140,8},{19,16},{156,24},{35,32},{172,40},{51,48},{188,56},{... | collective-permute-start | bytes 442376 | tf_op jit(solution)/shard_map/ppermute | solution.py:33
  20.0 5.7 %collective-permute-start.4 = (bf16[8,16,576]{2,1,0:T(8,128)(2,1)S(1)}, bf16[8,16,576]{2,1,0:T(8,128)(2,1)S(1)}, u32[]{:S(2)}, u32[]{:S(2)}) collective-permute-start(bf16[8,16,576]{2,1,0:T(8,128)(2,1)S(1)} %get-tuple-element.44), channel_id=1, source_target_pairs={{1,0},{136,8},{17,16},{152,24},{33,32},{168,40},{49,48},{184,56},{... | collective-permute-start | bytes 442376 | tf_op jit(solution)/shard_map/ppermute | solution.py:33
  20.0 1.6 %copy-start = (bf16[16,128,512]{2,1,0:T(8,128)(2,1)S(1)}, bf16[16,128,512]{2,1,0:T(8,128)(2,1)}, u32[]{:S(2)}) copy-start(bf16[16,128,512]{2,1,0:T(8,128)(2,1)} %uk_ref.1) | copy-start | bytes 6291460
  21.6 1.0 %copy-start.2 = (bf16[128,2048]{1,0:T(8,128)(2,1)S(1)}, bf16[128,2048]{1,0:T(8,128)(2,1)}, u32[]{:S(2)}) copy-start(bf16[128,2048]{1,0:T(8,128)(2,1)} %nope_ref.1) | copy-start | bytes 1572868
  22.7 0.9 %copy-start.3 = (bf16[128,1024]{1,0:T(8,128)(2,1)S(1)}, bf16[128,1024]{1,0:T(8,128)(2,1)}, u32[]{:S(2)}) copy-start(bf16[128,1024]{1,0:T(8,128)(2,1)} %rope_ref.1) | copy-start | bytes 786436
  25.8 8.5 %collective-permute-start.10 = (bf16[32,16,576]{2,1,0:T(8,128)(2,1)S(1)}, bf16[32,16,576]{2,1,0:T(8,128)(2,1)S(1)}, u32[]{:S(2)}, u32[]{:S(2)}) collective-permute-start(bf16[32,16,576]{2,1,0:T(8,128)(2,1)S(1)} %constant_dynamic-update-slice_fusion.4.refs_0_), channel_id=1, source_target_pairs={{0,8},{8,0},{16,24},{24,16},{32,40},{40,32},{48,56},{56,48},{64,72... | collective-permute-start | bytes 1769480 | tf_op jit(solution)/shard_map/ppermute | solution.py:37
  31.6 10.9 %collective-permute-start.9 = (bf16[32,16,576]{2,1,0:T(8,128)(2,1)S(1)}, bf16[32,16,576]{2,1,0:T(8,128)(2,1)S(1)}, u32[]{:S(2)}, u32[]{:S(2)}) collective-permute-start(bf16[32,16,576]{2,1,0:T(8,128)(2,1)S(1)} %constant_dynamic-update-slice_fusion.4.refs_0_), channel_id=1, source_target_pairs={{132,0},{11,8},{148,16},{27,24},{164,32},{43,40},{180,48},{59,56},... | collective-permute-start | bytes 1769480 | tf_op jit(solution)/shard_map/ppermute | solution.py:33
  31.6 10.9 %collective-permute-start.8 = (bf16[32,16,576]{2,1,0:T(8,128)(2,1)S(1)}, bf16[32,16,576]{2,1,0:T(8,128)(2,1)S(1)}, u32[]{:S(2)}, u32[]{:S(2)}) collective-permute-start(bf16[32,16,576]{2,1,0:T(8,128)(2,1)S(1)} %constant_dynamic-update-slice_fusion.4.refs_0_), channel_id=1, source_target_pairs={{128,0},{9,8},{144,16},{25,24},{160,32},{41,40},{176,48},{57,56},{... | collective-permute-start | bytes 1769480 | tf_op jit(solution)/shard_map/ppermute | solution.py:33
  42.5 18.1 %copy-start.1 = (bf16[16,512,128]{2,1,0:T(8,128)(2,1)S(1)}, bf16[16,512,128]{2,1,0:T(8,128)(2,1)}, u32[]{:S(2)}) copy-start(bf16[16,512,128]{2,1,0:T(8,128)(2,1)} %refs_5_.1) | copy-start | bytes 6291460
  42.5 3.2 %collective-permute-start.11 = (bf16[32,16,576]{2,1,0:T(8,128)(2,1)S(1)}, bf16[32,16,576]{2,1,0:T(8,128)(2,1)S(1)}, u32[]{:S(2)}, u32[]{:S(2)}) collective-permute-start(bf16[32,16,576]{2,1,0:T(8,128)(2,1)S(1)} %collective-permute-done.8.refs_0_), channel_id=1, source_target_pairs={{0,8},{8,0},{16,24},{24,16},{32,40},{40,32},{48,56},{56,48},{64,72... | collective-permute-start | bytes 1769480 | tf_op jit(solution)/shard_map/ppermute | solution.py:37
  44.0 2.7 %collective-permute-start.12 = (bf16[32,16,576]{2,1,0:T(8,128)(2,1)S(1)}, bf16[32,16,576]{2,1,0:T(8,128)(2,1)S(1)}, u32[]{:S(2)}, u32[]{:S(2)}) collective-permute-start(bf16[32,16,576]{2,1,0:T(8,128)(2,1)S(1)} %collective-permute-done.9.refs_2_), channel_id=1, source_target_pairs={{0,8},{8,0},{16,24},{24,16},{32,40},{40,32},{48,56},{56,48},{64,72... | collective-permute-start | bytes 1769480 | tf_op jit(solution)/shard_map/ppermute | solution.py:37
  44.0 14.4 %collective-permute-start.7 = (bf16[32,16,576]{2,1,0:T(8,128)(2,1)S(1)}, bf16[32,16,576]{2,1,0:T(8,128)(2,1)S(1)}, u32[]{:S(2)}, u32[]{:S(2)}) collective-permute-start(bf16[32,16,576]{2,1,0:T(8,128)(2,1)S(1)} %constant_dynamic-update-slice_fusion.4.refs_0_), channel_id=1, source_target_pairs={{4,0},{10,8},{20,16},{26,24},{36,32},{42,40},{52,48},{58,56},{68,6... | collective-permute-start | bytes 1769480 | tf_op jit(solution)/shard_map/ppermute | solution.py:33
  58.4 2.2 %collective-permute-start.13 = (bf16[32,16,576]{2,1,0:T(8,128)(2,1)S(1)}, bf16[32,16,576]{2,1,0:T(8,128)(2,1)S(1)}, u32[]{:S(2)}, u32[]{:S(2)}) collective-permute-start(bf16[32,16,576]{2,1,0:T(8,128)(2,1)S(1)} %collective-permute-done.7.refs_0_), channel_id=1, source_target_pairs={{0,8},{8,0},{16,24},{24,16},{32,40},{40,32},{48,56},{56,48},{64,72... | collective-permute-start | bytes 1769480 | tf_op jit(solution)/shard_map/ppermute | solution.py:37

commit v10 on v8

--- a/solution.py
+++ b/solution.py
@@ -225,8 +225,8 @@
             lat = []
             for half in range(2):
                 own = slice(half * rows + h * block, half * rows + (h + 1) * block)
-                whole = jnp.sum(total[own, :], axis=1, keepdims=True)
-                lat.append((acc[own, :] / whole).astype(jnp.bfloat16))
+                share = 1.0 / jnp.sum(total[own, :], axis=1, keepdims=True)
+                lat.append((acc[own, :] * share).astype(jnp.bfloat16))
             out_ref[:, h * value_width : (h + 1) * value_width] = jnp.dot(
                 jnp.concatenate(lat), uv_ref[h], preferred_element_type=jnp.float32
             ).astype(jnp.bfloat16)

time: 70 us -> 70.5 us (level)
  the two profiles are of different devices: /device:TPU:1 before, /device:TPU:5 now
where the time goes in v10:
time: 70.5 us; the launch traced here: 70 us
  Pallas kernels  27.4 us (39%)
  starting transfers between devices  25.7 us (36%)
  waiting for transfers between devices  11.5 us (16%)
  local copies, waits for them, and re-layouts  4.48 us (6%)
  other arithmetic  0.74 us (1%)
    pallas_call x3, Pallas kernels, absorb(): pl.pallas_call(functools.partial(absorb_kernel, lasts, finish), in_specs=...  26.7 us
    ppermute x10, starting transfers between devices, from_offset(): return lax.ppermute(value, BOTH, pairs)  16.1 us
    ppermute x4, starting transfers between devices, other_core(): return lax.ppermute(value, 'ctx', [(i, i ^ 1) for i in range(32)])  9.63 us
    ppermute x10, waiting for transfers between devices, from_offset(): return lax.ppermute(value, BOTH, pairs)  8.2 us
    unnamed x17, local copies, waits for them, and re-layouts  4.46 us
    ppermute x4, waiting for transfers between devices, other_core(): return lax.ppermute(value, 'ctx', [(i, i ^ 1) for i in range(32)])  3.28 us
  transfers between devices with their start and end apart: 14, of which 7 were waited for; matrix products, arithmetic and copies ran while one was open for 1% of the time, Pallas kernels for 25%

profile of v10, /device:TPU:5, one launch (start us, length us, event | category | flops | bytes accessed | tf_op | source)
XLA Modules:
  0.0 70.0 jit_solution(7305533871032316782)
XLA Ops:
  0.0 1.6 %collective-permute-start.1 = (bf16[1,16,576]{2,1,0:T(8,128)(2,1)}, bf16[1,16,576]{2,1,0:T(8,128)(2,1)S(1)}, u32[]{:S(2)}, u32[]{:S(2)}) collective-permute-start(bf16[1,16,576]{2,1,0:T(8,128)(2,1)} %bitcast.3), channel_id=1, source_target_pairs={{112,0},{120,8},{0,16},{8,24},{16,32},{24,40},{32,48},{40,56},{48,... | collective-permute-start | bytes 55304 | tf_op jit(solution)/shard_map/ppermute | solution.py:33
  1.6 3.9 %collective-permute-start = (bf16[1,16,576]{2,1,0:T(8,128)(2,1)}, bf16[1,16,576]{2,1,0:T(8,128)(2,1)S(1)}, u32[]{:S(2)}, u32[]{:S(2)}) collective-permute-start(bf16[1,16,576]{2,1,0:T(8,128)(2,1)} %bitcast.4), channel_id=1, source_target_pairs={{16,0},{24,8},{32,16},{40,24},{48,32},{56,40},{64,48},{72,56},{80,... | collective-permute-start | bytes 55304 | tf_op jit(solution)/shard_map/ppermute | solution.py:33
  5.6 0.8 %constant_dynamic-update-slice_fusion.10 = (bf16[32,16,576]{2,1,0:T(8,128)(2,1)S(1)}, bf16[8,16,576]{2,1,0:T(8,128)(2,1)S(1)}) fusion(bf16[16,576]{1,0:T(8,128)(2,1)} %param.8), kind=kLoop, calls=%fused_computation.13 | loop fusion | bytes 59392
  6.3 0.6 collective-permute-done.1
  7.0 0.0 collective-permute-done
  7.0 0.7 %pad_maximum_fusion = bf16[3,16,576]{2,1,0:T(8,128)(2,1)S(1)} fusion(bf16[1,16,576]{2,1,0:T(8,128)(2,1)S(1)} %collective-permute-done.1, bf16[1,16,576]{2,1,0:T(8,128)(2,1)S(1)} %collective-permute-done, bf16[1,16,576]{2,1,0:T(8,128)(2,1)} %bitcast.5), kind=kLoop, calls=%fused_computation | loop fusion | flops 55296 | bytes 110592 | tf_op jit(solution)/shard_map/concatenate | solution.py:44
  7.7 4.4 %collective-permute-start.3 = (bf16[3,16,576]{2,1,0:T(8,128)(2,1)S(1)}, bf16[3,16,576]{2,1,0:T(8,128)(2,1)S(1)}, u32[]{:S(2)}, u32[]{:S(2)}) collective-permute-start(bf16[3,16,576]{2,1,0:T(8,128)(2,1)S(1)} %pad_maximum_fusion), channel_id=1, source_target_pairs={{80,0},{88,8},{96,16},{104,24},{112,32},{120,40},{0,48},{8,56},{16... | collective-permute-start | bytes 165896 | tf_op jit(solution)/shard_map/ppermute | solution.py:33
  12.1 0.2 collective-permute-start.2
  12.3 4.7 %collective-permute-done.2 = bf16[3,16,576]{2,1,0:T(8,128)(2,1)S(1)} collective-permute-done((bf16[3,16,576]{2,1,0:T(8,128)(2,1)S(1)}, bf16[3,16,576]{2,1,0:T(8,128)(2,1)S(1)}, u32[]{:S(2)}, u32[]{:S(2)}) %collective-permute-start.2) | collective-permute-done | bytes 55328 | tf_op jit(solution)/shard_map/ppermute | solution.py:33
  17.0 0.0 copy-start.4
  17.0 0.3 collective-permute-start.6
  17.3 1.8 %collective-permute-start.5 = (bf16[8,16,576]{2,1,0:T(8,128)(2,1)S(1)}, bf16[8,16,576]{2,1,0:T(8,128)(2,1)S(1)}, u32[]{:S(2)}, u32[]{:S(2)}) collective-permute-start(bf16[8,16,576]{2,1,0:T(8,128)(2,1)S(1)} %get-tuple-element.44), channel_id=1, source_target_pairs={{3,0},{140,8},{19,16},{156,24},{35,32},{172,40},{51,48},{188,56},{... | collective-permute-start | bytes 442376 | tf_op jit(solution)/shard_map/ppermute | solution.py:33
  19.1 0.1 collective-permute-start.4
  19.2 1.6 %copy-done.1 = bf16[16,128,512]{2,1,0:T(8,128)(2,1)S(1)} copy-done((bf16[16,128,512]{2,1,0:T(8,128)(2,1)S(1)}, bf16[16,128,512]{2,1,0:T(8,128)(2,1)}, u32[]{:S(2)}) %copy-start.1) | copy-done | bytes 2097176
  20.8 1.0 %copy-done.2 = bf16[128,2048]{1,0:T(8,128)(2,1)S(1)} copy-done((bf16[128,2048]{1,0:T(8,128)(2,1)S(1)}, bf16[128,2048]{1,0:T(8,128)(2,1)}, u32[]{:S(2)}) %copy-start.2) | copy-done | bytes 524312
  21.8 0.9 %copy-done.3 = bf16[128,1024]{1,0:T(8,128)(2,1)S(1)} copy-done((bf16[128,1024]{1,0:T(8,128)(2,1)S(1)}, bf16[128,1024]{1,0:T(8,128)(2,1)}, u32[]{:S(2)}) %copy-start.3) | copy-done | bytes 262168
  22.8 0.8 %make_queries.1.query_ref = bf16[2,1024,576]{2,1,0:T(8,128)(2,1)S(1)} custom-call(bf16[128,2048]{1,0:T(8,128)(2,1)S(1)} %copy-done.2, bf16[128,1024]{1,0:T(8,128)(2,1)S(1)} %copy-done.3, bf16[16,128,512]{2,1,0:T(8,128)(2,1)S(1)} %copy-done.1), custom_call_target="tpu_custom_call" | custom-call | flops 268435456 | bytes 6291456 | tf_op jit(solution)/shard_map/make_queries/pallas_call | solution.py:80
  23.6 0.1 collective-permute-done.5
  23.7 0.0 collective-permute-done.4
  23.7 7.9 %collective-permute-start.10 = (bf16[32,16,576]{2,1,0:T(8,128)(2,1)S(1)}, bf16[32,16,576]{2,1,0:T(8,128)(2,1)S(1)}, u32[]{:S(2)}, u32[]{:S(2)}) collective-permute-start(bf16[32,16,576]{2,1,0:T(8,128)(2,1)S(1)} %constant_dynamic-update-slice_fusion.4.refs_0_), channel_id=1, source_target_pairs={{0,8},{8,0},{16,24},{24,16},{32,40},{40,32},{48,56},{56,48},{64,72... | collective-permute-start | bytes 1769480 | tf_op jit(solution)/shard_map/ppermute | solution.py:37
  31.7 2.7 %collective-permute-start.8 = (bf16[32,16,576]{2,1,0:T(8,128)(2,1)S(1)}, bf16[32,16,576]{2,1,0:T(8,128)(2,1)S(1)}, u32[]{:S(2)}, u32[]{:S(2)}) collective-permute-start(bf16[32,16,576]{2,1,0:T(8,128)(2,1)S(1)} %constant_dynamic-update-slice_fusion.4.refs_0_), channel_id=1, source_target_pairs={{128,0},{9,8},{144,16},{25,24},{160,32},{41,40},{176,48},{57,56},{... | collective-permute-start | bytes 1769480 | tf_op jit(solution)/shard_map/ppermute | solution.py:33
  34.3 5.1 %absorb_0.1 = (f32[2048,512]{1,0:T(8,128)S(1)}, f32[2048,128]{1,0:T(8,128)S(1)}, f32[2048,128]{1,0:T(8,128)S(1)}) custom-call(s32[64]{0:T(128)S(1)} %copy-done.4, bf16[2,1024,576]{2,1,0:T(8,128)(2,1)S(1)} %make_queries.1.query_ref, bf16[32,16,576]{2,1,0:T(8,128)(2,1)S(1)} %constant_dynamic-update-slice_fusion.4.refs_0_, ...), custom_call_target="tpu_custom_call" | custom-call | flops 2281701376 | bytes 10485760 | tf_op jit(solution)/shard_map/absorb_0/pallas_call | solution.py:254
  39.5 2.8 %collective-permute-done.9.refs_2_ = bf16[32,16,576]{2,1,0:T(8,128)(2,1)S(1)} collective-permute-done((bf16[32,16,576]{2,1,0:T(8,128)(2,1)S(1)}, bf16[32,16,576]{2,1,0:T(8,128)(2,1)S(1)}, u32[]{:S(2)}, u32[]{:S(2)}) %collective-permute-start.9) | collective-permute-done | bytes 589856 | tf_op jit(solution)/shard_map/ppermute | solution.py:33
  42.3 1.2 %collective-permute-start.11 = (bf16[32,16,576]{2,1,0:T(8,128)(2,1)S(1)}, bf16[32,16,576]{2,1,0:T(8,128)(2,1)S(1)}, u32[]{:S(2)}, u32[]{:S(2)}) collective-permute-start(bf16[32,16,576]{2,1,0:T(8,128)(2,1)S(1)} %collective-permute-done.8.refs_0_), channel_id=1, source_target_pairs={{0,8},{8,0},{16,24},{24,16},{32,40},{40,32},{48,56},{56,48},{64,72... | collective-permute-start | bytes 1769480 | tf_op jit(solution)/shard_map/ppermute | solution.py:37
  43.5 0.0 collective-permute-start.12
  43.6 1.1 %collective-permute-start.7 = (bf16[32,16,576]{2,1,0:T(8,128)(2,1)S(1)}, bf16[32,16,576]{2,1,0:T(8,128)(2,1)S(1)}, u32[]{:S(2)}, u32[]{:S(2)}) collective-permute-start(bf16[32,16,576]{2,1,0:T(8,128)(2,1)S(1)} %constant_dynamic-update-slice_fusion.4.refs_0_), channel_id=1, source_target_pairs={{4,0},{10,8},{20,16},{26,24},{36,32},{42,40},{52,48},{58,56},{68,6... | collective-permute-start | bytes 1769480 | tf_op jit(solution)/shard_map/ppermute | solution.py:33
  44.7 0.6 collective-permute-done.11.refs_1_
  45.3 0.9 %collective-permute-done.12.refs_3_ = bf16[32,16,576]{2,1,0:T(8,128)(2,1)S(1)} collective-permute-done((bf16[32,16,576]{2,1,0:T(8,128)(2,1)S(1)}, bf16[32,16,576]{2,1,0:T(8,128)(2,1)S(1)}, u32[]{:S(2)}, u32[]{:S(2)}) %collective-permute-start.12) | collective-permute-done | bytes 589856 | tf_op jit(solution)/shard_map/ppermute | solution.py:37
  46.2 11.5 %absorb_1.1 = (f32[2048,512]{1,0:T(8,128)S(1)}, f32[2048,128]{1,0:T(8,128)S(1)}, f32[2048,128]{1,0:T(8,128)S(1)}) custom-call(s32[64]{0:T(128)S(1)} %copy-done.4, bf16[2,1024,576]{2,1,0:T(8,128)(2,1)S(1)} %make_queries.1.query_ref, bf16[32,16,576]{2,1,0:T(8,128)(2,1)S(1)} %collective-permute-done.8.refs_0_, ...), custom_call_target="tpu_custom_call" | custom-call | flops 4563402752 | bytes 10485760 | tf_op jit(solution)/shard_map/absorb_1/pallas_call | solution.py:254
  57.7 0.5 collective-permute-start.13
  58.2 1.7 %collective-permute-done.13.refs_1_ = bf16[32,16,576]{2,1,0:T(8,128)(2,1)S(1)} collective-permute-done((bf16[32,16,576]{2,1,0:T(8,128)(2,1)S(1)}, bf16[32,16,576]{2,1,0:T(8,128)(2,1)S(1)}, u32[]{:S(2)}, u32[]{:S(2)}) %collective-permute-start.13) | collective-permute-done | bytes 589856 | tf_op jit(solution)/shard_map/ppermute | solution.py:37
  59.9 10.1 %absorb_3.1 = bf16[128,2048]{1,0:T(8,128)(2,1)} custom-call(s32[64]{0:T(128)S(1)} %copy-done.4, bf16[2,1024,576]{2,1,0:T(8,128)(2,1)S(1)} %make_queries.1.query_ref, bf16[32,16,576]{2,1,0:T(8,128)(2,1)S(1)} %collective-permute-done.7.refs_0_, bf16[32,16,576]{2,1,0:T(8,128)(2,1)S(1)} %collective-permute-done.13.refs_1_, ...), custom_call_target="tpu_custom_call" | custom-call | flops 2281701376 | bytes 10485760 | tf_op jit(solution)/shard_map/absorb_3/pallas_call | solution.py:254
  (19 shorter events, 0.2 us)
Async XLA Ops:
  0.0 7.0 %collective-permute-start.1 = (bf16[1,16,576]{2,1,0:T(8,128)(2,1)}, bf16[1,16,576]{2,1,0:T(8,128)(2,1)S(1)}, u32[]{:S(2)}, u32[]{:S(2)}) collective-permute-start(bf16[1,16,576]{2,1,0:T(8,128)(2,1)} %bitcast.3), channel_id=1, source_target_pairs={{112,0},{120,8},{0,16},{8,24},{16,32},{24,40},{32,48},{40,56},{48,... | collective-permute-start | bytes 55304 | tf_op jit(solution)/shard_map/ppermute | solution.py:33
  1.6 5.3 %collective-permute-start = (bf16[1,16,576]{2,1,0:T(8,128)(2,1)}, bf16[1,16,576]{2,1,0:T(8,128)(2,1)S(1)}, u32[]{:S(2)}, u32[]{:S(2)}) collective-permute-start(bf16[1,16,576]{2,1,0:T(8,128)(2,1)} %bitcast.4), channel_id=1, source_target_pairs={{16,0},{24,8},{32,16},{40,24},{48,32},{56,40},{64,48},{72,56},{80,... | collective-permute-start | bytes 55304 | tf_op jit(solution)/shard_map/ppermute | solution.py:33
  7.7 9.3 %collective-permute-start.3 = (bf16[3,16,576]{2,1,0:T(8,128)(2,1)S(1)}, bf16[3,16,576]{2,1,0:T(8,128)(2,1)S(1)}, u32[]{:S(2)}, u32[]{:S(2)}) collective-permute-start(bf16[3,16,576]{2,1,0:T(8,128)(2,1)S(1)} %pad_maximum_fusion), channel_id=1, source_target_pairs={{80,0},{88,8},{96,16},{104,24},{112,32},{120,40},{0,48},{8,56},{16... | collective-permute-start | bytes 165896 | tf_op jit(solution)/shard_map/ppermute | solution.py:33
  12.1 4.9 %collective-permute-start.2 = (bf16[3,16,576]{2,1,0:T(8,128)(2,1)S(1)}, bf16[3,16,576]{2,1,0:T(8,128)(2,1)S(1)}, u32[]{:S(2)}, u32[]{:S(2)}) collective-permute-start(bf16[3,16,576]{2,1,0:T(8,128)(2,1)S(1)} %pad_maximum_fusion), channel_id=1, source_target_pairs={{48,0},{56,8},{64,16},{72,24},{80,32},{88,40},{96,48},{104,56},{11... | collective-permute-start | bytes 165896 | tf_op jit(solution)/shard_map/ppermute | solution.py:33
  17.0 17.4 %copy-start.4 = (s32[64]{0:T(128)S(1)}, s32[64]{0:T(128)}, u32[]{:S(2)}) copy-start(s32[64]{0:T(128)} %starts_ref.5) | copy-start | bytes 772
  17.0 6.5 %collective-permute-start.6 = (bf16[8,16,576]{2,1,0:T(8,128)(2,1)S(1)}, bf16[8,16,576]{2,1,0:T(8,128)(2,1)S(1)}, u32[]{:S(2)}, u32[]{:S(2)}) collective-permute-start(bf16[8,16,576]{2,1,0:T(8,128)(2,1)S(1)} %get-tuple-element.44), channel_id=1, source_target_pairs={{2,0},{12,8},{18,16},{28,24},{34,32},{44,40},{50,48},{60,56},{66,6... | collective-permute-start | bytes 442376 | tf_op jit(solution)/shard_map/ppermute | solution.py:33
  17.3 6.3 %collective-permute-start.5 = (bf16[8,16,576]{2,1,0:T(8,128)(2,1)S(1)}, bf16[8,16,576]{2,1,0:T(8,128)(2,1)S(1)}, u32[]{:S(2)}, u32[]{:S(2)}) collective-permute-start(bf16[8,16,576]{2,1,0:T(8,128)(2,1)S(1)} %get-tuple-element.44), channel_id=1, source_target_pairs={{3,0},{140,8},{19,16},{156,24},{35,32},{172,40},{51,48},{188,56},{... | collective-permute-start | bytes 442376 | tf_op jit(solution)/shard_map/ppermute | solution.py:33
  19.1 4.5 %collective-permute-start.4 = (bf16[8,16,576]{2,1,0:T(8,128)(2,1)S(1)}, bf16[8,16,576]{2,1,0:T(8,128)(2,1)S(1)}, u32[]{:S(2)}, u32[]{:S(2)}) collective-permute-start(bf16[8,16,576]{2,1,0:T(8,128)(2,1)S(1)} %get-tuple-element.44), channel_id=1, source_target_pairs={{1,0},{136,8},{17,16},{152,24},{33,32},{168,40},{49,48},{184,56},{... | collective-permute-start | bytes 442376 | tf_op jit(solution)/shard_map/ppermute | solution.py:33
  19.2 1.6 %copy-start.1 = (bf16[16,128,512]{2,1,0:T(8,128)(2,1)S(1)}, bf16[16,128,512]{2,1,0:T(8,128)(2,1)}, u32[]{:S(2)}) copy-start(bf16[16,128,512]{2,1,0:T(8,128)(2,1)} %uk_ref.1) | copy-start | bytes 6291460
  20.8 1.0 %copy-start.2 = (bf16[128,2048]{1,0:T(8,128)(2,1)S(1)}, bf16[128,2048]{1,0:T(8,128)(2,1)}, u32[]{:S(2)}) copy-start(bf16[128,2048]{1,0:T(8,128)(2,1)} %nope_ref.1) | copy-start | bytes 1572868
  21.8 0.9 %copy-start.3 = (bf16[128,1024]{1,0:T(8,128)(2,1)S(1)}, bf16[128,1024]{1,0:T(8,128)(2,1)}, u32[]{:S(2)}) copy-start(bf16[128,1024]{1,0:T(8,128)(2,1)} %rope_ref.1) | copy-start | bytes 786436
  23.7 10.6 %collective-permute-start.10 = (bf16[32,16,576]{2,1,0:T(8,128)(2,1)S(1)}, bf16[32,16,576]{2,1,0:T(8,128)(2,1)S(1)}, u32[]{:S(2)}, u32[]{:S(2)}) collective-permute-start(bf16[32,16,576]{2,1,0:T(8,128)(2,1)S(1)} %constant_dynamic-update-slice_fusion.4.refs_0_), channel_id=1, source_target_pairs={{0,8},{8,0},{16,24},{24,16},{32,40},{40,32},{48,56},{56,48},{64,72... | collective-permute-start | bytes 1769480 | tf_op jit(solution)/shard_map/ppermute | solution.py:37
  31.7 10.6 %collective-permute-start.9 = (bf16[32,16,576]{2,1,0:T(8,128)(2,1)S(1)}, bf16[32,16,576]{2,1,0:T(8,128)(2,1)S(1)}, u32[]{:S(2)}, u32[]{:S(2)}) collective-permute-start(bf16[32,16,576]{2,1,0:T(8,128)(2,1)S(1)} %constant_dynamic-update-slice_fusion.4.refs_0_), channel_id=1, source_target_pairs={{132,0},{11,8},{148,16},{27,24},{164,32},{43,40},{180,48},{59,56},... | collective-permute-start | bytes 1769480 | tf_op jit(solution)/shard_map/ppermute | solution.py:33
  31.7 10.6 %collective-permute-start.8 = (bf16[32,16,576]{2,1,0:T(8,128)(2,1)S(1)}, bf16[32,16,576]{2,1,0:T(8,128)(2,1)S(1)}, u32[]{:S(2)}, u32[]{:S(2)}) collective-permute-start(bf16[32,16,576]{2,1,0:T(8,128)(2,1)S(1)} %constant_dynamic-update-slice_fusion.4.refs_0_), channel_id=1, source_target_pairs={{128,0},{9,8},{144,16},{25,24},{160,32},{41,40},{176,48},{57,56},{... | collective-permute-start | bytes 1769480 | tf_op jit(solution)/shard_map/ppermute | solution.py:33
  42.3 17.6 %copy-start = (bf16[16,512,128]{2,1,0:T(8,128)(2,1)S(1)}, bf16[16,512,128]{2,1,0:T(8,128)(2,1)}, u32[]{:S(2)}) copy-start(bf16[16,512,128]{2,1,0:T(8,128)(2,1)} %refs_5_.1) | copy-start | bytes 6291460
  42.3 3.0 %collective-permute-start.11 = (bf16[32,16,576]{2,1,0:T(8,128)(2,1)S(1)}, bf16[32,16,576]{2,1,0:T(8,128)(2,1)S(1)}, u32[]{:S(2)}, u32[]{:S(2)}) collective-permute-start(bf16[32,16,576]{2,1,0:T(8,128)(2,1)S(1)} %collective-permute-done.8.refs_0_), channel_id=1, source_target_pairs={{0,8},{8,0},{16,24},{24,16},{32,40},{40,32},{48,56},{56,48},{64,72... | collective-permute-start | bytes 1769480 | tf_op jit(solution)/shard_map/ppermute | solution.py:37
  43.5 2.7 %collective-permute-start.12 = (bf16[32,16,576]{2,1,0:T(8,128)(2,1)S(1)}, bf16[32,16,576]{2,1,0:T(8,128)(2,1)S(1)}, u32[]{:S(2)}, u32[]{:S(2)}) collective-permute-start(bf16[32,16,576]{2,1,0:T(8,128)(2,1)S(1)} %collective-permute-done.9.refs_2_), channel_id=1, source_target_pairs={{0,8},{8,0},{16,24},{24,16},{32,40},{40,32},{48,56},{56,48},{64,72... | collective-permute-start | bytes 1769480 | tf_op jit(solution)/shard_map/ppermute | solution.py:37
  43.6 14.1 %collective-permute-start.7 = (bf16[32,16,576]{2,1,0:T(8,128)(2,1)S(1)}, bf16[32,16,576]{2,1,0:T(8,128)(2,1)S(1)}, u32[]{:S(2)}, u32[]{:S(2)}) collective-permute-start(bf16[32,16,576]{2,1,0:T(8,128)(2,1)S(1)} %constant_dynamic-update-slice_fusion.4.refs_0_), channel_id=1, source_target_pairs={{4,0},{10,8},{20,16},{26,24},{36,32},{42,40},{52,48},{58,56},{68,6... | collective-permute-start | bytes 1769480 | tf_op jit(solution)/shard_map/ppermute | solution.py:33
  57.7 2.2 %collective-permute-start.13 = (bf16[32,16,576]{2,1,0:T(8,128)(2,1)S(1)}, bf16[32,16,576]{2,1,0:T(8,128)(2,1)S(1)}, u32[]{:S(2)}, u32[]{:S(2)}) collective-permute-start(bf16[32,16,576]{2,1,0:T(8,128)(2,1)S(1)} %collective-permute-done.7.refs_0_), channel_id=1, source_target_pairs={{0,8},{8,0},{16,24},{24,16},{32,40},{40,32},{48,56},{56,48},{64,72... | collective-permute-start | bytes 1769480 | tf_op jit(solution)/shard_map/ppermute | solution.py:37
